TPU v7x, 32 devices: a whole 2x2x4 slice. The times are simulated.
32 devices in a mesh: ctx: 8 (over z, core), pipe: 2 (over y), tp: 2 (over x).
Axes of the slice: x: 2, y: 2, z: 4, core: 2. Of those that a mesh axis runs over, the one named last changes fastest.
Arguments:
- section_inputs: bfloat16 [2, 4, 1, 1024, 1024], P('pipe', None, None, 'ctx', 'tp'), may hold values from -6 to 6
- doc_starts: int32 [4, 1, 4], replicated, may hold values from 0 to 1023, as said below
- ln_gains: float32 [2, 2, 1024], P('pipe')
- ln_shifts: float32 [2, 2, 1024], P('pipe'), may hold values from -3 to 3
- qkv_weight: bfloat16 [2, 1024, 3072], P('pipe', None, 'tp'), may hold values from -0.1875 to 0.1875
- qkv_bias: float32 [2, 3072], P('pipe', 'tp'), may hold values from -3 to 3
- feature_weight: float32 [2, 16, 64], P('pipe', 'tp'), may hold values from 0.25 to 4
- dense_weight: bfloat16 [2, 1024, 1024], P('pipe', 'tp'), may hold values from -1.5 to 1.5
- out_bias: float32 [2, 1024], P('pipe', 'tp'), may hold values from -3 to 3
- up_weight: bfloat16 [2, 1024, 4096], P('pipe', None, 'tp')
- up_bias: float32 [2, 4096], P('pipe', 'tp'), may hold values from -3 to 3
- down_weight: bfloat16 [2, 4096, 1024], P('pipe', 'tp'), may hold values from -0.09375 to 0.09375
Outputs:
- section_ends: float32 [2, 4, 1, 1024, 1024], P('pipe', None, None, 'ctx', 'tp')
- ln_gain_grad: float32 [2, 2, 1024], P('pipe', None, 'tp')
- ln_shift_grad: float32 [2, 2, 1024], P('pipe', None, 'tp')
- qkv_weight_grad: float32 [2, 1024, 3072], P('pipe', None, 'tp')
- qkv_bias_grad: float32 [2, 3072], P('pipe', 'tp')
- feature_weight_grad: float32 [2, 16, 64], P('pipe', 'tp')
- dense_weight_grad: float32 [2, 1024, 1024], P('pipe', 'tp')
- out_bias_grad: float32 [2, 1024], P('pipe', 'tp')
- up_weight_grad: float32 [2, 1024, 4096], P('pipe', None, 'tp')
- up_bias_grad: float32 [2, 4096], P('pipe', 'tp')
- down_weight_grad: float32 [2, 4096, 1024], P('pipe', 'tp')
Inputs may be any that keep to these rules, and one draw needn't show every extreme that they name: `doc_starts`: in each row the 4 offsets rise strictly from 0 and stay below 1024; each is the first token of a document that runs to the next offset or to the row's end.
All inputs are finite; a program needn't handle non-finite values.
Results may differ from a plain program's by a relative error of at most 0.012.
The roundings to bfloat16 on the way count: a program that leaves them out, or rounds other values in their place, can miss the bound.
Values may be sent and summed in bfloat16 or wider, within the bound.
A program may use at most 320 MiB of HBM per device.

v0:
```python
from functools import partial
import math

import jax
import jax.numpy as jnp
from jax import lax
from jax.sharding import PartitionSpec as P

D = 1024
HD = 64
ROT = 16
FEAT = 64
BLOCK = 64
MB = 4
ROWS = 1


HIGHEST = lax.Precision.HIGHEST
norm_eps = 1e-05


def entering(part, axis, combine, identity, reverse):
    count = lax.axis_size(axis)
    place = lax.axis_index(axis)
    ahead = count - 1 - place if reverse else place
    gathered = jax.tree.map(lambda a: lax.all_gather(a, axis), part)
    state = jax.tree.map(lambda a, e: jnp.zeros_like(a) + jnp.asarray(e, a.dtype), part, identity)

    def one(step, state):
        source = count - 1 - step if reverse else step
        return combine(
            state, jax.tree.map(lambda a: lax.dynamic_index_in_dim(a, source, 0, False), gathered)
        )

    return lax.fori_loop(0, ahead, one, state)


def passed_along(value, axis, by):
    peers = lax.axis_size(axis)
    pairs = [(i, i + by) for i in range(peers) if 0 <= i + by < peers]
    return lax.ppermute(value, axis, pairs)


def feature_table():
    index_rows = jnp.arange(HD, dtype=jnp.int32)[:, None]
    index_cols = jnp.arange(HD, dtype=jnp.int32)[None, :]
    cosine = jnp.cos(
        math.pi * (index_rows.astype(jnp.float32) + 0.5) * index_cols.astype(jnp.float32) / HD
    )
    scaling = jnp.where(index_cols == 0, math.sqrt(1.0 / HD), math.sqrt(2.0 / HD))
    lattice_index = (
        (jnp.arange(HD, dtype=jnp.int32)[:, None] + 1)
        * (17 * jnp.arange(FEAT, dtype=jnp.int32)[None, :] + 5)
        % 257
    )
    lattice = math.sqrt(2.0) * jnp.cos(2.0 * math.pi * lattice_index.astype(jnp.float32) / 257.0)
    return jnp.dot(cosine * scaling, lattice, precision=HIGHEST) / math.sqrt(HD)


def rotate(values, rot_cos, rot_sin):
    half_rot = ROT // 2
    first_half = values[..., :half_rot]
    second_half = values[..., half_rot:ROT]
    return jnp.concatenate(
        [
            first_half * rot_cos - second_half * rot_sin,
            second_half * rot_cos + first_half * rot_sin,
            values[..., ROT:],
        ],
        axis=-1,
    )


def make_features(projected, feat_weight, rot_cos, rot_sin, exp_table):
    queries = rotate(projected[..., 0, :], rot_cos, rot_sin)
    keys_rot = rotate(projected[..., 1, :], rot_cos, rot_sin)
    query_feat = feat_weight * jnp.exp(
        jnp.einsum("rthd,df->rthf", queries, exp_table, precision=HIGHEST)
    )
    key_feat = feat_weight * jnp.exp(
        jnp.einsum("rthd,df->rthf", keys_rot, exp_table, precision=HIGHEST)
    )
    return (query_feat, key_feat)


def document_masks(starts, positions, blocks):
    seg_ids = (
        jnp.sum((starts[:, None, :] <= positions[None, :, None]).astype(jnp.int32), axis=2) - 1
    )
    resets = jnp.any(starts[:, None, :] == positions[None, :, None], axis=2)
    seg_blocks = seg_ids.reshape(seg_ids.shape[0], blocks, BLOCK)
    reset_blocks = resets.reshape(seg_ids.shape[0], blocks, BLOCK)
    causal = jnp.arange(BLOCK)[:, None] >= jnp.arange(BLOCK)[None, :]
    keep_mask = (causal & (seg_blocks[..., :, None] == seg_blocks[..., None, :])).astype(
        jnp.float32
    )
    enters = ((seg_blocks == seg_blocks[..., :1]) & jnp.logical_not(reset_blocks[..., :1])).astype(
        jnp.float32
    )
    leaves = (seg_blocks == seg_blocks[..., -1:]).astype(jnp.float32)
    return (keep_mask, enters, leaves, enters[..., -1])


def combine_carry(earlier_part, later_part):
    early_state, early_total, early_pass = earlier_part
    late_state, late_total, late_pass = later_part
    return (
        late_state + late_pass[:, None, None, None] * early_state,
        late_total + late_pass[:, None, None] * early_total,
        late_pass * early_pass,
    )


def block_prefix(own_state, own_total, passing, backwards):

    def advance(carried, pieces):
        state_sum, total_sum, factor = carried
        block_state, block_total, block_pass = pieces
        updated = (
            block_pass[:, None, None, None] * state_sum + block_state,
            block_pass[:, None, None] * total_sum + block_total,
            factor * block_pass,
        )
        return (updated, carried)

    initial = (
        jnp.zeros_like(own_state[:, 0]),
        jnp.zeros_like(own_total[:, 0]),
        jnp.ones_like(passing[:, 0]),
    )
    pieces = (
        jnp.moveaxis(own_state, 1, 0),
        jnp.moveaxis(own_total, 1, 0),
        jnp.moveaxis(passing, 1, 0),
    )
    final_carry, emitted = lax.scan(advance, initial, pieces, reverse=backwards)
    return (final_carry, tuple((jnp.moveaxis(member, 0, 1) for member in emitted)))


def block_states(emitted, state_in, total_in):
    local_state, local_total, factor = emitted
    return (
        local_state + factor[..., None, None, None] * state_in[:, None],
        local_total + factor[..., None, None] * total_in[:, None],
    )


def attention_blocks(query_low, key_low, value_low, doc_masks):
    keep_mask, enters, leaves, passing = doc_masks
    scores = (
        jnp.einsum("rcihf,rcjhf->rchij", query_low, key_low, preferred_element_type=jnp.float32)
        * keep_mask[:, :, None]
    )
    weighted = key_low * leaves[..., None, None].astype(jnp.bfloat16)
    own_state = jnp.einsum(
        "rcjhf,rcjhd->rchfd", weighted, value_low, preferred_element_type=jnp.float32
    )
    own_total = jnp.sum(weighted.astype(jnp.float32), axis=2)
    summary, emitted = block_prefix(own_state, own_total, passing, False)
    return (scores, summary, emitted)


def split_features(projected, feat_weight, row_count, blocks, rot_cos, rot_sin, exp_table):
    heads_here = feat_weight.shape[0]
    proj_rows = projected.reshape(row_count, blocks * BLOCK, heads_here, 3, HD)
    features, feat_pull = jax.vjp(
        lambda proj_arg, weight_arg: make_features(
            proj_arg, weight_arg, rot_cos, rot_sin, exp_table
        ),
        proj_rows,
        feat_weight,
    )
    block_shape = (row_count, blocks, BLOCK, heads_here)
    query_low = features[0].astype(jnp.bfloat16).reshape(block_shape + (FEAT,))
    key_low = features[1].astype(jnp.bfloat16).reshape(block_shape + (FEAT,))
    value_low = proj_rows[..., 2, :].astype(jnp.bfloat16).reshape(block_shape + (HD,))
    return (query_low, key_low, value_low, feat_pull)


def layer_forward(input_slice, weights, doc_masks, rot_cos, rot_sin, exp_table):
    (
        gain_rows,
        shift_rows,
        qkv_weight,
        qkv_bias,
        feat_weight,
        dense_weight,
        out_bias,
        up_weight,
        up_bias,
        down_weight,
    ) = weights
    keep_mask, enters, leaves, passing = doc_masks
    row_count, blocks = (enters.shape[0], enters.shape[1])
    heads_here = feat_weight.shape[0]
    full_rows = lax.all_gather(input_slice, "tp", axis=1, tiled=True).astype(jnp.float32)
    mean_row = jnp.mean(full_rows, axis=-1, keepdims=True)
    centered = full_rows - mean_row
    inv_std = lax.rsqrt(jnp.mean(centered * centered, axis=-1, keepdims=True) + norm_eps)
    first_norm = (centered * inv_std * gain_rows[0] + shift_rows[0]).astype(jnp.bfloat16)
    second_norm = (centered * inv_std * gain_rows[1] + shift_rows[1]).astype(jnp.bfloat16)
    projected = jnp.dot(first_norm, qkv_weight, preferred_element_type=jnp.float32) + qkv_bias
    query_low, key_low, value_low, feat_pull = split_features(
        projected, feat_weight, row_count, blocks, rot_cos, rot_sin, exp_table
    )
    scores, summary, emitted = attention_blocks(query_low, key_low, value_low, doc_masks)
    identity = (jnp.zeros_like(summary[0]), jnp.zeros_like(summary[1]), jnp.ones_like(summary[2]))
    carried = entering((summary[0], summary[1], summary[2]), "ctx", combine_carry, identity, False)
    state_in, total_in = (carried[0], carried[1])
    pre_act = jnp.dot(second_norm, up_weight, preferred_element_type=jnp.float32) + up_bias
    hidden_low = jax.nn.gelu(pre_act, approximate=False).astype(jnp.bfloat16)
    mlp_part = jnp.dot(hidden_low, down_weight, preferred_element_type=jnp.float32)
    block_state, block_total = block_states(emitted, state_in, total_in)
    numerator = jnp.einsum(
        "rchij,rcjhd->rcihd",
        scores.astype(jnp.bfloat16),
        value_low,
        preferred_element_type=jnp.float32,
    )
    numerator = numerator + enters[..., None, None] * jnp.einsum(
        "rcihf,rchfd->rcihd",
        query_low,
        block_state.astype(jnp.bfloat16),
        preferred_element_type=jnp.float32,
    )
    denominator = jnp.transpose(jnp.sum(scores, axis=-1), (0, 1, 3, 2))
    denominator = denominator + enters[..., None] * jnp.einsum(
        "rcihf,rchf->rcih", query_low.astype(jnp.float32), block_total, precision=HIGHEST
    )
    output = numerator / denominator[..., None]
    attended_low = output.astype(jnp.bfloat16).reshape(row_count * blocks * BLOCK, heads_here * HD)
    partial_sums = (
        jnp.dot(attended_low, dense_weight, preferred_element_type=jnp.float32) + mlp_part
    )
    layer_out = (
        lax.psum_scatter(partial_sums, "tp", scatter_dimension=1, tiled=True)
        + input_slice.astype(jnp.float32)
        + out_bias
    )
    kept_values = (
        input_slice,
        projected,
        pre_act,
        attended_low,
        output,
        denominator,
        state_in,
        total_in,
        mean_row,
        inv_std,
    )
    kept_values = kept_values + (first_norm, second_norm)
    return (layer_out, kept_values)


def layer_backward(grad_slice, kept_values, weights, doc_masks, rot_cos, rot_sin, exp_table):
    (
        gain_rows,
        shift_rows,
        qkv_weight,
        qkv_bias,
        feat_weight,
        dense_weight,
        out_bias,
        up_weight,
        up_bias,
        down_weight,
    ) = weights
    keep_mask, enters, leaves, passing = doc_masks
    (
        input_slice,
        projected,
        pre_act,
        attended_low,
        output,
        denominator,
        state_in,
        total_in,
        mean_row,
        inv_std,
    ) = kept_values[:10]
    row_count, blocks = (enters.shape[0], enters.shape[1])
    heads_here = feat_weight.shape[0]
    token_count = input_slice.shape[0]
    width_here = input_slice.shape[1]
    grad_full = lax.all_gather(grad_slice, "tp", axis=1, tiled=True)
    first_norm, second_norm = (kept_values[10], kept_values[11])
    gelu_value, gelu_pull = jax.vjp(partial(jax.nn.gelu, approximate=False), pre_act)
    hidden_low = gelu_value.astype(jnp.bfloat16)
    grad_down = jnp.einsum("tk,td->kd", hidden_low, grad_full, preferred_element_type=jnp.float32)
    grad_hidden = jnp.einsum(
        "td,kd->tk", grad_full, down_weight, preferred_element_type=jnp.float32
    )
    grad_pre = gelu_pull(grad_hidden)[0].astype(jnp.bfloat16)
    grad_up = jnp.einsum("tm,tk->mk", second_norm, grad_pre, preferred_element_type=jnp.float32)
    grad_up_bias = jnp.sum(grad_pre.astype(jnp.float32), axis=0)
    grad_second = jnp.einsum("tk,mk->tm", grad_pre, up_weight, preferred_element_type=jnp.float32)
    grad_attended = jnp.einsum(
        "td,kd->tk", grad_full, dense_weight, preferred_element_type=jnp.float32
    ).astype(jnp.bfloat16)
    grad_dense = jnp.einsum(
        "tk,td->kd", attended_low, grad_full, preferred_element_type=jnp.float32
    )
    query_low, key_low, value_low, feat_pull = split_features(
        projected, feat_weight, row_count, blocks, rot_cos, rot_sin, exp_table
    )
    scores, summary, emitted = attention_blocks(query_low, key_low, value_low, doc_masks)
    block_state, block_total = block_states(emitted, state_in, total_in)
    query_full = query_low.astype(jnp.float32)
    key_full = key_low.astype(jnp.float32)
    value_full = value_low.astype(jnp.float32)
    grad_output = grad_attended.astype(jnp.float32).reshape(
        row_count, blocks, BLOCK, heads_here, HD
    )
    grad_numer = grad_output / denominator[..., None]
    grad_denom = -jnp.sum(grad_output * output, axis=-1) / denominator
    grad_scores = (
        jnp.einsum("rcihd,rcjhd->rchij", grad_numer, value_full, precision=HIGHEST)
        + jnp.transpose(grad_denom, (0, 1, 3, 2))[..., None]
    )
    grad_scores = grad_scores * keep_mask[:, :, None]
    carry_term = jnp.einsum(
        "rcihd,rchfd->rcihf",
        grad_numer,
        block_state.astype(jnp.bfloat16).astype(jnp.float32),
        precision=HIGHEST,
    )
    carry_term = carry_term + grad_denom[..., None] * block_total[:, :, None]
    grad_query = (
        jnp.einsum("rchij,rcjhf->rcihf", grad_scores, key_full, precision=HIGHEST)
        + enters[..., None, None] * carry_term
    )
    grad_key = jnp.einsum("rchij,rcihf->rcjhf", grad_scores, query_full, precision=HIGHEST)
    grad_value = jnp.einsum(
        "rchij,rcihd->rcjhd",
        scores.astype(jnp.bfloat16).astype(jnp.float32),
        grad_numer,
        precision=HIGHEST,
    )
    query_enter = query_full * enters[..., None, None]
    own_grad_state = jnp.einsum("rcihf,rcihd->rchfd", query_enter, grad_numer, precision=HIGHEST)
    own_grad_total = jnp.einsum("rcih,rcihf->rchf", grad_denom, query_enter, precision=HIGHEST)
    back_summary, back_emitted = block_prefix(own_grad_state, own_grad_total, passing, True)
    identity = (
        jnp.zeros_like(back_summary[0]),
        jnp.zeros_like(back_summary[1]),
        jnp.ones_like(back_summary[2]),
    )
    later_in = entering(
        (back_summary[0], back_summary[1], back_summary[2]), "ctx", combine_carry, identity, True
    )
    later_state, later_total = block_states(back_emitted, later_in[0], later_in[1])
    leave_mask = leaves[..., None, None]
    grad_key = grad_key + leave_mask * (
        jnp.einsum("rcjhd,rchfd->rcjhf", value_full, later_state, precision=HIGHEST)
        + later_total[:, :, None]
    )
    grad_value = grad_value + leave_mask * jnp.einsum(
        "rcjhf,rchfd->rcjhd", key_full, later_state, precision=HIGHEST
    )
    flat_shape = (row_count, blocks * BLOCK, heads_here)
    grad_proj_feat, grad_feat_weight = feat_pull(
        (grad_query.reshape(flat_shape + (FEAT,)), grad_key.reshape(flat_shape + (FEAT,)))
    )
    grad_proj = jnp.concatenate(
        [grad_proj_feat[..., :2, :], grad_value.reshape(flat_shape + (1, HD))], axis=3
    )
    grad_proj_low = grad_proj.reshape(token_count, heads_here * 3 * HD).astype(jnp.bfloat16)
    grad_qkv = jnp.einsum(
        "tm,tk->mk", first_norm, grad_proj_low, preferred_element_type=jnp.float32
    )
    grad_qkv_bias = jnp.sum(grad_proj_low.astype(jnp.float32), axis=0)
    grad_first = jnp.einsum(
        "tk,mk->tm", grad_proj_low, qkv_weight, preferred_element_type=jnp.float32
    )
    normed = (input_slice.astype(jnp.float32) - mean_row) * inv_std
    grad_input = grad_slice.astype(jnp.float32)
    grad_norm_one, grad_norm_two = (
        lax.psum_scatter(grad_first, "tp", scatter_dimension=1, tiled=True),
        lax.psum_scatter(grad_second, "tp", scatter_dimension=1, tiled=True),
    )
    col_start = lax.axis_index("tp") * width_here
    gain_slice = lax.dynamic_slice_in_dim(gain_rows, col_start, width_here, 1)
    scaled_one = grad_norm_one * gain_slice[0]
    scaled_two = grad_norm_two * gain_slice[1]
    totals = lax.psum(
        (
            jnp.sum(scaled_one, axis=-1, keepdims=True),
            jnp.sum(scaled_one * normed, axis=-1, keepdims=True),
            jnp.sum(scaled_two, axis=-1, keepdims=True),
            jnp.sum(scaled_two * normed, axis=-1, keepdims=True),
        ),
        "tp",
    )
    grad_input = grad_input + inv_std * (scaled_one - totals[0] / D - normed * (totals[1] / D))
    grad_input = grad_input + inv_std * (scaled_two - totals[2] / D - normed * (totals[3] / D))
    grad_gain = jnp.stack(
        [jnp.sum(grad_norm_one * normed, axis=0), jnp.sum(grad_norm_two * normed, axis=0)]
    )
    grad_shift = jnp.stack([jnp.sum(grad_norm_one, axis=0), jnp.sum(grad_norm_two, axis=0)])
    grad_out_bias = jnp.sum(grad_slice.astype(jnp.float32), axis=0)
    return (
        grad_input,
        (
            grad_gain,
            grad_shift,
            grad_qkv,
            grad_qkv_bias,
            grad_feat_weight,
            grad_dense,
            grad_out_bias,
            grad_up,
            grad_up_bias,
            grad_down,
        ),
    )


def local(
    section_inputs,
    doc_starts,
    ln_gains,
    ln_shifts,
    qkv_weight,
    qkv_bias,
    feature_weight,
    dense_weight,
    out_bias,
    up_weight,
    up_bias,
    down_weight,
):
    section_index = lax.axis_index("pipe")
    ctx_place = lax.axis_index("ctx")
    width_here = section_inputs.shape[-1]
    local_tokens = section_inputs.shape[3]
    blocks = local_tokens // BLOCK
    token_count = ROWS * local_tokens
    local_inputs = section_inputs[0].reshape(MB, token_count, width_here)
    weights = (
        ln_gains[0],
        ln_shifts[0],
        qkv_weight[0],
        qkv_bias[0],
        feature_weight[0],
        dense_weight[0],
        out_bias[0],
        up_weight[0],
        up_bias[0],
        down_weight[0],
    )
    exp_table = feature_table()
    positions = ctx_place * local_tokens + jnp.arange(local_tokens, dtype=jnp.int32)
    inv_freq = 10000.0 ** (-(2.0 * jnp.arange(ROT // 2).astype(jnp.float32)) / ROT)
    angles = positions.astype(jnp.float32)[:, None] * inv_freq[None, :]
    rot_cos = jnp.cos(angles)[:, None, :]
    rot_sin = jnp.sin(angles)[:, None, :]

    def masks_for(micro_index):
        starts = lax.dynamic_index_in_dim(doc_starts, micro_index, 0, keepdims=False)
        return document_masks(starts, positions, blocks)

    received = jnp.zeros((token_count, width_here), jnp.bfloat16)
    kept_ticks = []
    block_outputs = []
    for step_index in range(MB + 1):
        own_input = local_inputs[min(step_index, MB - 1)]
        layer_input = jnp.where(section_index == 0, own_input, received)
        micro_index = jnp.clip(step_index - section_index, 0, MB - 1)
        layer_out, kept_values = layer_forward(
            layer_input, weights, masks_for(micro_index), rot_cos, rot_sin, exp_table
        )
        kept_ticks.append(kept_values)
        if step_index >= 1:
            block_outputs.append(layer_out)
        if step_index < MB:
            received = passed_along(layer_out.astype(jnp.bfloat16), "pipe", 1)
    received_grad = jnp.zeros((token_count, width_here), jnp.bfloat16)
    totals_grad = None
    input_grads = []
    for step_index in range(MB + 1):
        late_tick = min(step_index + 1, MB)
        early_tick = max(step_index - 1, 0)
        kept_values = jax.tree.map(
            lambda late_item, early_item: jnp.where(section_index == 1, late_item, early_item),
            kept_ticks[late_tick],
            kept_ticks[early_tick],
        )
        micro_index = jnp.where(section_index == 1, min(step_index, MB - 1), early_tick)
        valid_flag = jnp.where(section_index == 1, step_index < MB, step_index >= 1).astype(
            jnp.float32
        )
        cotangent = jnp.where(
            section_index == 1, local_inputs[min(step_index, MB - 1)], received_grad
        )
        grad_input, grad_terms = layer_backward(
            cotangent, kept_values, weights, masks_for(micro_index), rot_cos, rot_sin, exp_table
        )
        if step_index < MB:
            received_grad = passed_along(grad_input.astype(jnp.bfloat16), "pipe", -1)
        if step_index >= 1:
            input_grads.append(grad_input)
        scaled = tuple((member * valid_flag for member in grad_terms))
        if totals_grad is None:
            totals_grad = tuple(scaled)
        else:
            totals_grad = tuple(
                (first_term + second_term for first_term, second_term in zip(totals_grad, scaled))
            )
    totals_grad = lax.psum(
        (
            totals_grad[0],
            totals_grad[1],
            totals_grad[2],
            totals_grad[3],
            totals_grad[4],
            totals_grad[5],
            totals_grad[6],
            totals_grad[7],
            totals_grad[8],
            totals_grad[9],
        ),
        "ctx",
    )
    end_values = jnp.where(section_index == 0, jnp.stack(input_grads), jnp.stack(block_outputs))
    section_ends = end_values.reshape(1, MB, ROWS, local_tokens, width_here)
    return (section_ends,) + tuple((member[None] for member in totals_grad))


def solution(mesh):
    in_specs = (
        P("pipe", None, None, "ctx", "tp"),
        P(),
        P("pipe", None, None),
        P("pipe", None, None),
        P("pipe", None, "tp"),
        P("pipe", "tp"),
        P("pipe", "tp", None),
        P("pipe", "tp", None),
        P("pipe", "tp"),
        P("pipe", None, "tp"),
        P("pipe", "tp"),
        P("pipe", "tp", None),
    )
    out_specs = (
        P("pipe", None, None, "ctx", "tp"),
        P("pipe", None, "tp"),
        P("pipe", None, "tp"),
        P("pipe", None, "tp"),
        P("pipe", "tp"),
        P("pipe", "tp", None),
        P("pipe", "tp", None),
        P("pipe", "tp"),
        P("pipe", None, "tp"),
        P("pipe", "tp"),
        P("pipe", "tp", None),
    )
    return jax.shard_map(local, mesh=mesh, in_specs=in_specs, out_specs=out_specs, check_vma=False)
```

profile of v0, /device:TPU:0, one launch (start us, length us, event | category | flops | bytes accessed | tf_op | source)
XLA Modules:
  0.0 2499.7 jit_solution(1164531139592611132)
XLA Ops:
  47.4 13.3 while.495
  123.3 16.6 all-reduce.40
  139.8 15.0 all-gather.3
  169.3 8.0 all-gather.4
  210.2 33.0 %reduce-scatter.16.cloned.1.call-done = f32[128,512]{1,0:T(8,128)} async-done(((f32[128,1024]{1,0:T(8,128)}), f32[128,512]{1,0:T(8,128)}) %reduce-scatter.16.cloned.1.call-update) | async-done | bytes 262160 | tf_op jit(solution)/shard_map/reduce_scatter | solution.py:236
  281.8 20.2 while.496
  309.7 16.0 all-reduce.41
  330.3 15.1 all-gather.7
  388.2 23.5 reduce-scatter.22.cloned.1.call-done
  476.5 20.9 while.498
  517.9 20.7 while.497
  542.8 18.3 while.499
  616.2 16.6 all-gather.13
  635.1 14.8 all-gather.10
  657.1 15.7 all-reduce.53
  673.5 34.7 %while.487 = (s32[]{:T(128)}, f32[1,8,64,64]{3,2,1,0:T(8,128)}, f32[1,8,64]{2,1,0:T(8,128)S(1)}, s32[]{:T(128)}, f32[8,1,8,64,64]{4,3,2,1,0:T(8,128)}, /*index=5...) while((s32[]{:T(128)}, f32[1,8,64,64]{3,2,1,0:T(8,128)}, ...), condition=%wide.region_27.28_spmd, body=%wide.region_26.27_spmd.sunk | while | flops 66566 | bytes 399551 | solution.py:35
  800.2 7.6 convert_reduce_fusion.3
  859.7 18.1 while.502
  881.9 20.6 while.501
  922.1 18.2 while.500
  969.6 14.9 all-gather.19
  986.7 14.0 all-gather.16
  1010.9 16.7 all-reduce.52
  1029.1 25.9 %while.489 = (s32[]{:T(128)}, f32[1,8,64,64]{3,2,1,0:T(8,128)}, f32[1,8,64]{2,1,0:T(8,128)S(1)}, s32[]{:T(128)}, f32[8,1,8,64,64]{4,3,2,1,0:T(8,128)}, /*index=5...) while((s32[]{:T(128)}, f32[1,8,64,64]{3,2,1,0:T(8,128)}, ...), condition=%wide.region_58.59_spmd, body=%wide.region_57.58_spmd.sunk | while | flops 66566 | bytes 399551 | solution.py:35
  1142.4 7.7 convert_reduce_fusion.2
  1222.4 17.9 while.504
  1268.6 20.4 while.503
  1293.2 18.0 while.505
  1363.2 14.8 all-gather.22
  1380.8 12.0 while.507
  1393.4 14.7 all-gather.25
  1418.8 17.8 all-reduce.51
  1439.5 34.5 %while.491 = (s32[]{:T(128)}, f32[1,8,64,64]{3,2,1,0:T(8,128)}, f32[1,8,64]{2,1,0:T(8,128)S(1)}, s32[]{:T(128)}, f32[8,1,8,64,64]{4,3,2,1,0:T(8,128)}, /*index=5...) while((s32[]{:T(128)}, f32[1,8,64,64]{3,2,1,0:T(8,128)}, ...), condition=%wide.region_89.90_spmd, body=%wide.region_88.89_spmd.sunk | while | flops 66566 | bytes 399551 | solution.py:35
  1581.4 17.9 while.506
  1606.2 14.7 all-reduce.48
  1626.0 15.3 all-gather.28
  1656.2 30.0 %while.493 = (s32[]{:T(128)}, f32[1,8,64,64]{3,2,1,0:T(8,128)}, f32[1,8,64]{2,1,0:T(8,128)S(1)}, s32[]{:T(128)}, f32[8,1,8,64,64]{4,3,2,1,0:T(8,128)}, /*index=5...) while((s32[]{:T(128)}, f32[1,8,64,64]{3,2,1,0:T(8,128)}, ...), condition=%wide.region_120.121_spmd, body=%wide.region_119.120_spmd.sunk | while | flops 66566 | bytes 399551 | solution.py:35
  1710.5 14.5 while.509
  1783.8 16.7 while.508
  1800.6 7.8 fusion.350
  1820.7 14.4 all-reduce.49
  1841.7 14.9 all-gather.31
  1879.9 15.8 add_bitcast_fusion.1
  1895.8 16.3 add_bitcast_fusion
  1912.9 30.5 %while.494 = (s32[]{:T(128)}, f32[1,8,64,64]{3,2,1,0:T(8,128)}, f32[1,8,64]{2,1,0:T(8,128)S(1)}, s32[]{:T(128)}, f32[8,1,8,64,64]{4,3,2,1,0:T(8,128)}, /*index=5...) while((s32[]{:T(128)}, f32[1,8,64,64]{3,2,1,0:T(8,128)}, ...), condition=%wide.region_140.141_spmd, body=%wide.region_139.140_spmd.sunk | while | flops 66566 | bytes 399551 | solution.py:35
  1966.9 13.1 add_bitcast_fusion.2
  2003.0 28.9 %all-reduce.50 = (f32[1,2,512]{2,1,0:T(2,128)}, f32[1,2,512]{2,1,0:T(2,128)}, f32[1,1536]{1,0:T(1,128)}, f32[1,8,64]{2,1,0:T(8,128)}, f32[1,512]{1,0:T(1,128)}, /*index=5*/f32[1,2048]{1,0:T(1,128)}) all-reduce(f32[1,2,512]{2,1,0:T(2,128)S(1)} %fusion.886, ...), channel_id=1, replica_groups=mesh['ctx'=8,'pipe'=2,'tp'=2] {'ctx'}, use_global_device_ids=true, to_apply=%region_165.166 | all-reduce | flops 6656 | bytes 53248 | tf_op jit(solution)/shard_map/psum | solution.py:510
  2035.8 439.1 %all-reduce.62.cloned.1.call-done = (f32[1,1024,1536]{2,1,0:T(8,128)}, f32[1,512,1024]{2,1,0:T(8,128)}, f32[1,1024,2048]{2,1,0:T(8,128)}, f32[1,2048,1024]{2,1,0:T(8,128)}) async-done(((f32[1,1024,1536]{2,1,0:T(8,128)}, f32[1,512,1024]{2,1,0:T(8,128)}, f32[1,1024,2048]{2,1,0:T(8,128)}, f32[1,2048,1024]{2,1,0:T(8,128)}), (f32[1,1024,1536]{2,1,0:T(8,128)}, f32[1,512,1024]{2,1,0:T(8,128)}, ...) | async-done | bytes 25165840 | tf_op jit(solution)/shard_map/psum | solution.py:510
  (1587 shorter events, 1600.0 us)
Async XLA Ops:
  7.2 182.1 %all-gather.43.cloned.1.call-start = ((), (), s32[]{:S(2)}) async-start(), calls=%async_computation.30 | async-start | bytes 2359296 | tf_op jit(solution)/shard_map/all_gather | solution.py:26
  20.0 161.8 %copy-start.5 = (bf16[1,1,1,128,1024]{4,3,2,1,0:T(8,128)(2,1)}, bf16[1,1,1,128,1024]{4,3,2,1,0:T(8,128)(2,1)S(1)}, u32[]{:S(2)}) copy-start(bf16[1,1,1,128,1024]{4,3,2,1,0:T(8,128)(2,1)S(1)} %all-gather) | copy-start | bytes 786436
  47.4 134.3 %copy-start.78 = (f32[1,2048]{1,0:T(1,128)S(1)}, f32[1,2048]{1,0:T(1,128)}, u32[]{:S(2)}) copy-start(f32[1,2048]{1,0:T(1,128)} %param.72) | copy-start | bytes 24580
  60.7 108.5 %copy-start.130 = (f32[2,1,8,64]{3,2,1,0:T(8,128)}, f32[2,1,8,64]{3,2,1,0:T(8,128)S(1)}, u32[]{:S(2)}) copy-start(f32[2,1,8,64]{3,2,1,0:T(8,128)S(1)} %get-tuple-element.2447) | copy-start | bytes 12292
  60.8 182.5 %reduce-scatter.16.cloned.1.call-start = ((), (), s32[]{:S(2)}) async-start(), calls=%async_computation.15 | async-start | bytes 786432 | tf_op jit(solution)/shard_map/reduce_scatter | solution.py:236
  62.9 106.3 %copy-start.143 = (s32[2,64]{1,0:T(2,128)}, s32[2,64]{1,0:T(2,128)S(1)}, u32[]{:S(2)}) copy-start(s32[2,64]{1,0:T(2,128)S(1)} %sub.517) | copy-start | bytes 1540
  67.4 101.8 %copy-start.144 = (s32[2,64]{1,0:T(2,128)}, s32[2,64]{1,0:T(2,128)S(1)}, u32[]{:S(2)}) copy-start(s32[2,64]{1,0:T(2,128)S(1)} %sub.494) | copy-start | bytes 1540
  74.4 94.9 %copy-start.145 = (s32[2,64]{1,0:T(2,128)}, s32[2,64]{1,0:T(2,128)S(1)}, u32[]{:S(2)}) copy-start(s32[2,64]{1,0:T(2,128)S(1)} %sub.471) | copy-start | bytes 1540
  78.2 91.0 %copy-start.146 = (s32[2,64]{1,0:T(2,128)}, s32[2,64]{1,0:T(2,128)S(1)}, u32[]{:S(2)}) copy-start(s32[2,64]{1,0:T(2,128)S(1)} %sub.447) | copy-start | bytes 1540
  116.1 53.1 %copy-start.174 = (s32[2]{0:T(128)}, s32[2]{0:T(128)S(1)}, u32[]{:S(2)}) copy-start(s32[2]{0:T(128)S(1)} %get-tuple-element.4795) | copy-start | bytes 28
  139.8 45.9 %copy-start.194 = (bf16[1,2048,1024]{2,1,0:T(8,128)(2,1)S(1)}, bf16[1,2048,1024]{2,1,0:T(8,128)(2,1)}, u32[]{:S(2)}) copy-start(bf16[1,2048,1024]{2,1,0:T(8,128)(2,1)} %param.73) | copy-start | bytes 12582916
  202.2 153.3 %all-gather.45.cloned.1.call-start = ((), (), s32[]{:S(2)}) async-start(), calls=%async_computation.31 | async-start | bytes 2359296 | tf_op jit(solution)/shard_map/all_gather | solution.py:26
  244.3 6.1 collective-permute-start
  257.6 90.3 %copy-start.4 = (bf16[128,1024]{1,0:T(8,128)(2,1)}, bf16[128,1024]{1,0:T(8,128)(2,1)S(1)}, u32[]{:S(2)}) copy-start(bf16[128,1024]{1,0:T(8,128)(2,1)S(1)} %all_gather.217) | copy-start | bytes 786436
  302.0 109.7 %reduce-scatter.22.cloned.1.call-start = ((), (), s32[]{:S(2)}) async-start(), calls=%async_computation.18 | async-start | bytes 786432 | tf_op jit(solution)/shard_map/reduce_scatter | solution.py:236
  370.2 302.6 %all-gather.47.cloned.1.call-start = ((), (), s32[]{:S(2)}) async-start(), calls=%async_computation.32 | async-start | bytes 2359296 | tf_op jit(solution)/shard_map/all_gather | solution.py:26
  413.5 6.1 collective-permute-start.2
  538.6 183.3 %all-gather.49.cloned.1.call-start = ((), (), s32[]{:S(2)}) async-start(), calls=%async_computation.33 | async-start | bytes 2359296 | tf_op jit(solution)/shard_map/all_gather | solution.py:26
  561.1 187.7 %reduce-scatter.20.cloned.1.call-start = ((), (), s32[]{:S(2)}) async-start(), calls=%async_computation.17 | async-start | bytes 786432 | tf_op jit(solution)/shard_map/reduce_scatter | solution.py:380
  583.0 168.6 %reduce-scatter.18.cloned.1.call-start = ((), (), s32[]{:S(2)}) async-start(), calls=%async_computation.16 | async-start | bytes 786432 | tf_op jit(solution)/shard_map/reduce_scatter | solution.py:379
  738.4 70.3 %reduce-scatter.28.cloned.1.call-start = ((), (), s32[]{:S(2)}) async-start(), calls=%async_computation.21 | async-start | bytes 786432 | tf_op jit(solution)/shard_map/reduce_scatter | solution.py:236
  763.7 6.9 collective-permute-start.1
  794.9 232.7 %all-gather.53.cloned.1.call-start = ((), (), s32[]{:S(2)}) async-start(), calls=%async_computation.35 | async-start | bytes 2359296 | tf_op jit(solution)/shard_map/all_gather | solution.py:26
  810.4 6.1 collective-permute-start.4
  877.8 150.6 %all-gather.51.cloned.1.call-start = ((), (), s32[]{:S(2)}) async-start(), calls=%async_computation.34 | async-start | bytes 2359296 | tf_op jit(solution)/shard_map/all_gather | solution.py:26
  940.3 148.5 %reduce-scatter.26.cloned.1.call-start = ((), (), s32[]{:S(2)}) async-start(), calls=%async_computation.20 | async-start | bytes 786432 | tf_op jit(solution)/shard_map/reduce_scatter | solution.py:380
  959.6 135.6 %reduce-scatter.24.cloned.1.call-start = ((), (), s32[]{:S(2)}) async-start(), calls=%async_computation.19 | async-start | bytes 786432 | tf_op jit(solution)/shard_map/reduce_scatter | solution.py:379
  1078.4 73.1 %reduce-scatter.34.cloned.1.call-start = ((), (), s32[]{:S(2)}) async-start(), calls=%async_computation.24 | async-start | bytes 786432 | tf_op jit(solution)/shard_map/reduce_scatter | solution.py:236
  1107.2 6.8 collective-permute-start.3
  1109.1 47.6 %copy-start.92 = (f32[1,2,8,64]{3,2,1,0:T(8,128)}, f32[1,2,8,64]{3,2,1,0:T(8,128)S(1)}, u32[]{:S(2)}) copy-start(f32[1,2,8,64]{3,2,1,0:T(8,128)S(1)} %get-tuple-element.4523) | copy-start | bytes 12292
  1137.8 300.9 %all-gather.55.cloned.1.call-start = ((), (), s32[]{:S(2)}) async-start(), calls=%async_computation.36 | async-start | bytes 2359296 | tf_op jit(solution)/shard_map/all_gather | solution.py:26
  1153.3 6.1 collective-permute-start.6
  1289.1 198.7 %all-gather.57.cloned.1.call-start = ((), (), s32[]{:S(2)}) async-start(), calls=%async_computation.37 | async-start | bytes 2359296 | tf_op jit(solution)/shard_map/all_gather | solution.py:26
  1311.3 207.6 %reduce-scatter.32.cloned.1.call-start = ((), (), s32[]{:S(2)}) async-start(), calls=%async_computation.23 | async-start | bytes 786432 | tf_op jit(solution)/shard_map/reduce_scatter | solution.py:380
  1331.0 189.7 %reduce-scatter.30.cloned.1.call-start = ((), (), s32[]{:S(2)}) async-start(), calls=%async_computation.22 | async-start | bytes 786432 | tf_op jit(solution)/shard_map/reduce_scatter | solution.py:379
  1347.1 33.7 %copy-start.95 = (f32[1,8,64]{2,1,0:T(8,128)S(1)}, f32[1,8,64]{2,1,0:T(8,128)}, u32[]{:S(2)}) copy-start(f32[1,8,64]{2,1,0:T(8,128)} %custom-call.25) | copy-start | bytes 6148
  1347.1 33.7 %copy-start.196 = (f32[2]{0:T(128)S(1)}, f32[2]{0:T(128)}, u32[]{:S(2)}) copy-start(f32[2]{0:T(128)} %fusion.906) | copy-start | bytes 28
  1508.2 147.2 %all-gather.59.cloned.1.call-start = ((), (), s32[]{:S(2)}) async-start(), calls=%async_computation.38 | async-start | bytes 2359296 | tf_op jit(solution)/shard_map/all_gather | solution.py:26
  1530.2 6.8 collective-permute-start.5
  1599.3 125.8 %reduce-scatter.38.cloned.1.call-start = ((), (), s32[]{:S(2)}) async-start(), calls=%async_computation.26 | async-start | bytes 786432 | tf_op jit(solution)/shard_map/reduce_scatter | solution.py:380
  1653.0 33.2 %copy-start.140 = (f32[2,64]{1,0:T(2,128)S(1)}, f32[2,64]{1,0:T(2,128)}, u32[]{:S(2)}) copy-start(f32[2,64]{1,0:T(2,128)} %get-tuple-element.4516) | copy-start | bytes 1540
  1655.4 69.7 %reduce-scatter.36.cloned.1.call-start = ((), (), s32[]{:S(2)}) async-start(), calls=%async_computation.25 | async-start | bytes 786432 | tf_op jit(solution)/shard_map/reduce_scatter | solution.py:379
  1709.6 202.6 %all-gather.61.cloned.1.call-start = ((), (), s32[]{:S(2)}) async-start(), calls=%async_computation.39 | async-start | bytes 2359296 | tf_op jit(solution)/shard_map/all_gather | solution.py:26
  1735.1 7.0 collective-permute-start.7
  1800.5 193.2 %reduce-scatter.44.cloned.1.call-start = ((), (), s32[]{:S(2)}) async-start(), calls=%async_computation.29 | async-start | bytes 786432 | tf_op jit(solution)/shard_map/reduce_scatter | solution.py:236
  1863.9 129.9 %reduce-scatter.42.cloned.1.call-start = ((), (), s32[]{:S(2)}) async-start(), calls=%async_computation.28 | async-start | bytes 786432 | tf_op jit(solution)/shard_map/reduce_scatter | solution.py:380
  1874.2 119.6 %reduce-scatter.40.cloned.1.call-start = ((), (), s32[]{:S(2)}) async-start(), calls=%async_computation.27 | async-start | bytes 786432 | tf_op jit(solution)/shard_map/reduce_scatter | solution.py:379
  1966.8 508.0 %all-reduce.62.cloned.1.call-start = ((), (), s32[]{:S(2)}) async-start(), calls=%async_computation.40 | async-start | bytes 50331648 | tf_op jit(solution)/shard_map/psum | solution.py:510
  (189 other events, 1775.0 us)
Sparse Core Ops, SparseCore 0:
  60.9 30.6 all-gather.42
  202.3 40.8 reduce-scatter.15
  302.1 30.4 all-gather.44
  370.3 41.3 reduce-scatter.21
  538.7 32.0 all-gather.46
  572.3 28.5 all-gather.48
  603.2 14.0 reduce-scatter.19
  738.5 13.0 reduce-scatter.17
  795.0 13.6 reduce-scatter.27
  877.9 30.1 all-gather.52
  940.4 30.1 all-gather.50
  972.8 14.0 reduce-scatter.25
  1078.6 16.6 reduce-scatter.23
  1137.9 13.6 reduce-scatter.33
  1289.2 29.6 all-gather.54
  1320.3 28.5 all-gather.56
  1351.0 14.0 reduce-scatter.31
  1508.3 12.3 reduce-scatter.29
  1599.4 28.5 all-gather.58
  1655.5 11.3 reduce-scatter.37
  1709.7 10.3 reduce-scatter.35
  1800.6 25.0 all-gather.60
  1864.0 10.8 reduce-scatter.43
  1877.1 14.5 reduce-scatter.41
  1967.0 10.3 reduce-scatter.39
  1981.6 493.2 all-reduce.61
where the time goes:
time: 2530 us; the launch traced here: 2500 us
  local copies, waits for them, and re-layouts  557 us (22%)
  waiting for transfers between devices  533 us (21%)
  matrix products  493 us (19%)
  other arithmetic  480 us (19%)
  blocking collectives  377 us (15%)
    psum x1, waiting for transfers between devices, local(): lax.psum((totals_grad[0], totals_grad[1], totals_grad[2], totals_grad[3],...  439 us
    all_gather x10, blocking collectives, entering(): gathered = jax.tree.map(lambda a: lax.all_gather(a, axis), part)  150 us
    unnamed x7, blocking collectives  112 us
    add x35, other arithmetic, combine_carry(): late_state + late_pass[:, None, None, None] * early_state  84.1 us
    unnamed x441, local copies, waits for them, and re-layouts  73.9 us
    add x30, other arithmetic, advance(): block_pass[:, None, None, None] * state_sum + block_state  69.6 us
    another operation x85, local copies, waits for them, and re-layouts  67.5 us
    reduce_scatter x5, waiting for transfers between devices, layer_forward(): lax.psum_scatter(partial_sums, 'tp', scatter_dimension=1, tiled=True)  58.9 us
  transfers between devices with their start and end apart: 34, of which 15 were waited for; matrix products, arithmetic and copies ran while one was open for 37% of the time, Pallas kernels for 0%

commit v1 on v0

v1 whole, which is shorter than its diff:
```python
from functools import partial
import math

import jax
import jax.numpy as jnp
from jax import lax
from jax.experimental import pallas as pl
from jax.experimental.pallas import tpu as pltpu
from jax.sharding import PartitionSpec as P

D = 1024
HD = 64
ROT = 16
FEAT = 64
MB = 4
ROWS = 1
NDOC = 4
PAIR = 2 * HD

BF = jnp.bfloat16
F32 = jnp.float32
HIGHEST = lax.Precision.HIGHEST
norm_eps = 1e-05
VMEM_LIMIT = 56 * 1024 * 1024


def feature_table():
    index_rows = jnp.arange(HD, dtype=jnp.int32)[:, None]
    index_cols = jnp.arange(HD, dtype=jnp.int32)[None, :]
    cosine = jnp.cos(
        math.pi * (index_rows.astype(F32) + 0.5) * index_cols.astype(F32) / HD
    )
    scaling = jnp.where(index_cols == 0, math.sqrt(1.0 / HD), math.sqrt(2.0 / HD))
    lattice_index = (
        (jnp.arange(HD, dtype=jnp.int32)[:, None] + 1)
        * (17 * jnp.arange(FEAT, dtype=jnp.int32)[None, :] + 5)
        % 257
    )
    lattice = math.sqrt(2.0) * jnp.cos(2.0 * math.pi * lattice_index.astype(F32) / 257.0)
    return jnp.dot(cosine * scaling, lattice, precision=HIGHEST) / math.sqrt(HD)


def table_pair():
    table = feature_table()
    zero = jnp.zeros_like(table)
    both = jnp.concatenate(
        [jnp.concatenate([table, zero], 1), jnp.concatenate([zero, table], 1)], 0
    )
    high = lax.reduce_precision(both, 8, 7).astype(BF)
    return high, (both - high.astype(F32)).astype(BF)


def rotary_tables(place, tokens):
    half = ROT // 2
    positions = place * tokens + jnp.arange(tokens, dtype=jnp.int32)
    inv_freq = 10000.0 ** (-(2.0 * jnp.arange(half).astype(F32)) / ROT)
    angles = positions.astype(F32)[:, None] * inv_freq[None, :]
    cos, sin = jnp.cos(angles), jnp.sin(angles)
    rest = jnp.ones((tokens, HD - ROT), F32)
    none = jnp.zeros((tokens, half), F32)
    same = jnp.concatenate([cos, cos, rest], 1)
    down = jnp.concatenate([-sin, none, 0.0 * rest], 1)
    up = jnp.concatenate([none, sin, 0.0 * rest], 1)
    return tuple(jnp.concatenate([t, t], 1) for t in (same, down, up))


def dot(a, b, ca=1, cb=0):
    return lax.dot_general(a, b, (((ca,), (cb,)), ((), ())), preferred_element_type=F32)


def split_dot(a, b, cb=0):
    high = a.astype(BF)
    low = (a - high.astype(F32)).astype(BF)
    return dot(high, b, 1, cb) + dot(low, b, 1, cb)


def lane_masks(rows):
    low = lax.broadcasted_iota(jnp.int32, (rows, PAIR), 1) < HD
    first = low.astype(F32)
    return low, first.astype(BF), (1.0 - first).astype(BF)


def count_starts(starts_ref, row, position):
    total = jnp.int32(0)
    for n in range(NDOC):
        total = total + (starts_ref[row, n] <= position).astype(jnp.int32)
    return total


def seg_grid(starts_ref, row, base, shape, dim):
    position = base + lax.broadcasted_iota(jnp.int32, shape, dim)
    total = jnp.zeros(shape, jnp.int32)
    for n in range(NDOC):
        total = total + (starts_ref[row, n] <= position).astype(jnp.int32)
    return total


def causal_mask(starts_ref, row, base, tokens):
    shape = (tokens, tokens)
    same = seg_grid(starts_ref, row, base, shape, 0) == seg_grid(starts_ref, row, base, shape, 1)
    earlier = lax.broadcasted_iota(jnp.int32, shape, 1) <= lax.broadcasted_iota(
        jnp.int32, shape, 0
    )
    rows = lax.broadcasted_iota(jnp.int32, shape, 0) < tokens // 2
    cols = lax.broadcasted_iota(jnp.int32, shape, 1) < tokens // 2
    mask = same & earlier
    return mask.astype(F32), (mask & (rows == cols)).astype(F32)


def middle_state(starts_ref, row, base, tokens, k, v, state_in, total_in, low):
    half = tokens // 2
    end = count_starts(starts_ref, row, base + half - 1)
    passing = (end == count_starts(starts_ref, row, base - 1)).astype(F32)
    seg = seg_grid(starts_ref, row, base, (half, PAIR), 0)
    key = k[:half] * (seg == end).astype(F32).astype(BF)
    state = passing * state_in.astype(F32) + compact(dot(key, v[:half], 0, 0), low)
    total = passing * total_in + jnp.sum(key.astype(F32), 0, keepdims=True)
    later = seg_grid(starts_ref, row, base + half, (half, PAIR), 0)
    return state.astype(BF), total, (later == end).astype(F32)


def entering_mask(starts_ref, row, base, tokens):
    seg = seg_grid(starts_ref, row, base, (tokens, PAIR), 0)
    return (seg == count_starts(starts_ref, row, base - 1)).astype(F32)


def leaving_mask(starts_ref, row, base, tokens):
    seg = seg_grid(starts_ref, row, base, (tokens, PAIR), 0)
    return (seg == count_starts(starts_ref, row, base + tokens - 1)).astype(F32)


def rotate(x, same, down, up):
    half = ROT // 2
    return x * same + pltpu.roll(x, PAIR - half, 1) * down + pltpu.roll(x, half, 1) * up


def rotate_back(x, same, down, up):
    half = ROT // 2
    return x * same + pltpu.roll(x * down, half, 1) + pltpu.roll(x * up, PAIR - half, 1)


def compact(state, low):
    return jnp.where(low[:HD], state[:HD], state[HD:])


def spread(state, first, second):
    return jnp.concatenate([state * first[:HD], state * second[:HD]], 0)


def features_kernel(
    starts_ref, place_ref, norm_ref, weight_ref, bias_ref, feat_ref,
    same_ref, down_ref, up_ref, high_ref, low_ref,
    q_ref, k_ref, v_ref, state_ref, total_ref,
):
    tokens = same_ref.shape[0]
    base = place_ref[0, 0] * tokens
    low, first, second = lane_masks(tokens)
    feat = feat_ref[0]
    for row in range(MB * ROWS):
        here = slice(row * tokens, (row + 1) * tokens)
        proj = dot(norm_ref[here, :], weight_ref[...]) + bias_ref[0]
        c0, c1, c2 = proj[:, :PAIR], proj[:, PAIR : 2 * PAIR], proj[:, 2 * PAIR :]
        query = jnp.where(low, c0, c1)
        key = pltpu.roll(jnp.where(low, c2, c0), HD, 1)
        value = jnp.where(low, c1, c2).astype(BF)
        out = []
        for x in (query, key):
            x = rotate(x, same_ref[...], down_ref[...], up_ref[...])
            arg = split_dot(x, high_ref[...]) + dot(x.astype(BF), low_ref[...])
            out.append((feat * jnp.exp(arg)).astype(BF))
        q_ref[here, :] = out[0]
        k_ref[here, :] = out[1]
        v_ref[here, :] = value
        leaving = leaving_mask(starts_ref, row, base, tokens)
        key_out = out[1] * leaving.astype(BF)
        state_ref[0, row] = compact(dot(key_out, value, 0, 0), low).astype(BF)
        total_ref[0, row : row + 1, :] = jnp.sum(key_out.astype(F32), 0, keepdims=True)


def attend_kernel(
    starts_ref, place_ref, q_ref, k_ref, v_ref, state_ref, total_ref, low_ref, out_ref, den_ref
):
    tokens = q_ref.shape[0] // (MB * ROWS)
    base = place_ref[0, 0] * tokens
    low, first, second = lane_masks(tokens)
    ones = head_ones()
    for row in range(MB * ROWS):
        here = slice(row * tokens, (row + 1) * tokens)
        q, k, v = q_ref[here, :], k_ref[here, :], v_ref[here, :]
        mask, mask_in = causal_mask(starts_ref, row, base, tokens)
        enter = entering_mask(starts_ref, row, base, tokens)
        state, total = state_ref[0, row], total_ref[0, row : row + 1, :]
        middle, _, reach = middle_state(starts_ref, row, base, tokens, k, v, state, total, low)
        half = tokens // 2
        num = jnp.concatenate(
            [
                dot(q[:half] * enter[:half].astype(BF), spread(state, first, second)),
                dot(q[half:] * reach.astype(BF), spread(middle, first, second)),
            ],
            0,
        )
        for head in (first, second):
            scores = dot(q * head, k, 1, 1) * mask_in
            num = num + dot(scores.astype(BF), v * head)
        totals = dot(mask.astype(BF), k) + enter * total
        den = split_dot(q.astype(F32) * totals, ones)
        att = num / den
        low_ref[here, :] = att.astype(BF)
        out_ref[here, :] = att
        den_ref[here, :] = den


def head_ones():
    rows = lax.broadcasted_iota(jnp.int32, (PAIR, PAIR), 0) < HD
    cols = lax.broadcasted_iota(jnp.int32, (PAIR, PAIR), 1) < HD
    return (rows == cols).astype(F32).astype(BF)


def head_spread():
    rows = lax.broadcasted_iota(jnp.int32, (PAIR, 2 * PAIR), 0) < HD
    cols = lax.broadcasted_iota(jnp.int32, (PAIR, 2 * PAIR), 1) < PAIR
    return (rows == cols).astype(F32).astype(BF)


def back_state_kernel(
    starts_ref, place_ref, q_ref, ga_ref, att_ref, den_ref, state_ref, total_ref
):
    tokens = q_ref.shape[0] // (MB * ROWS)
    base = place_ref[0, 0] * tokens
    low, first, second = lane_masks(tokens)
    ones = head_ones()
    for row in range(MB * ROWS):
        here = slice(row * tokens, (row + 1) * tokens)
        grad_num = (ga_ref[here, :].astype(F32) / den_ref[here, :]).astype(BF)
        grad_den = -split_dot(grad_num.astype(F32) * att_ref[here, :], ones)
        enter = entering_mask(starts_ref, row, base, tokens)
        query = q_ref[here, :] * enter.astype(BF)
        state_ref[0, row] = compact(dot(query, grad_num, 0, 0), low)
        total_ref[0, row : row + 1, :] = jnp.sum(grad_den * query.astype(F32), 0, keepdims=True)


def back_kernel(
    starts_ref, place_ref, q_ref, k_ref, v_ref, ga_ref, att_ref, den_ref,
    state_ref, total_ref, later_ref, later_total_ref, feat_ref,
    same_ref, down_ref, up_ref, high_ref, low_ref,
    grad_ref, sums_ref,
):
    tokens = q_ref.shape[0] // (MB * ROWS)
    base = place_ref[0, 0] * tokens
    low, first, second = lane_masks(tokens)
    spreading = head_spread()
    feat_sum = jnp.zeros((1, PAIR), F32)
    bias_sum = [jnp.zeros((1, PAIR), F32) for _ in range(3)]
    for row in range(MB * ROWS):
        here = slice(row * tokens, (row + 1) * tokens)
        q, k, v = q_ref[here, :], k_ref[here, :], v_ref[here, :]
        grad_num = (ga_ref[here, :].astype(F32) / den_ref[here, :]).astype(BF)
        both = -split_dot(grad_num.astype(F32) * att_ref[here, :], spreading)
        dens = (both[:, :PAIR], both[:, PAIR:])
        grad_den = jnp.where(low, dens[0], dens[1])
        mask, mask_in = causal_mask(starts_ref, row, base, tokens)
        enter = entering_mask(starts_ref, row, base, tokens)
        leave = leaving_mask(starts_ref, row, base, tokens)
        state, total = state_ref[0, row], total_ref[0, row : row + 1, :]
        middle, middle_total, reach = middle_state(
            starts_ref, row, base, tokens, k, v, state, total, low
        )
        half = tokens // 2
        gq = jnp.concatenate(
            [
                enter[:half]
                * (dot(grad_num[:half], spread(state, first, second), 1, 1) + grad_den[:half] * total),
                reach
                * (
                    dot(grad_num[half:], spread(middle, first, second), 1, 1)
                    + grad_den[half:] * middle_total
                ),
            ],
            0,
        )
        later = later_ref[0, row]
        later_high = later.astype(BF)
        later_low = spread((later - later_high.astype(F32)).astype(BF), first, second)
        later_high = spread(later_high, first, second)
        gk = leave * (
            dot(v, later_high, 1, 1) + dot(v, later_low, 1, 1) + later_total_ref[0, row : row + 1, :]
        )
        gv = leave * (dot(k, later_high) + dot(k, later_low))
        for head, den in zip((first, second), dens):
            q_head, grad_head = q * head, grad_num * head
            scores = (dot(q_head, k, 1, 1) * mask).astype(BF)
            grad_scores = dot(grad_head, v, 1, 1) + den
            gq = gq + dot((grad_scores * mask_in).astype(BF), k * head)
            gk = gk + dot((grad_scores * mask).astype(BF), q_head, 0, 0)
            gv = gv + dot(scores, grad_head, 0, 0)
        arg_grads = (gq * q.astype(F32), gk * k.astype(F32))
        feat_sum = feat_sum + jnp.sum(arg_grads[0] + arg_grads[1], 0, keepdims=True)
        turned = []
        for x in arg_grads:
            x = split_dot(x, high_ref[...], 1) + dot(x.astype(BF), low_ref[...], 1, 1)
            turned.append(rotate_back(x, same_ref[...], down_ref[...], up_ref[...]))
        dq, dk = turned[0], pltpu.roll(turned[1], HD, 1)
        parts = (jnp.where(low, dq, dk), jnp.where(low, gv, dq), jnp.where(low, dk, gv))
        for n, part in enumerate(parts):
            part = part.astype(BF)
            grad_ref[here, n * PAIR : (n + 1) * PAIR] = part
            bias_sum[n] = bias_sum[n] + jnp.sum(part.astype(F32), 0, keepdims=True)
    sums_ref[0, 0:1, :] = feat_sum / feat_ref[0]
    for n in range(3):
        sums_ref[0, n + 1 : n + 2, :] = bias_sum[n]


SMEM = pl.BlockSpec(memory_space=pltpu.SMEM)


def whole(shape):
    return pl.BlockSpec(shape, lambda p: (0,) * len(shape))


def column(rows, width):
    return pl.BlockSpec((rows, width), lambda p: (0, p))


def stacked(*shape):
    return pl.BlockSpec((1,) + shape, lambda p: (p,) + (0,) * len(shape))


def call(kernel, pairs, in_specs, out_specs, out_shape, flops):
    return pl.pallas_call(
        kernel,
        grid=(pairs,),
        in_specs=in_specs,
        out_specs=out_specs,
        out_shape=out_shape,
        compiler_params=pltpu.CompilerParams(vmem_limit_bytes=VMEM_LIMIT),
        cost_estimate=pl.CostEstimate(flops=flops, bytes_accessed=8 << 20, transcendentals=0),
    )


def shaped(shape, dtype):
    return jax.ShapeDtypeStruct(shape, dtype)


def gather_tp(value):
    if lax.axis_size("tp") != 2:
        return lax.all_gather(value, "tp", axis=1, tiled=True)
    other = lax.ppermute(value, "tp", [(0, 1), (1, 0)])
    return jnp.where(
        lax.axis_index("tp") == 0,
        jnp.concatenate([value, other], 1),
        jnp.concatenate([other, value], 1),
    )


def scatter_tp(value):
    peers = lax.axis_size("tp")
    if peers != 2:
        return lax.psum_scatter(value, "tp", scatter_dimension=1, tiled=True)
    me = lax.axis_index("tp")
    width = value.shape[1] // 2
    left, right = value[:, :width], value[:, width:]
    other = lax.ppermute(jnp.where(me == 0, right, left).astype(BF), "tp", [(0, 1), (1, 0)])
    return jnp.where(me == 0, left, right) + other.astype(F32)


def local(
    section_inputs,
    doc_starts,
    ln_gains,
    ln_shifts,
    qkv_weight,
    qkv_bias,
    feature_weight,
    dense_weight,
    out_bias,
    up_weight,
    up_bias,
    down_weight,
):
    section = lax.axis_index("pipe")
    place = lax.axis_index("ctx")
    peers = lax.axis_size("ctx")
    width = section_inputs.shape[-1]
    tokens = section_inputs.shape[3]
    rows = MB * ROWS
    total = rows * tokens
    heads = feature_weight.shape[1]
    pairs = heads // 2
    gain, shift = ln_gains[0], ln_shifts[0]
    w_qkv, w_dense, w_up, w_down = qkv_weight[0], dense_weight[0], up_weight[0], down_weight[0]
    b_qkv = qkv_bias[0].reshape(pairs, 1, 3 * PAIR)
    b_up, b_out = up_bias[0], out_bias[0]
    feat = feature_weight[0].reshape(pairs, 1, PAIR)
    starts = doc_starts.reshape(rows, NDOC)
    place_in = place.astype(jnp.int32).reshape(1, 1)
    high, low = table_pair()
    same, down, up = rotary_tables(place, tokens)
    tables = (same, down, up, high, low)
    table_specs = [whole((tokens, PAIR))] * 3 + [whole((PAIR, PAIR))] * 2
    state_shape = shaped((pairs, rows, HD, PAIR), BF)
    total_shape = shaped((pairs, 8, PAIR), F32)
    state_spec, total_spec = stacked(rows, HD, PAIR), stacked(8, PAIR)
    low_shape, full_shape = shaped((total, pairs * PAIR), BF), shaped((total, pairs * PAIR), F32)
    unit = 2 * rows * tokens * PAIR * PAIR * pairs

    ends = jnp.arange(peers, dtype=jnp.int32)[:, None, None] * tokens
    seg_last = jnp.sum((starts[None] <= ends + tokens - 1).astype(jnp.int32), 2)
    seg_prev = jnp.sum((starts[None] <= ends - 1).astype(jnp.int32), 2)
    order = jnp.arange(peers)[:, None]
    from_earlier = ((order < place) & (seg_last == seg_prev[place][None])).astype(F32)
    from_later = ((order > place) & (seg_prev == seg_last[place][None])).astype(F32)

    def carried(state, totals, weights):
        states, sums = lax.all_gather((state, totals), "ctx")
        state_in = jnp.sum(states.astype(F32) * weights[:, None, :, None, None], 0)
        padded = jnp.concatenate([weights, jnp.zeros((peers, 8 - rows), F32)], 1)
        total_in = jnp.sum(jnp.where(padded[:, None, :, None] > 0, sums, 0.0), 0)
        return state_in.astype(state.dtype), total_in

    def forward(u_low, own):
        u = u_low.astype(F32)
        centered = u - jnp.mean(u, -1, keepdims=True)
        inv = lax.rsqrt(jnp.mean(centered * centered, -1, keepdims=True) + norm_eps)
        xhat = centered * inv
        first = (xhat * gain[0] + shift[0]).astype(BF)
        second = (xhat * gain[1] + shift[1]).astype(BF)
        q, k, v, state, totals = call(
            features_kernel,
            pairs,
            [SMEM, SMEM, whole((total, D)), column(D, 3 * PAIR), stacked(1, 3 * PAIR),
             stacked(1, PAIR)] + table_specs,
            [column(total, PAIR)] * 3 + [state_spec, total_spec],
            [low_shape] * 3 + [state_shape, total_shape],
            30 * unit,
        )(starts, place_in, first, w_qkv, b_qkv, feat, *tables)
        state_in, total_in = carried(state, totals, from_earlier)
        pre = jnp.dot(second, w_up, preferred_element_type=F32) + b_up
        hidden = jax.nn.gelu(pre, approximate=False).astype(BF)
        mlp = jnp.dot(hidden, w_down, preferred_element_type=F32)
        att_low, att, den = call(
            attend_kernel,
            pairs,
            [SMEM, SMEM] + [column(total, PAIR)] * 3 + [state_spec, total_spec],
            [column(total, PAIR)] * 3,
            [low_shape, full_shape, full_shape],
            8 * unit,
        )(starts, place_in, q, k, v, state_in, total_in)
        part = jnp.dot(att_low, w_dense, preferred_element_type=F32) + mlp
        out = scatter_tp(part) + own.astype(F32) + b_out
        kept = (xhat, inv, first, second, q, k, v, pre, hidden, att_low, att, den, state_in, total_in)
        return out, kept

    def backward(dy, own, kept, want):
        xhat, inv, first, second, q, k, v, pre, hidden, att_low, att, den, state_in, total_in = kept
        ga = lax.dot_general(
            dy, w_dense, (((1,), (1,)), ((), ())), preferred_element_type=F32
        ).astype(BF)
        state, totals = call(
            back_state_kernel,
            pairs,
            [SMEM, SMEM] + [column(total, PAIR)] * 4,
            [state_spec, total_spec],
            [shaped(state_shape.shape, F32), total_shape],
            3 * unit,
        )(starts, place_in, q, ga, att, den)
        later, later_total = carried(state, totals, from_later)
        grad_hidden = lax.dot_general(
            dy, w_down, (((1,), (1,)), ((), ())), preferred_element_type=F32
        )
        cdf = 0.5 * (1.0 + lax.erf(pre * math.sqrt(0.5)))
        slope = cdf + pre * jnp.exp(-0.5 * pre * pre) * (1.0 / math.sqrt(2.0 * math.pi))
        grad_pre = (grad_hidden * slope).astype(BF)
        grad_second = lax.dot_general(
            grad_pre, w_up, (((1,), (1,)), ((), ())), preferred_element_type=F32
        )
        grad_proj, sums = call(
            back_kernel,
            pairs,
            [SMEM, SMEM] + [column(total, PAIR)] * 6
            + [state_spec, total_spec, state_spec, total_spec, stacked(1, PAIR)] + table_specs,
            [column(total, 3 * PAIR), stacked(8, PAIR)],
            [shaped((total, pairs * 3 * PAIR), BF), shaped((pairs, 8, PAIR), F32)],
            20 * unit,
        )(starts, place_in, q, k, v, ga, att, den, state_in, total_in, later, later_total, feat, *tables)
        grad_first = lax.dot_general(
            grad_proj, w_qkv, (((1,), (1,)), ((), ())), preferred_element_type=F32
        )
        both = grad_first * gain[0] + grad_second * gain[1]
        part = inv * (
            both
            - jnp.mean(both, -1, keepdims=True)
            - xhat * jnp.mean(both * xhat, -1, keepdims=True)
        )
        grad_input = scatter_tp(part) + own.astype(F32)
        if not want:
            return grad_input, None

        def weight_grad(a, b):
            return lax.dot_general(
                a, b, (((0,), (0,)), ((), ())), preferred_element_type=F32
            ).astype(BF)

        large = (
            weight_grad(hidden, dy),
            weight_grad(second, grad_pre),
            weight_grad(att_low, dy),
            weight_grad(first, grad_proj),
        )
        norm_sums = jnp.stack(
            [
                jnp.sum(grad_first * xhat, 0),
                jnp.sum(grad_second * xhat, 0),
                jnp.sum(grad_first, 0),
                jnp.sum(grad_second, 0),
            ]
        )
        small = (
            sums[:, 1:4, :].reshape(pairs * 3 * PAIR),
            sums[:, 0, :].reshape(heads, FEAT),
            jnp.sum(own.astype(F32), 0),
            jnp.sum(grad_pre.astype(F32), 0),
        )
        return grad_input, (large, norm_sums, small)

    mine = section_inputs[0].reshape(total, width)
    mine_full = gather_tp(mine)
    y0, _ = forward(mine_full, mine)
    sent = lax.ppermute(y0.astype(BF), "pipe", [(0, 1)])
    own_in = jnp.where(section == 0, mine, sent)
    full_in = jnp.where(section == 0, mine_full, gather_tp(sent))
    y1, kept = forward(full_in, own_in)
    du1, _ = backward(mine_full, mine, kept, False)
    sent = lax.ppermute(du1.astype(BF), "pipe", [(1, 0)])
    own_grad = jnp.where(section == 1, mine, sent)
    full_grad = jnp.where(section == 1, mine_full, gather_tp(sent))
    du0, (large, norm_sums, small) = backward(full_grad, own_grad, kept, True)
    g_down, g_up, g_dense, g_qkv = (
        g.astype(F32) for g in lax.psum(large, "ctx")
    )
    norm_sums = lax.psum(norm_sums, ("ctx", "tp"))
    norm_sums = lax.dynamic_slice_in_dim(norm_sums, lax.axis_index("tp") * width, width, 1)
    g_qkv_bias, g_feat, g_out_bias, g_up_bias = lax.psum(small, "ctx")
    section_ends = jnp.where(section == 0, du0, y1).reshape(1, MB, ROWS, tokens, width)
    grads = (
        norm_sums[:2], norm_sums[2:], g_qkv, g_qkv_bias, g_feat, g_dense, g_out_bias,
        g_up, g_up_bias, g_down,
    )
    return (section_ends,) + tuple(g[None] for g in grads)


def solution(mesh):
    in_specs = (
        P("pipe", None, None, "ctx", "tp"),
        P(),
        P("pipe", None, None),
        P("pipe", None, None),
        P("pipe", None, "tp"),
        P("pipe", "tp"),
        P("pipe", "tp", None),
        P("pipe", "tp", None),
        P("pipe", "tp"),
        P("pipe", None, "tp"),
        P("pipe", "tp"),
        P("pipe", "tp", None),
    )
    out_specs = (
        P("pipe", None, None, "ctx", "tp"),
        P("pipe", None, "tp"),
        P("pipe", None, "tp"),
        P("pipe", None, "tp"),
        P("pipe", "tp"),
        P("pipe", "tp", None),
        P("pipe", "tp", None),
        P("pipe", "tp"),
        P("pipe", None, "tp"),
        P("pipe", "tp"),
        P("pipe", "tp", None),
    )
    return jax.shard_map(local, mesh=mesh, in_specs=in_specs, out_specs=out_specs, check_vma=False)
```

time: 2530 us -> 675 us (0.27)
  local copies, waits for them, and re-layouts: 557 us -> 12 us
  other arithmetic: 480 us -> 51.9 us
  matrix products: 493 us -> 86 us
  waiting for transfers between devices: 533 us -> 241 us
  blocking collectives: 377 us -> 159 us
  Pallas kernels: 0 us -> 88.1 us
    dot_general x170 -> x16, matrix products: 492 us -> 85.5 us  [the longest x2 22.6 us: forward(): mlp = jnp.dot(hidden, w_down, preferred_element_type=F32)]
    psum x1, waiting for transfers between devices: 439 us -> 133 us  [local(): lax.psum(large, 'ctx')]
    add x150 -> x0, other arithmetic: 250 us -> none  [the longest x35 84.1 us: combine_carry(): late_state + late_pass[:, None, None, None] * early_state]
    all_gather x20 -> x4, blocking collectives: 211 us -> 58.4 us  [carried(): states, sums = lax.all_gather((state, totals), 'ctx')]
    unnamed x7 -> x0, blocking collectives: 112 us -> none
    reshape x55 -> x0, local copies, waits for them, and re-layouts: 97.5 us -> none  [the longest x20 39.5 us: layer_backward(): grad_attended.astype(jnp.float32)]
    pallas_call x0 -> x8, Pallas kernels: none -> 88.1 us  [the longest x2 36.5 us: backward(): call(back_kernel, pairs, [SMEM, SMEM] + [column(total, PAIR)] * 6 + [stat...]
    reduce_scatter x15 -> x0, waiting for transfers between devices: 69.8 us -> none  [the longest x5 58.9 us: layer_forward(): lax.psum_scatter(partial_sums, 'tp', scatter_dimension=1, tiled=True)]
  transfers between devices with their start and end apart: 34 -> 14, of which waited for: 15 -> 11; matrix products, arithmetic and copies ran while one was open for 37% -> 14% of each run, Pallas kernels for 0% -> 0%
where the time goes in v1:
time: 675 us; the launch traced here: 670 us
  waiting for transfers between devices  241 us (36%)
  blocking collectives  159 us (24%)
  Pallas kernels  88.1 us (13%)
  matrix products  86 us (13%)
  other arithmetic  51.9 us (8%)
  starting transfers between devices  16.9 us (3%)
  between operations  14.7 us (2%)
  local copies, waits for them, and re-layouts  12 us (2%)
    psum x1, waiting for transfers between devices, local(): lax.psum(large, 'ctx')  133 us
    psum x1, blocking collectives, local(): norm_sums = lax.psum(norm_sums, ('ctx', 'tp'))  71.7 us
    all_gather x4, blocking collectives, carried(): states, sums = lax.all_gather((state, totals), 'ctx')  58.4 us
    pallas_call x2, Pallas kernels, backward(): call(back_kernel, pairs, [SMEM, SMEM] + [column(total, PAIR)] * 6 + [stat...  36.5 us
    all_gather x4, waiting for transfers between devices, carried(): states, sums = lax.all_gather((state, totals), 'ctx')  32.3 us
    psum x1, blocking collectives, local(): g_qkv_bias, g_feat, g_out_bias, g_up_bias = lax.psum(small, 'ctx')  28.7 us
    ppermute x3, waiting for transfers between devices, gather_tp(): other = lax.ppermute(value, 'tp', [(0, 1), (1, 0)])  26.5 us
    pallas_call x2, Pallas kernels, forward(): call(features_kernel, pairs, [SMEM, SMEM, whole((total, D)), column(D, 3...  25.9 us
  transfers between devices with their start and end apart: 14, of which 11 were waited for; matrix products, arithmetic and copies ran while one was open for 14% of the time, Pallas kernels for 0%

profile of v1, /device:TPU:0, one launch (start us, length us, event | category | flops | bytes accessed | tf_op | source)
XLA Modules:
  0.0 669.9 jit_solution(13540661865525098034)
XLA Ops:
  7.2 3.0 collective-permute-start
  18.0 4.3 collective-permute-done
  27.3 13.0 %shard_map.203 = (bf16[512,512]{1,0:T(8,128)(2,1)}, bf16[512,512]{1,0:T(8,128)(2,1)}, bf16[512,512]{1,0:T(8,128)(2,1)}, bf16[4,4,64,128]{3,2,1,0:T(8,128)(2,1)}, f32[4,8,128]{2,1,0:T(8,128)}) custom-call(s32[4,4]{1,0:T(4,128)} %bitcast.129, s32[1,1]{1,0:T(1,128)} %bitcast.2.place_ref, bf16[512,1024]{1,0:T(8,128)(2,1)} %fusion.64.norm_ref, ...), custom_call_target="tpu_custom_call" | custom-call | flops 2013265920 | bytes 8388608 | tf_op jit(solution)/shard_map/pallas_call | solution.py:427
  40.6 14.9 %all-gather.1 = f32[32,8,128]{2,1,0:T(8,128)S(1)} all-gather(f32[4,8,128]{2,1,0:T(8,128)} %get-tuple-element.36), channel_id=3, replica_groups=mesh['ctx'=8,'pipe'=2,'tp'=2] {'ctx'}, dimensions={0}, use_global_device_ids=true | all-gather | bytes 147456 | tf_op jit(solution)/shard_map/all_gather | solution.py:414
  56.2 17.4 %fusion.18 = f32[512,1024]{1,0:T(8,128)} fusion(bf16[1,2048,1024]{2,1,0:T(8,128)(2,1)} %param.23, bf16[1,1024,2048]{2,1,0:T(8,128)(2,1)} %param.21, f32[2048]{0:T(1024)S(1)} %bitcast.161, f32[1024]{0:T(1024)S(1)} %bitcast.152, f32[1024]{0:T(1024)S(1)} %bitcast.147, f32[512]{0:T(512)S(1)} %add_rsqrt_fusion.1, f32[512]{0:T(512)S(1)} %broadcast_multiply_fusion.5, ...), kind=kOutput, calls=%fused_computation.23 | convolution fusion | flops 4372037632 | bytes 11554817 | tf_op jit(solution)/shard_map/dot_general | solution.py:439
  73.6 3.1 fusion.11.state_ref
  76.7 8.3 %shard_map.204 = (bf16[512,512]{1,0:T(8,128)(2,1)}, f32[512,512]{1,0:T(8,128)}, f32[512,512]{1,0:T(8,128)}) custom-call(s32[4,4]{1,0:T(4,128)} %bitcast.130, s32[1,1]{1,0:T(1,128)} %bitcast.2.place_ref, bf16[512,512]{1,0:T(8,128)(2,1)} %get-tuple-element.32.q_ref, bf16[512,512]{1,0:T(8,128)(2,1)} %get-tuple-element.33.k_ref, ...), custom_call_target="tpu_custom_call" | custom-call | flops 536870912 | bytes 8388608 | tf_op jit(solution)/shard_map/pallas_call | solution.py:440
  88.5 12.7 %collective-permute-done.1 = bf16[512,512]{1,0:T(8,128)(2,1)S(1)} collective-permute-done((bf16[512,512]{1,0:T(8,128)(2,1)S(1)}, bf16[512,512]{1,0:T(8,128)(2,1)S(1)}, u32[]{:S(2)}, u32[]{:S(2)}) %collective-permute-start.1) | collective-permute-done | bytes 524320 | tf_op jit(solution)/shard_map/ppermute | solution.py:362
  101.6 3.4 collective-permute-start.2
  105.0 10.8 %collective-permute-done.2 = bf16[512,512]{1,0:T(8,128)(2,1)S(1)} collective-permute-done((bf16[512,512]{1,0:T(8,128)(2,1)S(1)}, bf16[512,512]{1,0:T(8,128)(2,1)S(1)}, u32[]{:S(2)}, u32[]{:S(2)}) %collective-permute-start.2) | collective-permute-done | bytes 524320 | tf_op jit(solution)/shard_map/ppermute | solution.py:528
  117.3 11.0 %collective-permute-done.3 = bf16[512,512]{1,0:T(8,128)(2,1)} collective-permute-done((bf16[512,512]{1,0:T(8,128)(2,1)S(1)}, bf16[512,512]{1,0:T(8,128)(2,1)}, u32[]{:S(2)}, u32[]{:S(2)}) %collective-permute-start.3) | collective-permute-done | bytes 524320 | tf_op jit(solution)/shard_map/ppermute | solution.py:347
  132.3 13.0 %shard_map.205 = (bf16[512,512]{1,0:T(8,128)(2,1)}, bf16[512,512]{1,0:T(8,128)(2,1)}, bf16[512,512]{1,0:T(8,128)(2,1)}, bf16[4,4,64,128]{3,2,1,0:T(8,128)(2,1)}, f32[4,8,128]{2,1,0:T(8,128)}) custom-call(s32[4,4]{1,0:T(4,128)} %bitcast.131, s32[1,1]{1,0:T(1,128)} %bitcast.2.place_ref, bf16[512,1024]{1,0:T(8,128)(2,1)} %fusion.68.norm_ref, ...), custom_call_target="tpu_custom_call" | custom-call | flops 2013265920 | bytes 8388608 | tf_op jit(solution)/shard_map/pallas_call | solution.py:427
  146.9 14.1 %all-gather.3 = f32[32,8,128]{2,1,0:T(8,128)S(1)} all-gather(f32[4,8,128]{2,1,0:T(8,128)S(1)} %copy-done.15), channel_id=5, replica_groups=mesh['ctx'=8,'pipe'=2,'tp'=2] {'ctx'}, dimensions={0}, use_global_device_ids=true | all-gather | bytes 147456 | tf_op jit(solution)/shard_map/all_gather | solution.py:414
  161.8 15.2 %all-gather.15.cloned.1.call-done = bf16[32,4,64,128]{3,2,1,0:T(8,128)(2,1)} async-done(((bf16[4,4,64,128]{3,2,1,0:T(8,128)(2,1)}), bf16[32,4,64,128]{3,2,1,0:T(8,128)(2,1)}) %all-gather.15.cloned.1.call-update) | async-done | bytes 2097168 | tf_op jit(solution)/shard_map/all_gather | solution.py:414
  177.0 2.9 fusion.10.state_ref
  179.9 8.4 %shard_map.206 = (bf16[512,512]{1,0:T(8,128)(2,1)}, f32[512,512]{1,0:T(8,128)}, f32[512,512]{1,0:T(8,128)}) custom-call(s32[4,4]{1,0:T(4,128)} %bitcast.132, s32[1,1]{1,0:T(1,128)} %bitcast.2.place_ref, bf16[512,512]{1,0:T(8,128)(2,1)} %get-tuple-element.38.q_ref, bf16[512,512]{1,0:T(8,128)(2,1)} %get-tuple-element.39.k_ref, ...), custom_call_target="tpu_custom_call" | custom-call | flops 536870912 | bytes 8388608 | tf_op jit(solution)/shard_map/pallas_call | solution.py:440
  188.3 4.5 shard_map.207
  193.7 14.4 %fusion.9 = (bf16[512,2048]{1,0:T(8,128)(2,1)}, f32[512,2048]{1,0:T(8,128)}) fusion(f32[2048]{0:T(1024)S(1)} %bitcast.162, bf16[1,1024,2048]{2,1,0:T(8,128)(2,1)} %param.21, bf16[512,1024]{1,0:T(8,128)(2,1)S(1)} %get-tuple-element.143, f32[512]{0:T(512)S(1)} %add_rsqrt_fusion, f32[512]{0:T(512)S(1)} %broadcast_multiply_fusion.4, f32[1024]{0:T(1024)S(1)} %bitcast.153, ...), kind=kOutput, calls=%fused_computation.12 | convolution fusion | flops 2219835392 | bytes 11554816 | tf_op jit(solution)/shard_map/dot_general | solution.py:437
  208.2 10.8 %fusion.22 = f32[512,1024]{1,0:T(8,128)} fusion(bf16[1,1024,2048]{2,1,0:T(8,128)(2,1)} %param.21, bf16[1,2048,1024]{2,1,0:T(8,128)(2,1)} %param.23, bf16[512,512]{1,0:T(8,128)(2,1)S(1)} %collective-permute-done, bf16[512,512]{1,0:T(8,128)(2,1)S(1)} %bitcast.117, pred[]{:T(512)S(6)} %eq.64, f32[512,2048]{1,0:T(8,128)} %get-tuple-element.159, ...), kind=kOutput, calls=%fused_computation.27 | convolution fusion | flops 4311220224 | bytes 15736833 | tf_op jit(solution)/shard_map/dot_general | solution.py:473
  219.0 14.5 %all-gather.5 = f32[32,8,128]{2,1,0:T(8,128)S(1)} all-gather(f32[4,8,128]{2,1,0:T(8,128)S(1)} %copy-done.14), channel_id=7, replica_groups=mesh['ctx'=8,'pipe'=2,'tp'=2] {'ctx'}, dimensions={0}, use_global_device_ids=true | all-gather | bytes 147456 | tf_op jit(solution)/shard_map/all_gather | solution.py:414
  234.2 6.6 all-gather.17.cloned.1.call-done
  240.8 3.7 multiply_reduce_fusion.1.later_ref
  244.6 18.1 %shard_map.208 = (bf16[512,1536]{1,0:T(8,128)(2,1)}, f32[4,8,128]{2,1,0:T(8,128)}) custom-call(s32[4,4]{1,0:T(4,128)} %bitcast.134, s32[1,1]{1,0:T(1,128)} %bitcast.2.place_ref, bf16[512,512]{1,0:T(8,128)(2,1)} %get-tuple-element.38.q_ref, bf16[512,512]{1,0:T(8,128)(2,1)} %get-tuple-element.39.k_ref, bf16[512,512]{1,0:T(8,128)(2,1)} %get-tuple-element.40.v_ref, ...), custom_call_target="tpu_custom_call" | custom-call | flops 1342177280 | bytes 8388608 | tf_op jit(solution)/shard_map/pallas_call | solution.py:476
  262.7 4.2 fusion.174
  269.1 12.6 %collective-permute-done.4 = bf16[512,512]{1,0:T(8,128)(2,1)S(1)} collective-permute-done((bf16[512,512]{1,0:T(8,128)(2,1)S(1)}, bf16[512,512]{1,0:T(8,128)(2,1)S(1)}, u32[]{:S(2)}, u32[]{:S(2)}) %collective-permute-start.4) | collective-permute-done | bytes 524320 | tf_op jit(solution)/shard_map/ppermute | solution.py:362
  283.4 13.9 %collective-permute-done.5 = bf16[512,512]{1,0:T(8,128)(2,1)} collective-permute-done((bf16[512,512]{1,0:T(8,128)(2,1)S(1)}, bf16[512,512]{1,0:T(8,128)(2,1)}, u32[]{:S(2)}, u32[]{:S(2)}) %collective-permute-start.5) | collective-permute-done | bytes 524320 | tf_op jit(solution)/shard_map/ppermute | solution.py:533
  298.8 11.1 %collective-permute-done.6 = bf16[512,512]{1,0:T(8,128)(2,1)} collective-permute-done((bf16[512,512]{1,0:T(8,128)(2,1)}, bf16[512,512]{1,0:T(8,128)(2,1)}, u32[]{:S(2)}, u32[]{:S(2)}) %collective-permute-start.6) | collective-permute-done | bytes 524320 | tf_op jit(solution)/shard_map/ppermute | solution.py:347
  314.7 4.5 shard_map.209
  319.2 14.8 %all-gather.7 = f32[32,8,128]{2,1,0:T(8,128)S(1)} all-gather(f32[4,8,128]{2,1,0:T(8,128)} %get-tuple-element.49), channel_id=9, replica_groups=mesh['ctx'=8,'pipe'=2,'tp'=2] {'ctx'}, dimensions={0}, use_global_device_ids=true | all-gather | bytes 147456 | tf_op jit(solution)/shard_map/all_gather | solution.py:414
  334.7 3.1 fusion.83
  337.9 6.5 convert_bitcast_fusion
  344.3 3.8 convert_reduce_fusion
  349.6 4.6 convert_bitcast_fusion.1
  354.2 10.4 %all-gather.19.cloned.1.call-done = f32[32,4,64,128]{3,2,1,0:T(8,128)} async-done(((f32[4,4,64,128]{3,2,1,0:T(8,128)}), f32[32,4,64,128]{3,2,1,0:T(8,128)}) %all-gather.19.cloned.1.call-update) | async-done | bytes 4194320 | tf_op jit(solution)/shard_map/all_gather | solution.py:414
  364.6 3.7 multiply_reduce_fusion.later_ref
  368.3 18.4 %shard_map.210 = (bf16[512,1536]{1,0:T(8,128)(2,1)}, f32[4,8,128]{2,1,0:T(8,128)}) custom-call(s32[4,4]{1,0:T(4,128)} %bitcast.136, s32[1,1]{1,0:T(1,128)} %bitcast.2.place_ref, bf16[512,512]{1,0:T(8,128)(2,1)} %get-tuple-element.38.q_ref, bf16[512,512]{1,0:T(8,128)(2,1)} %get-tuple-element.39.k_ref, bf16[512,512]{1,0:T(8,128)(2,1)} %get-tuple-element.40.v_ref, ...), custom_call_target="tpu_custom_call" | custom-call | flops 1342177280 | bytes 8388608 | tf_op jit(solution)/shard_map/pallas_call | solution.py:476
  386.7 4.9 fusion.42
  391.7 5.2 fusion.12
  401.3 2.4 fusion.20
  403.7 2.6 fusion.173
  409.6 71.7 %psum.63 = f32[4,1024]{1,0:T(4,128)S(1)} all-reduce(f32[4,1024]{1,0:T(4,128)S(1)} %pad_maximum_fusion), channel_id=1, replica_groups=mesh['ctx'=8,'pipe'=2,'tp'=2] {'ctx','tp'}, use_global_device_ids=true, to_apply=%region_22.23 | all-reduce | flops 4096 | bytes 32768 | tf_op jit(solution)/shard_map/psum | solution.py:540
  482.0 4.2 convert_reduce_fusion.3
  486.2 28.7 %all-reduce.4 = (f32[1,1536]{1,0:T(1,128)}, f32[1,8,64]{2,1,0:T(8,128)}, f32[1,512]{1,0:T(1,128)}, f32[1,2048]{1,0:T(1,128)}) all-reduce(f32[1,1536]{1,0:T(1,128)S(1)} %broadcast_in_dim.118, f32[1,8,64]{2,1,0:T(8,128)S(1)} %broadcast_in_dim.119, f32[1,512]{1,0:T(1,128)S(1)} %bitcast.146, ...), channel_id=1, replica_groups=mesh['ctx'=8,'pipe'=2,'tp'=2] {'ctx'}, use_global_device_ids=true, to_apply=%region_24.25 | all-reduce | flops 4608 | bytes 36864 | tf_op jit(solution)/shard_map/psum | solution.py:542
  514.9 132.5 %all-reduce.8.cloned.1.call-done = (bf16[1,1024,1536]{2,1,0:T(8,128)(2,1)}, bf16[1,512,1024]{2,1,0:T(8,128)(2,1)}, bf16[1,1024,2048]{2,1,0:T(8,128)(2,1)}, bf16[1,2048,1024]{2,1,0:T(8,128)(2,1)}) async-done(((bf16[1,1024,1536]{2,1,0:T(8,128)(2,1)}, bf16[1,512,1024]{2,1,0:T(8,128)(2,1)}, bf16[1,1024,2048]{2,1,0:T(8,128)(2,1)}, bf16[1,2048,1024]{2,1,0:T(8,128)(2,1)}), (bf16[1,1024,1536]{2,1,0:T(8,128)(2,1)}, ...) | async-done | bytes 12582928 | tf_op jit(solution)/shard_map/psum | solution.py:538
  647.5 2.9 broadcast_in_dim.121
  650.4 3.6 broadcast_in_dim.117
  654.0 4.4 broadcast_in_dim.124
  658.4 4.4 broadcast_in_dim.127
  (141 shorter events, 47.5 us)
Async XLA Ops:
  7.2 77.9 %copy-start = (bf16[1,512,1024]{2,1,0:T(8,128)(2,1)S(1)}, bf16[1,512,1024]{2,1,0:T(8,128)(2,1)}, u32[]{:S(2)}) copy-start(bf16[1,512,1024]{2,1,0:T(8,128)(2,1)} %param.19) | copy-start | bytes 3145732
  7.2 18.6 %copy-start.1 = (bf16[1,4,1,128,512]{4,3,2,1,0:T(8,128)(2,1)S(1)}, bf16[1,4,1,128,512]{4,3,2,1,0:T(8,128)(2,1)}, u32[]{:S(2)}) copy-start(bf16[1,4,1,128,512]{4,3,2,1,0:T(8,128)(2,1)} %param.12) | copy-start | bytes 1572868
  7.2 66.4 %all-gather.13.cloned.1.call-start = ((), (), s32[]{:S(2)}) async-start(), calls=%async_computation | async-start | bytes 2359296 | tf_op jit(solution)/shard_map/all_gather | solution.py:414
  7.2 15.1 %collective-permute-start = (bf16[512,512]{1,0:T(8,128)(2,1)}, bf16[512,512]{1,0:T(8,128)(2,1)S(1)}, u32[]{:S(2)}, u32[]{:S(2)}) collective-permute-start(bf16[512,512]{1,0:T(8,128)(2,1)} %bitcast.110), channel_id=1, source_target_pairs={{0,1},{1,0},{2,3},{3,2},{4,5},{5,4},{6,7},{7,6},{8,9},{9,8},{10,11... | collective-permute-start | bytes 1572872 | tf_op jit(solution)/shard_map/ppermute | solution.py:347
  27.3 28.9 %copy-start.23 = (f32[1,2048]{1,0:T(1,128)S(1)}, f32[1,2048]{1,0:T(1,128)}, u32[]{:S(2)}) copy-start(f32[1,2048]{1,0:T(1,128)} %param.22) | copy-start | bytes 24580
  40.3 136.7 %all-gather.15.cloned.1.call-start = ((), (), s32[]{:S(2)}) async-start(), calls=%async_computation.1 | async-start | bytes 2359296 | tf_op jit(solution)/shard_map/all_gather | solution.py:414
  73.6 11.4 %copy-start.7 = (f32[512,1024]{1,0:T(8,128)S(1)}, f32[512,1024]{1,0:T(8,128)}, u32[]{:S(2)}) copy-start(f32[512,1024]{1,0:T(8,128)} %fusion.18) | copy-start | bytes 6291460
  76.7 24.4 %copy-start.16 = (f32[1,512]{1,0:T(1,128)S(1)}, f32[1,512]{1,0:T(1,128)}, u32[]{:S(2)}) copy-start(f32[1,512]{1,0:T(1,128)} %param.20) | copy-start | bytes 6148
  86.9 14.2 %collective-permute-start.1 = (bf16[512,512]{1,0:T(8,128)(2,1)S(1)}, bf16[512,512]{1,0:T(8,128)(2,1)S(1)}, u32[]{:S(2)}, u32[]{:S(2)}) collective-permute-start(bf16[512,512]{1,0:T(8,128)(2,1)S(1)} %select_convert_fusion.3), channel_id=1, source_target_pairs={{0,1},{1,0},{2,3},{3,2},{4,5},{5,4},{6,7},{7,6},{8,9},{9,8},{10,11... | collective-permute-start | bytes 1572872 | tf_op jit(solution)/shard_map/ppermute | solution.py:362
  101.6 14.2 %collective-permute-start.2 = (bf16[512,512]{1,0:T(8,128)(2,1)S(1)}, bf16[512,512]{1,0:T(8,128)(2,1)S(1)}, u32[]{:S(2)}, u32[]{:S(2)}) collective-permute-start(bf16[512,512]{1,0:T(8,128)(2,1)S(1)} %fusion.85), channel_id=1, source_target_pairs={{0,2},{1,3},{4,6},{5,7},{8,10},{9,11},{12,14},{13,15},{16,18},{17,... | collective-permute-start | bytes 1572872 | tf_op jit(solution)/shard_map/ppermute | solution.py:528
  115.8 1.5 copy-start.8
  115.8 12.5 %collective-permute-start.3 = (bf16[512,512]{1,0:T(8,128)(2,1)S(1)}, bf16[512,512]{1,0:T(8,128)(2,1)}, u32[]{:S(2)}, u32[]{:S(2)}) collective-permute-start(bf16[512,512]{1,0:T(8,128)(2,1)S(1)} %collective-permute-done.2), channel_id=1, source_target_pairs={{0,1},{1,0},{2,3},{3,2},{4,5},{5,4},{6,7},{7,6},{8,9},{9,8},{10,11... | collective-permute-start | bytes 1572872 | tf_op jit(solution)/shard_map/ppermute | solution.py:347
  145.3 1.7 copy-start.15
  145.3 95.5 %all-gather.17.cloned.1.call-start = ((), (), s32[]{:S(2)}) async-start(), calls=%async_computation.2 | async-start | bytes 4718592 | tf_op jit(solution)/shard_map/all_gather | solution.py:414
  192.8 171.8 %all-gather.19.cloned.1.call-start = ((), (), s32[]{:S(2)}) async-start(), calls=%async_computation.3 | async-start | bytes 4718592 | tf_op jit(solution)/shard_map/all_gather | solution.py:414
  208.2 10.8 %copy-start.14 = (f32[4,8,128]{2,1,0:T(8,128)S(1)}, f32[4,8,128]{2,1,0:T(8,128)}, u32[]{:S(2)}) copy-start(f32[4,8,128]{2,1,0:T(8,128)} %get-tuple-element.46) | copy-start | bytes 49156
  240.8 21.9 %copy-start.20 = (bf16[1,1024,1536]{2,1,0:T(8,128)(2,1)S(1)}, bf16[1,1024,1536]{2,1,0:T(8,128)(2,1)}, u32[]{:S(2)}) copy-start(bf16[1,1024,1536]{2,1,0:T(8,128)(2,1)} %param.16) | copy-start | bytes 9437188
  267.6 14.1 %collective-permute-start.4 = (bf16[512,512]{1,0:T(8,128)(2,1)S(1)}, bf16[512,512]{1,0:T(8,128)(2,1)S(1)}, u32[]{:S(2)}, u32[]{:S(2)}) collective-permute-start(bf16[512,512]{1,0:T(8,128)(2,1)S(1)} %select_convert_fusion.2), channel_id=1, source_target_pairs={{0,1},{1,0},{2,3},{3,2},{4,5},{5,4},{6,7},{7,6},{8,9},{9,8},{10,11... | collective-permute-start | bytes 1572872 | tf_op jit(solution)/shard_map/ppermute | solution.py:362
  282.1 15.2 %collective-permute-start.5 = (bf16[512,512]{1,0:T(8,128)(2,1)S(1)}, bf16[512,512]{1,0:T(8,128)(2,1)}, u32[]{:S(2)}, u32[]{:S(2)}) collective-permute-start(bf16[512,512]{1,0:T(8,128)(2,1)S(1)} %fusion.86), channel_id=1, source_target_pairs={{2,0},{3,1},{6,4},{7,5},{10,8},{11,9},{14,12},{15,13},{18,16},{19,... | collective-permute-start | bytes 1572872 | tf_op jit(solution)/shard_map/ppermute | solution.py:533
  297.4 12.6 %collective-permute-start.6 = (bf16[512,512]{1,0:T(8,128)(2,1)}, bf16[512,512]{1,0:T(8,128)(2,1)}, u32[]{:S(2)}, u32[]{:S(2)}) collective-permute-start(bf16[512,512]{1,0:T(8,128)(2,1)} %collective-permute-done.5), channel_id=1, source_target_pairs={{0,1},{1,0},{2,3},{3,2},{4,5},{5,4},{6,7},{7,6},{8,9},{9,8},{10,11... | collective-permute-start | bytes 1572872 | tf_op jit(solution)/shard_map/ppermute | solution.py:347
  312.2 1.0 copy-start.11
  319.2 328.3 %all-reduce.8.cloned.1.call-start = ((), (), s32[]{:S(2)}) async-start(), calls=%async_computation.4 | async-start | bytes 25165824 | tf_op jit(solution)/shard_map/psum | solution.py:538
  337.9 6.5 copy-start.12
  337.9 6.5 copy-start.18
  337.9 6.5 copy-start.26
  348.2 1.4 copy-start.24
  364.6 22.1 %copy-start.10 = (bf16[512,1024]{1,0:T(8,128)(2,1)S(1)}, bf16[512,1024]{1,0:T(8,128)(2,1)}, u32[]{:S(2)}) copy-start(bf16[512,1024]{1,0:T(8,128)(2,1)} %fusion.68.norm_ref) | copy-start | bytes 3145732
  391.6 5.2 copy-start.13
  396.9 4.4 copy-start.19
  396.9 4.4 copy-start.25
  397.6 1.3 copy-start.3
  399.8 3.8 copy-start.21
  399.8 3.8 copy-start.22
  399.8 82.2 %collective-permute-start.8 = (bf16[512,512]{1,0:T(8,128)(2,1)}, bf16[512,512]{1,0:T(8,128)(2,1)}, u32[]{:S(2)}, u32[]{:S(2)}) collective-permute-start(bf16[512,512]{1,0:T(8,128)(2,1)} %select_convert_fusion), channel_id=1, source_target_pairs={{0,1},{1,0},{2,3},{3,2},{4,5},{5,4},{6,7},{7,6},{8,9},{9,8},{10,11... | collective-permute-start | bytes 1572872 | tf_op jit(solution)/shard_map/ppermute | solution.py:362
  406.2 3.2 copy-start.17
  406.2 75.8 %copy-start.9 = (bf16[512,512]{1,0:T(8,128)(2,1)S(1)}, bf16[512,512]{1,0:T(8,128)(2,1)}, u32[]{:S(2)}) copy-start(bf16[512,512]{1,0:T(8,128)(2,1)} %copy-done.8) | copy-start | bytes 1572868
  406.9 1.4 copy-start.2
  408.4 73.6 %collective-permute-start.7 = (bf16[512,512]{1,0:T(8,128)(2,1)S(1)}, bf16[512,512]{1,0:T(8,128)(2,1)S(1)}, u32[]{:S(2)}, u32[]{:S(2)}) collective-permute-start(bf16[512,512]{1,0:T(8,128)(2,1)S(1)} %select_convert_fusion.1), channel_id=1, source_target_pairs={{0,1},{1,0},{2,3},{3,2},{4,5},{5,4},{6,7},{7,6},{8,9},{9,8},{10,11... | collective-permute-start | bytes 1572872 | tf_op jit(solution)/shard_map/ppermute | solution.py:362
  647.5 2.9 copy-start.6
  650.4 3.6 copy-start.5
  654.0 4.5 copy-start.4
Sparse Core Ops, SparseCore 0:
  40.4 30.7 all-gather.12
  145.4 31.5 all-gather.14
  193.0 47.8 all-gather.16
  319.3 45.2 all-gather.18
  391.8 255.6 all-reduce.7

commit v2 on v1

--- a/solution.py
+++ b/solution.py
@@ -22,6 +22,7 @@
 HIGHEST = lax.Precision.HIGHEST
 norm_eps = 1e-05
 VMEM_LIMIT = 56 * 1024 * 1024
+REDUCE_LIMIT = 60 * 1024 * 1024
 
 
 def feature_table():
@@ -339,6 +340,213 @@
 
 def shaped(shape, dtype):
     return jax.ShapeDtypeStruct(shape, dtype)
+
+
+CHUNK = 256
+PANEL = 512
+RING = 4
+LAG = 6
+
+
+def reduce_kernel(plan, *refs):
+    count, terms = plan
+    factors, small_ref = refs[: 2 * len(terms)], refs[2 * len(terms)]
+    outs = refs[2 * len(terms) + 1 : 3 * len(terms) + 2]
+    (
+        work, give, take, part, outside, inside,
+        give_send, give_recv, part_send, outer_recv, inner_recv, total_send,
+        final_send, final_recv, own_sem,
+    ) = refs[3 * len(terms) + 2 :]
+    half = CHUNK // 2
+    place, peers = lax.axis_index("ctx"), lax.axis_size("ctx")
+    core, z, chips = place % 2, place // 2, peers // 2
+    below = z < chips // 2
+    middle = (z == chips // 2 - 1) | (z == chips // 2)
+    has_outer = (z != 0) & (z != chips - 1)
+    step = jnp.where(below, 2, -2)
+    inner, outer, twin = place + step, place - step, place + 1 - 2 * core
+    mine = pl.ds(pl.multiple_of(core * half, half), half)
+    theirs = pl.ds(pl.multiple_of((1 - core) * half, half), half)
+
+    def remote(src, dst, send, recv, to):
+        return pltpu.make_async_remote_copy(
+            src_ref=src, dst_ref=dst, send_sem=send, recv_sem=recv,
+            device_id={"ctx": to}, device_id_type=pl.DeviceIdType.MESH,
+        )
+
+    def give_copy(t):
+        return remote(give.at[t], take.at[t], give_send.at[t], give_recv.at[t], twin)
+
+    def to_outside(t):
+        return remote(part.at[t], outside.at[t], part_send.at[t], outer_recv.at[t], inner)
+
+    def across(t):
+        return remote(part.at[t], inside.at[t], part_send.at[t], inner_recv.at[t], inner)
+
+    def outward(t):
+        return remote(take.at[t], inside.at[t], total_send.at[t], inner_recv.at[t], outer)
+
+    def final_copy(t, target):
+        return remote(take.at[t], target, final_send.at[t], final_recv.at[t], twin)
+
+    def own_copy(t, target):
+        return pltpu.make_async_copy(take.at[t], target, own_sem.at[t])
+
+    def block_of(j, panels):
+        rows = (j // panels) * CHUNK
+        return rows, pl.ds(pl.multiple_of((j % panels) * PANEL, PANEL), PANEL)
+
+    def deliver(t, target):
+        final_copy(t, target).start()
+        own_copy(t, target).start()
+
+    some_target = outs[-1].at[mine]
+
+    barrier = pltpu.get_barrier_semaphore()
+    for peer in (inner, twin):
+        pl.semaphore_signal(
+            barrier, inc=1, device_id={"ctx": peer}, device_id_type=pl.DeviceIdType.MESH
+        )
+
+    @pl.when(has_outer)
+    def _():
+        pl.semaphore_signal(
+            barrier, inc=1, device_id={"ctx": outer}, device_id_type=pl.DeviceIdType.MESH
+        )
+
+    pl.semaphore_wait(barrier, 2 + has_outer.astype(jnp.int32))
+    lag = jnp.where(middle, 2, LAG)
+
+    def one(t, carry):
+        slot = t % RING
+        begin = 0
+        for n, (blocks, panels) in enumerate(terms):
+            left, right = factors[2 * n], factors[2 * n + 1]
+
+            @pl.when((t >= begin) & (t < begin + blocks * panels))
+            def _(left=left, right=right, panels=panels, begin=begin):
+                start, cols = block_of(t - begin, panels)
+                rows = pl.ds(pl.multiple_of(start, CHUNK), CHUNK)
+                work[slot] = dot(left[:, rows], right[:, cols], 0, 0)
+
+            begin += blocks * panels
+
+        @pl.when(t == begin)
+        def _():
+            work[slot] = small_ref[...]
+
+        @pl.when(t < count)
+        def _():
+            give[t] = work[slot, theirs, :].astype(BF)
+            give_copy(t).start()
+
+        tb = t - 1
+
+        @pl.when((tb >= 0) & (tb < count))
+        def _():
+            give_copy(tb).wait_recv()
+            total = work[(t + RING - 1) % RING, mine, :] + take[tb].astype(F32)
+
+            @pl.when(has_outer)
+            def _():
+                to_outside(tb).wait_recv()
+                part[tb] = (total + outside[tb].astype(F32)).astype(BF)
+
+            @pl.when(jnp.logical_not(has_outer))
+            def _():
+                part[tb] = total.astype(BF)
+
+            @pl.when(middle)
+            def _():
+                across(tb).start()
+
+            @pl.when(jnp.logical_not(middle))
+            def _():
+                to_outside(tb).start()
+
+        tc = t - lag
+
+        @pl.when((tc >= 0) & (tc < count))
+        def _():
+            across(tc).wait_recv()
+
+            @pl.when(middle)
+            def _():
+                take[tc] = (part[tc].astype(F32) + inside[tc].astype(F32)).astype(BF)
+
+            @pl.when(jnp.logical_not(middle))
+            def _():
+                take[tc] = inside[tc]
+
+            @pl.when(has_outer)
+            def _():
+                outward(tc).start()
+
+            begin = 0
+            for n, (blocks, panels) in enumerate(terms):
+
+                @pl.when((tc >= begin) & (tc < begin + blocks * panels))
+                def _(n=n, panels=panels, begin=begin):
+                    start, cols = block_of(tc - begin, panels)
+                    rows = pl.ds(pl.multiple_of(start + core * half, half), half)
+                    deliver(tc, outs[n].at[rows, cols])
+
+                begin += blocks * panels
+
+            @pl.when(tc == begin)
+            def _():
+                deliver(tc, some_target)
+
+        return carry
+
+    lax.fori_loop(0, count + LAG, one, 0)
+
+    def drain(t, carry):
+        give_copy(t).wait_send()
+        across(t).wait_send()
+        final_copy(t, some_target).wait_send()
+        final_copy(t, some_target).wait_recv()
+        own_copy(t, some_target).wait()
+
+        @pl.when(has_outer)
+        def _():
+            outward(t).wait_send()
+
+        return carry
+
+    lax.fori_loop(0, count, drain, 0)
+
+
+def reduce_over_ctx(factors, small):
+    terms = tuple((a.shape[1] // CHUNK, b.shape[1] // PANEL) for a, b in factors)
+    count = sum(x * y for x, y in terms) + 1
+    half = CHUNK // 2
+    flat = [x for pair in factors for x in pair] + [small]
+    slots = pltpu.VMEM((count, half, PANEL), BF)
+    sums = pl.pallas_call(
+        partial(reduce_kernel, (count, terms)),
+        in_specs=[pl.BlockSpec(memory_space=pltpu.VMEM)] * len(flat),
+        out_specs=[pl.BlockSpec(memory_space=pl.ANY)] * (len(terms) + 1),
+        out_shape=[shaped((a.shape[1], b.shape[1]), BF) for a, b in factors]
+        + [shaped((CHUNK, PANEL), BF)],
+        scratch_shapes=[pltpu.VMEM((RING, CHUNK, PANEL), F32)]
+        + [slots] * 5
+        + [pltpu.SemaphoreType.DMA((count,))] * 9,
+        compiler_params=pltpu.CompilerParams(
+            collective_id=0, has_side_effects=True, vmem_limit_bytes=REDUCE_LIMIT
+        ),
+        cost_estimate=pl.CostEstimate(
+            flops=count * 2 * CHUNK * PANEL * 512, bytes_accessed=40 << 20, transcendentals=0
+        ),
+    )(*flat)
+    return [g.astype(F32) for g in sums[:-1]], sums[-1].astype(F32)
+
+
+def fits_reduce(factors):
+    even = lax.axis_size("ctx") % 4 == 0
+    return even and all(
+        a.shape[1] % CHUNK == 0 and b.shape[1] % PANEL == 0 for a, b in factors
+    )
 
 
 def gather_tp(value):
@@ -495,17 +703,7 @@
         if not want:
             return grad_input, None
 
-        def weight_grad(a, b):
-            return lax.dot_general(
-                a, b, (((0,), (0,)), ((), ())), preferred_element_type=F32
-            ).astype(BF)
-
-        large = (
-            weight_grad(hidden, dy),
-            weight_grad(second, grad_pre),
-            weight_grad(att_low, dy),
-            weight_grad(first, grad_proj),
-        )
+        large = ((hidden, dy), (second, grad_pre), (att_low, dy), (first, grad_proj))
         norm_sums = jnp.stack(
             [
                 jnp.sum(grad_first * xhat, 0),
@@ -534,12 +732,27 @@
     own_grad = jnp.where(section == 1, mine, sent)
     full_grad = jnp.where(section == 1, mine_full, gather_tp(sent))
     du0, (large, norm_sums, small) = backward(full_grad, own_grad, kept, True)
-    g_down, g_up, g_dense, g_qkv = (
-        g.astype(F32) for g in lax.psum(large, "ctx")
-    )
-    norm_sums = lax.psum(norm_sums, ("ctx", "tp"))
-    norm_sums = lax.dynamic_slice_in_dim(norm_sums, lax.axis_index("tp") * width, width, 1)
-    g_qkv_bias, g_feat, g_out_bias, g_up_bias = lax.psum(small, "ctx")
+    if lax.axis_size("tp") == 2:
+        me = lax.axis_index("tp")
+        away = lax.dynamic_slice_in_dim(norm_sums, (1 - me) * width, width, 1)
+        norm_sums = lax.dynamic_slice_in_dim(norm_sums, me * width, width, 1)
+        norm_sums = norm_sums + lax.ppermute(away, "tp", [(0, 1), (1, 0)])
+    else:
+        norm_sums = lax.psum_scatter(norm_sums, "tp", scatter_dimension=1, tiled=True)
+    small = small + (norm_sums,)
+    if fits_reduce(large):
+        flat = jnp.concatenate([x.reshape(-1) for x in small])
+        flat = jnp.pad(flat, (0, CHUNK * PANEL - flat.size)).reshape(CHUNK, PANEL)
+        (g_down, g_up, g_dense, g_qkv), flat = reduce_over_ctx(large, flat)
+        flat, summed, begin = flat.reshape(-1), [], 0
+        for x in small:
+            summed.append(flat[begin : begin + x.size].reshape(x.shape))
+            begin += x.size
+    else:
+        products = tuple(dot(a, b, 0, 0).astype(BF) for a, b in large)
+        g_down, g_up, g_dense, g_qkv = (g.astype(F32) for g in lax.psum(products, "ctx"))
+        summed = lax.psum(small, "ctx")
+    g_qkv_bias, g_feat, g_out_bias, g_up_bias, norm_sums = summed
     section_ends = jnp.where(section == 0, du0, y1).reshape(1, MB, ROWS, tokens, width)
     grads = (
         norm_sums[:2], norm_sums[2:], g_qkv, g_qkv_bias, g_feat, g_dense, g_out_bias,

time: 675 us -> 610 us (0.904)
  Pallas kernels: 88.1 us -> 249 us
  waiting for transfers between devices: 241 us -> 123 us
  blocking collectives: 159 us -> 58.5 us
  matrix products: 86 us -> 70.7 us
    pallas_call x0 -> x1, Pallas kernels: none -> 161 us  [reduce_over_ctx(): pl.pallas_call(partial(reduce_kernel, (count, terms)), in_specs=[pl.Block...]
    psum x1 -> x0, waiting for transfers between devices: 133 us -> none  [local(): lax.psum(large, 'ctx')]
    psum x2 -> x0, blocking collectives: 100 us -> none  [the longest x1 71.7 us: local(): norm_sums = lax.psum(norm_sums, ('ctx', 'tp'))]
    dot_general x4 -> x0, matrix products: 19.1 us -> none  [weight_grad(): lax.dot_general(a, b, (((0,), (0,)), ((), ())), preferred_element_type=F32)]
    ppermute x0 -> x1, waiting for transfers between devices: none -> 12.1 us  [local(): norm_sums = norm_sums + lax.ppermute(away, 'tp', [(0, 1), (1, 0)])]
  transfers between devices with their start and end apart: 14 -> 14, of which waited for: 11 -> 11; matrix products, arithmetic and copies ran while one was open for 14% -> 13% of each run, Pallas kernels for 0% -> 3%
where the time goes in v2:
time: 610 us; the launch traced here: 605 us
  Pallas kernels  249 us (41%)
  waiting for transfers between devices  123 us (20%)
  matrix products  70.7 us (12%)
  blocking collectives  58.5 us (10%)
  other arithmetic  54.6 us (9%)
  starting transfers between devices  17.9 us (3%)
  local copies, waits for them, and re-layouts  17.2 us (3%)
  between operations  14.5 us (2%)
    pallas_call x1, Pallas kernels, reduce_over_ctx(): pl.pallas_call(partial(reduce_kernel, (count, terms)), in_specs=[pl.Block...  161 us
    all_gather x4, blocking collectives, carried(): states, sums = lax.all_gather((state, totals), 'ctx')  58.5 us
    pallas_call x2, Pallas kernels, backward(): call(back_kernel, pairs, [SMEM, SMEM] + [column(total, PAIR)] * 6 + [stat...  36.3 us
    all_gather x4, waiting for transfers between devices, carried(): states, sums = lax.all_gather((state, totals), 'ctx')  33.9 us
    ppermute x3, waiting for transfers between devices, gather_tp(): other = lax.ppermute(value, 'tp', [(0, 1), (1, 0)])  26.6 us
    pallas_call x2, Pallas kernels, forward(): call(features_kernel, pairs, [SMEM, SMEM, whole((total, D)), column(D, 3...  25.9 us
    ppermute x4, waiting for transfers between devices, scatter_tp(): lax.ppermute(jnp.where(me == 0, right, left).astype(BF), 'tp', [(0, 1), (...  25.2 us
    dot_general x2, matrix products, forward(): mlp = jnp.dot(hidden, w_down, preferred_element_type=F32)  23 us
  transfers between devices with their start and end apart: 14, of which 11 were waited for; matrix products, arithmetic and copies ran while one was open for 13% of the time, Pallas kernels for 3%

profile of v2, /device:TPU:0, one launch (start us, length us, event | category | flops | bytes accessed | tf_op | source)
XLA Modules:
  0.0 604.6 jit_solution(5084095616813330611)
XLA Ops:
  7.2 3.0 collective-permute-start
  18.0 4.4 collective-permute-done
  22.4 1.6 convert_reduce_fusion.2
  24.0 1.8 fusion.79
  27.3 13.0 %shard_map.203 = (bf16[512,512]{1,0:T(8,128)(2,1)}, bf16[512,512]{1,0:T(8,128)(2,1)}, bf16[512,512]{1,0:T(8,128)(2,1)}, bf16[4,4,64,128]{3,2,1,0:T(8,128)(2,1)}, f32[4,8,128]{2,1,0:T(8,128)}) custom-call(s32[4,4]{1,0:T(4,128)} %bitcast.137, s32[1,1]{1,0:T(1,128)} %bitcast.2.place_ref, bf16[512,1024]{1,0:T(8,128)(2,1)} %fusion.63.norm_ref, ...), custom_call_target="tpu_custom_call" | custom-call | flops 2013265920 | bytes 8388608 | tf_op jit(solution)/shard_map/pallas_call | solution.py:635
  40.6 15.0 %all-gather.1 = f32[32,8,128]{2,1,0:T(8,128)S(1)} all-gather(f32[4,8,128]{2,1,0:T(8,128)} %get-tuple-element.41), channel_id=3, replica_groups=mesh['ctx'=8,'pipe'=2,'tp'=2] {'ctx'}, dimensions={0}, use_global_device_ids=true | all-gather | bytes 147456 | tf_op jit(solution)/shard_map/all_gather | solution.py:622
  56.3 17.7 %fusion.18 = f32[512,1024]{1,0:T(8,128)} fusion(bf16[1,2048,1024]{2,1,0:T(8,128)(2,1)} %param.23, bf16[1,1024,2048]{2,1,0:T(8,128)(2,1)} %param.21, f32[2048]{0:T(1024)S(1)} %bitcast.169, f32[1024]{0:T(1024)S(1)} %bitcast.156, f32[1024]{0:T(1024)S(1)} %bitcast.152, f32[512]{0:T(512)S(1)} %add_rsqrt_fusion.1, f32[512]{0:T(512)S(1)} %broadcast_multiply_fusion.5, ...), kind=kOutput, calls=%fused_computation.25 | convolution fusion | flops 4372037632 | bytes 11554817 | tf_op jit(solution)/shard_map/dot_general | solution.py:647
  74.0 3.1 fusion.11.state_ref
  77.1 8.3 %shard_map.204 = (bf16[512,512]{1,0:T(8,128)(2,1)}, f32[512,512]{1,0:T(8,128)}, f32[512,512]{1,0:T(8,128)}) custom-call(s32[4,4]{1,0:T(4,128)} %bitcast.138, s32[1,1]{1,0:T(1,128)} %bitcast.2.place_ref, bf16[512,512]{1,0:T(8,128)(2,1)} %get-tuple-element.37.q_ref, bf16[512,512]{1,0:T(8,128)(2,1)} %get-tuple-element.38.k_ref, ...), custom_call_target="tpu_custom_call" | custom-call | flops 536870912 | bytes 8388608 | tf_op jit(solution)/shard_map/pallas_call | solution.py:648
  85.4 1.8 convolution_add_fusion.1
  88.9 12.7 %collective-permute-done.1 = bf16[512,512]{1,0:T(8,128)(2,1)S(1)} collective-permute-done((bf16[512,512]{1,0:T(8,128)(2,1)S(1)}, bf16[512,512]{1,0:T(8,128)(2,1)S(1)}, u32[]{:S(2)}, u32[]{:S(2)}) %collective-permute-start.1) | collective-permute-done | bytes 524320 | tf_op jit(solution)/shard_map/ppermute | solution.py:570
  101.9 3.5 collective-permute-start.2
  105.4 10.8 %collective-permute-done.2 = bf16[512,512]{1,0:T(8,128)(2,1)S(1)} collective-permute-done((bf16[512,512]{1,0:T(8,128)(2,1)S(1)}, bf16[512,512]{1,0:T(8,128)(2,1)S(1)}, u32[]{:S(2)}, u32[]{:S(2)}) %collective-permute-start.2) | collective-permute-done | bytes 524320 | tf_op jit(solution)/shard_map/ppermute | solution.py:726
  117.8 11.0 %collective-permute-done.3 = bf16[512,512]{1,0:T(8,128)(2,1)} collective-permute-done((bf16[512,512]{1,0:T(8,128)(2,1)S(1)}, bf16[512,512]{1,0:T(8,128)(2,1)}, u32[]{:S(2)}, u32[]{:S(2)}) %collective-permute-start.3) | collective-permute-done | bytes 524320 | tf_op jit(solution)/shard_map/ppermute | solution.py:555
  128.8 2.2 convert_reduce_fusion.1
  131.4 1.9 fusion.67
  133.3 13.0 %shard_map.205 = (bf16[512,512]{1,0:T(8,128)(2,1)}, bf16[512,512]{1,0:T(8,128)(2,1)}, bf16[512,512]{1,0:T(8,128)(2,1)}, bf16[4,4,64,128]{3,2,1,0:T(8,128)(2,1)}, f32[4,8,128]{2,1,0:T(8,128)}) custom-call(s32[4,4]{1,0:T(4,128)} %bitcast.139, s32[1,1]{1,0:T(1,128)} %bitcast.2.place_ref, bf16[512,1024]{1,0:T(8,128)(2,1)} %get-tuple-element.146.norm_ref.refs_6_, ...), custom_call_target="tpu_custom_call" | custom-call | flops 2013265920 | bytes 8388608 | tf_op jit(solution)/shard_map/pallas_call | solution.py:635
  147.9 14.1 %all-gather.3 = f32[32,8,128]{2,1,0:T(8,128)S(1)} all-gather(f32[4,8,128]{2,1,0:T(8,128)S(1)} %copy-done.15), channel_id=5, replica_groups=mesh['ctx'=8,'pipe'=2,'tp'=2] {'ctx'}, dimensions={0}, use_global_device_ids=true | all-gather | bytes 147456 | tf_op jit(solution)/shard_map/all_gather | solution.py:622
  162.7 15.3 %all-gather.15.cloned.1.call-done = bf16[32,4,64,128]{3,2,1,0:T(8,128)(2,1)} async-done(((bf16[4,4,64,128]{3,2,1,0:T(8,128)(2,1)}), bf16[32,4,64,128]{3,2,1,0:T(8,128)(2,1)}) %all-gather.15.cloned.1.call-update) | async-done | bytes 2097168 | tf_op jit(solution)/shard_map/all_gather | solution.py:622
  178.0 2.9 fusion.10.state_ref
  181.0 8.3 %shard_map.206 = (bf16[512,512]{1,0:T(8,128)(2,1)}, f32[512,512]{1,0:T(8,128)}, f32[512,512]{1,0:T(8,128)}) custom-call(s32[4,4]{1,0:T(4,128)} %bitcast.140, s32[1,1]{1,0:T(1,128)} %bitcast.2.place_ref, bf16[512,512]{1,0:T(8,128)(2,1)} %get-tuple-element.43.q_ref, bf16[512,512]{1,0:T(8,128)(2,1)} %get-tuple-element.44.k_ref, ...), custom_call_target="tpu_custom_call" | custom-call | flops 536870912 | bytes 8388608 | tf_op jit(solution)/shard_map/pallas_call | solution.py:648
  189.3 4.5 shard_map.207
  194.5 14.5 %fusion.9 = (bf16[512,2048]{1,0:T(8,128)(2,1)}, f32[512,2048]{1,0:T(8,128)}) fusion(f32[2048]{0:T(1024)S(1)} %bitcast.170, bf16[512,1024]{1,0:T(8,128)(2,1)} %get-tuple-element.147.refs_2_, bf16[1,1024,2048]{2,1,0:T(8,128)(2,1)} %param.21), kind=kOutput, calls=%fused_computation.12 | convolution fusion | flops 2216689664 | bytes 11542528 | tf_op jit(solution)/shard_map/dot_general | solution.py:645
  209.0 10.8 %fusion.22 = f32[512,1024]{1,0:T(8,128)} fusion(bf16[1,1024,2048]{2,1,0:T(8,128)(2,1)} %param.21, bf16[1,2048,1024]{2,1,0:T(8,128)(2,1)} %param.23, bf16[512,512]{1,0:T(8,128)(2,1)S(1)} %collective-permute-done, bf16[512,512]{1,0:T(8,128)(2,1)S(1)} %bitcast.125, pred[]{:T(512)S(6)} %eq.64, f32[512,2048]{1,0:T(8,128)} %get-tuple-element.163, ...), kind=kOutput, calls=%fused_computation.29 | convolution fusion | flops 4311220224 | bytes 15736833 | tf_op jit(solution)/shard_map/dot_general | solution.py:681
  219.8 14.5 %all-gather.5 = f32[32,8,128]{2,1,0:T(8,128)S(1)} all-gather(f32[4,8,128]{2,1,0:T(8,128)S(1)} %copy-done.14), channel_id=7, replica_groups=mesh['ctx'=8,'pipe'=2,'tp'=2] {'ctx'}, dimensions={0}, use_global_device_ids=true | all-gather | bytes 147456 | tf_op jit(solution)/shard_map/all_gather | solution.py:622
  235.0 6.7 %all-gather.17.cloned.1.call-done = f32[32,4,64,128]{3,2,1,0:T(8,128)} async-done(((f32[4,4,64,128]{3,2,1,0:T(8,128)}), f32[32,4,64,128]{3,2,1,0:T(8,128)}) %all-gather.17.cloned.1.call-update) | async-done | bytes 4194320 | tf_op jit(solution)/shard_map/all_gather | solution.py:622
  241.7 3.7 multiply_reduce_fusion.1.later_ref
  245.5 18.1 %shard_map.208 = (bf16[512,1536]{1,0:T(8,128)(2,1)}, f32[4,8,128]{2,1,0:T(8,128)}) custom-call(s32[4,4]{1,0:T(4,128)} %bitcast.142, s32[1,1]{1,0:T(1,128)} %bitcast.2.place_ref, bf16[512,512]{1,0:T(8,128)(2,1)} %get-tuple-element.43.q_ref, bf16[512,512]{1,0:T(8,128)(2,1)} %get-tuple-element.44.k_ref, bf16[512,512]{1,0:T(8,128)(2,1)} %get-tuple-element.45.v_ref, ...), custom_call_target="tpu_custom_call" | custom-call | flops 1342177280 | bytes 8388608 | tf_op jit(solution)/shard_map/pallas_call | solution.py:684
  263.6 4.2 fusion.170
  270.1 12.6 %collective-permute-done.4 = bf16[512,512]{1,0:T(8,128)(2,1)S(1)} collective-permute-done((bf16[512,512]{1,0:T(8,128)(2,1)S(1)}, bf16[512,512]{1,0:T(8,128)(2,1)S(1)}, u32[]{:S(2)}, u32[]{:S(2)}) %collective-permute-start.4) | collective-permute-done | bytes 524320 | tf_op jit(solution)/shard_map/ppermute | solution.py:570
  284.4 14.0 %collective-permute-done.5 = bf16[512,512]{1,0:T(8,128)(2,1)} collective-permute-done((bf16[512,512]{1,0:T(8,128)(2,1)S(1)}, bf16[512,512]{1,0:T(8,128)(2,1)}, u32[]{:S(2)}, u32[]{:S(2)}) %collective-permute-start.5) | collective-permute-done | bytes 524320 | tf_op jit(solution)/shard_map/ppermute | solution.py:731
  299.8 11.2 %collective-permute-done.6 = bf16[512,512]{1,0:T(8,128)(2,1)} collective-permute-done((bf16[512,512]{1,0:T(8,128)(2,1)}, bf16[512,512]{1,0:T(8,128)(2,1)}, u32[]{:S(2)}, u32[]{:S(2)}) %collective-permute-start.6) | collective-permute-done | bytes 524320 | tf_op jit(solution)/shard_map/ppermute | solution.py:555
  311.0 2.2 fusion.89.refs_1_.refs_5_
  315.7 4.5 shard_map.209
  320.3 5.3 fusion.12
  330.0 14.9 %all-gather.7 = f32[32,8,128]{2,1,0:T(8,128)S(1)} all-gather(f32[4,8,128]{2,1,0:T(8,128)S(1)} %copy-done.13), channel_id=9, replica_groups=mesh['ctx'=8,'pipe'=2,'tp'=2] {'ctx'}, dimensions={0}, use_global_device_ids=true | all-gather | bytes 147456 | tf_op jit(solution)/shard_map/all_gather | solution.py:622
  345.6 3.8 convert_reduce_fusion
  350.8 3.7 fusion.20
  354.5 11.9 %all-gather.19.cloned.1.call-done = f32[32,4,64,128]{3,2,1,0:T(8,128)} async-done(((f32[4,4,64,128]{3,2,1,0:T(8,128)}), f32[32,4,64,128]{3,2,1,0:T(8,128)}) %all-gather.19.cloned.1.call-update) | async-done | bytes 4194320 | tf_op jit(solution)/shard_map/all_gather | solution.py:622
  366.4 3.8 multiply_reduce_fusion.later_ref
  370.2 18.2 %shard_map.210 = (bf16[512,1536]{1,0:T(8,128)(2,1)}, f32[4,8,128]{2,1,0:T(8,128)}) custom-call(s32[4,4]{1,0:T(4,128)} %bitcast.144, s32[1,1]{1,0:T(1,128)} %bitcast.2.place_ref, bf16[512,512]{1,0:T(8,128)(2,1)} %get-tuple-element.43.q_ref, bf16[512,512]{1,0:T(8,128)(2,1)} %get-tuple-element.44.k_ref, bf16[512,512]{1,0:T(8,128)(2,1)} %get-tuple-element.45.v_ref, ...), custom_call_target="tpu_custom_call" | custom-call | flops 1342177280 | bytes 8388608 | tf_op jit(solution)/shard_map/pallas_call | solution.py:684
  389.8 4.6 fusion.169
  398.7 12.1 %collective-permute-done.9 = f32[4,512]{1,0:T(4,128)S(1)} collective-permute-done((f32[4,512]{1,0:T(4,128)S(1)}, f32[4,512]{1,0:T(4,128)S(1)}, u32[]{:S(2)}, u32[]{:S(2)}) %collective-permute-start.9) | collective-permute-done | bytes 8224 | tf_op jit(solution)/shard_map/ppermute | solution.py:739
  410.8 4.2 convert_reduce_fusion.3
  415.9 160.8 %shard_map.211 = (bf16[2048,1024]{1,0:T(8,128)(2,1)}, bf16[1024,2048]{1,0:T(8,128)(2,1)}, bf16[512,1024]{1,0:T(8,128)(2,1)}, bf16[1024,1536]{1,0:T(8,128)(2,1)}, bf16[256,512]{1,0:T(8,128)(2,1)}) custom-call(bf16[512,2048]{1,0:T(8,128)(2,1)} %get-tuple-element.162.refs_0_, bf16[512,1024]{1,0:T(8,128)(2,1)} %copy-done.10, ...), custom_call_target="tpu_custom_call" | custom-call | flops 6576668672 | bytes 41943040 | tf_op jit(solution)/shard_map/pallas_call | solution.py:526
  579.6 6.8 %bitcast_convert_fusion = f32[1,2048,1024]{2,1,0:T(8,128)} fusion(bf16[2048,1024]{1,0:T(8,128)(2,1)} %get-tuple-element.62), kind=kLoop, calls=%fused_computation.13 | loop fusion | flops 2097152 | bytes 12582912 | tf_op jit(solution)/shard_map/broadcast_in_dim | solution.py:761
  586.4 4.4 bitcast_convert_fusion.1
  590.9 3.6 bitcast_convert_fusion.2
  (147 shorter events, 45.2 us)
Async XLA Ops:
  7.2 78.2 %copy-start = (bf16[1,512,1024]{2,1,0:T(8,128)(2,1)S(1)}, bf16[1,512,1024]{2,1,0:T(8,128)(2,1)}, u32[]{:S(2)}) copy-start(bf16[1,512,1024]{2,1,0:T(8,128)(2,1)} %param.19) | copy-start | bytes 3145732
  7.2 18.6 %copy-start.1 = (bf16[1,4,1,128,512]{4,3,2,1,0:T(8,128)(2,1)S(1)}, bf16[1,4,1,128,512]{4,3,2,1,0:T(8,128)(2,1)}, u32[]{:S(2)}) copy-start(bf16[1,4,1,128,512]{4,3,2,1,0:T(8,128)(2,1)} %param.12) | copy-start | bytes 1572868
  7.2 66.8 %all-gather.13.cloned.1.call-start = ((), (), s32[]{:S(2)}) async-start(), calls=%async_computation | async-start | bytes 2359296 | tf_op jit(solution)/shard_map/all_gather | solution.py:622
  7.2 15.1 %collective-permute-start = (bf16[512,512]{1,0:T(8,128)(2,1)}, bf16[512,512]{1,0:T(8,128)(2,1)S(1)}, u32[]{:S(2)}, u32[]{:S(2)}) collective-permute-start(bf16[512,512]{1,0:T(8,128)(2,1)} %bitcast.118), channel_id=1, source_target_pairs={{0,1},{1,0},{2,3},{3,2},{4,5},{5,4},{6,7},{7,6},{8,9},{9,8},{10,11... | collective-permute-start | bytes 1572872 | tf_op jit(solution)/shard_map/ppermute | solution.py:555
  27.3 29.0 %copy-start.21 = (f32[1,2048]{1,0:T(1,128)S(1)}, f32[1,2048]{1,0:T(1,128)}, u32[]{:S(2)}) copy-start(f32[1,2048]{1,0:T(1,128)} %param.22) | copy-start | bytes 24580
  40.3 137.7 %all-gather.15.cloned.1.call-start = ((), (), s32[]{:S(2)}) async-start(), calls=%async_computation.1 | async-start | bytes 2359296 | tf_op jit(solution)/shard_map/all_gather | solution.py:622
  74.0 11.4 %copy-start.6 = (f32[512,1024]{1,0:T(8,128)S(1)}, f32[512,1024]{1,0:T(8,128)}, u32[]{:S(2)}) copy-start(f32[512,1024]{1,0:T(8,128)} %fusion.18) | copy-start | bytes 6291460
  77.1 24.4 %copy-start.16 = (f32[1,512]{1,0:T(1,128)S(1)}, f32[1,512]{1,0:T(1,128)}, u32[]{:S(2)}) copy-start(f32[1,512]{1,0:T(1,128)} %param.20) | copy-start | bytes 6148
  87.3 14.2 %collective-permute-start.1 = (bf16[512,512]{1,0:T(8,128)(2,1)S(1)}, bf16[512,512]{1,0:T(8,128)(2,1)S(1)}, u32[]{:S(2)}, u32[]{:S(2)}) collective-permute-start(bf16[512,512]{1,0:T(8,128)(2,1)S(1)} %select_convert_fusion.3), channel_id=1, source_target_pairs={{0,1},{1,0},{2,3},{3,2},{4,5},{5,4},{6,7},{7,6},{8,9},{9,8},{10,11... | collective-permute-start | bytes 1572872 | tf_op jit(solution)/shard_map/ppermute | solution.py:570
  101.9 14.3 %collective-permute-start.2 = (bf16[512,512]{1,0:T(8,128)(2,1)S(1)}, bf16[512,512]{1,0:T(8,128)(2,1)S(1)}, u32[]{:S(2)}, u32[]{:S(2)}) collective-permute-start(bf16[512,512]{1,0:T(8,128)(2,1)S(1)} %fusion.83), channel_id=1, source_target_pairs={{0,2},{1,3},{4,6},{5,7},{8,10},{9,11},{12,14},{13,15},{16,18},{17,... | collective-permute-start | bytes 1572872 | tf_op jit(solution)/shard_map/ppermute | solution.py:726
  116.2 1.5 copy-start.7
  116.2 12.5 %collective-permute-start.3 = (bf16[512,512]{1,0:T(8,128)(2,1)S(1)}, bf16[512,512]{1,0:T(8,128)(2,1)}, u32[]{:S(2)}, u32[]{:S(2)}) collective-permute-start(bf16[512,512]{1,0:T(8,128)(2,1)S(1)} %collective-permute-done.2), channel_id=1, source_target_pairs={{0,1},{1,0},{2,3},{3,2},{4,5},{5,4},{6,7},{7,6},{8,9},{9,8},{10,11... | collective-permute-start | bytes 1572872 | tf_op jit(solution)/shard_map/ppermute | solution.py:555
  146.3 1.6 copy-start.15
  146.3 95.4 %all-gather.17.cloned.1.call-start = ((), (), s32[]{:S(2)}) async-start(), calls=%async_computation.2 | async-start | bytes 4718592 | tf_op jit(solution)/shard_map/all_gather | solution.py:622
  193.8 172.6 %all-gather.19.cloned.1.call-start = ((), (), s32[]{:S(2)}) async-start(), calls=%async_computation.3 | async-start | bytes 4718592 | tf_op jit(solution)/shard_map/all_gather | solution.py:622
  209.0 10.8 %copy-start.14 = (f32[4,8,128]{2,1,0:T(8,128)S(1)}, f32[4,8,128]{2,1,0:T(8,128)}, u32[]{:S(2)}) copy-start(f32[4,8,128]{2,1,0:T(8,128)} %get-tuple-element.51) | copy-start | bytes 49156
  241.7 21.9 %copy-start.19 = (bf16[1,1024,1536]{2,1,0:T(8,128)(2,1)S(1)}, bf16[1,1024,1536]{2,1,0:T(8,128)(2,1)}, u32[]{:S(2)}) copy-start(bf16[1,1024,1536]{2,1,0:T(8,128)(2,1)} %param.16) | copy-start | bytes 9437188
  268.5 14.1 %collective-permute-start.4 = (bf16[512,512]{1,0:T(8,128)(2,1)S(1)}, bf16[512,512]{1,0:T(8,128)(2,1)S(1)}, u32[]{:S(2)}, u32[]{:S(2)}) collective-permute-start(bf16[512,512]{1,0:T(8,128)(2,1)S(1)} %select_convert_fusion.2), channel_id=1, source_target_pairs={{0,1},{1,0},{2,3},{3,2},{4,5},{5,4},{6,7},{7,6},{8,9},{9,8},{10,11... | collective-permute-start | bytes 1572872 | tf_op jit(solution)/shard_map/ppermute | solution.py:570
  283.1 15.3 %collective-permute-start.5 = (bf16[512,512]{1,0:T(8,128)(2,1)S(1)}, bf16[512,512]{1,0:T(8,128)(2,1)}, u32[]{:S(2)}, u32[]{:S(2)}) collective-permute-start(bf16[512,512]{1,0:T(8,128)(2,1)S(1)} %fusion.84), channel_id=1, source_target_pairs={{2,0},{3,1},{6,4},{7,5},{10,8},{11,9},{14,12},{15,13},{18,16},{19,... | collective-permute-start | bytes 1572872 | tf_op jit(solution)/shard_map/ppermute | solution.py:731
  298.3 12.7 %collective-permute-start.6 = (bf16[512,512]{1,0:T(8,128)(2,1)}, bf16[512,512]{1,0:T(8,128)(2,1)}, u32[]{:S(2)}, u32[]{:S(2)}) collective-permute-start(bf16[512,512]{1,0:T(8,128)(2,1)} %collective-permute-done.5), channel_id=1, source_target_pairs={{0,1},{1,0},{2,3},{3,2},{4,5},{5,4},{6,7},{7,6},{8,9},{9,8},{10,11... | collective-permute-start | bytes 1572872 | tf_op jit(solution)/shard_map/ppermute | solution.py:555
  313.2 1.0 copy-start.10
  320.2 5.4 copy-start.12
  320.3 25.3 %copy-start.23 = (f32[512,2048]{1,0:T(8,128)S(1)}, f32[512,2048]{1,0:T(8,128)}, u32[]{:S(2)}) copy-start(f32[512,2048]{1,0:T(8,128)} %get-tuple-element.163) | copy-start | bytes 12582916
  325.6 4.4 copy-start.13
  325.6 20.0 %copy-start.11 = (bf16[512,1024]{1,0:T(8,128)(2,1)S(1)}, bf16[512,1024]{1,0:T(8,128)(2,1)}, u32[]{:S(2)}) copy-start(bf16[512,1024]{1,0:T(8,128)(2,1)} %copy-done.10) | copy-start | bytes 3145732
  325.6 20.0 %copy-start.17 = (bf16[1,2048,1024]{2,1,0:T(8,128)(2,1)S(1)}, bf16[1,2048,1024]{2,1,0:T(8,128)(2,1)}, u32[]{:S(2)}) copy-start(bf16[1,2048,1024]{2,1,0:T(8,128)(2,1)} %param.23) | copy-start | bytes 12582916
  326.3 1.3 copy-start.3
  328.5 82.2 %collective-permute-start.8 = (bf16[512,512]{1,0:T(8,128)(2,1)}, bf16[512,512]{1,0:T(8,128)(2,1)}, u32[]{:S(2)}, u32[]{:S(2)}) collective-permute-start(bf16[512,512]{1,0:T(8,128)(2,1)} %select_convert_fusion), channel_id=1, source_target_pairs={{0,1},{1,0},{2,3},{3,2},{4,5},{5,4},{6,7},{7,6},{8,9},{9,8},{10,11... | collective-permute-start | bytes 1572872 | tf_op jit(solution)/shard_map/ppermute | solution.py:570
  345.6 5.2 copy-start.18
  349.5 1.3 copy-start.22
  366.4 23.4 %copy-start.20 = (bf16[1,1024,1536]{2,1,0:T(8,128)(2,1)S(1)}, bf16[1,1024,1536]{2,1,0:T(8,128)(2,1)}, u32[]{:S(2)}) copy-start(bf16[1,1024,1536]{2,1,0:T(8,128)(2,1)} %param.16) | copy-start | bytes 9437188
  394.4 16.4 %copy-start.8 = (bf16[512,512]{1,0:T(8,128)(2,1)S(1)}, bf16[512,512]{1,0:T(8,128)(2,1)}, u32[]{:S(2)}) copy-start(bf16[512,512]{1,0:T(8,128)(2,1)} %copy-done.7) | copy-start | bytes 1572868
  395.0 1.3 copy-start.2
  396.4 14.3 %collective-permute-start.7 = (bf16[512,512]{1,0:T(8,128)(2,1)S(1)}, bf16[512,512]{1,0:T(8,128)(2,1)S(1)}, u32[]{:S(2)}, u32[]{:S(2)}) collective-permute-start(bf16[512,512]{1,0:T(8,128)(2,1)S(1)} %select_convert_fusion.1), channel_id=1, source_target_pairs={{0,1},{1,0},{2,3},{3,2},{4,5},{5,4},{6,7},{7,6},{8,9},{9,8},{10,11... | collective-permute-start | bytes 1572872 | tf_op jit(solution)/shard_map/ppermute | solution.py:570
  398.0 12.7 %collective-permute-start.9 = (f32[4,512]{1,0:T(4,128)S(1)}, f32[4,512]{1,0:T(4,128)S(1)}, u32[]{:S(2)}, u32[]{:S(2)}) collective-permute-start(f32[4,512]{1,0:T(4,128)S(1)} %constant_dynamic-slice_fusion), channel_id=1, source_target_pairs={{0,1},{1,0},{2,3},{3,2},{4,5},{5,4},{6,7},{7,6},{8,9},{9,8},{10,11... | collective-permute-start | bytes 24584 | tf_op jit(solution)/shard_map/ppermute | solution.py:739
  579.6 6.8 %copy-start.4 = (bf16[1024,2048]{1,0:T(8,128)(2,1)S(1)}, bf16[1024,2048]{1,0:T(8,128)(2,1)}, u32[]{:S(2)}) copy-start(bf16[1024,2048]{1,0:T(8,128)(2,1)} %get-tuple-element.61) | copy-start | bytes 12582916
  586.4 4.5 copy-start.5
  590.9 3.6 copy-start.9
Sparse Core Ops, SparseCore 0:
  40.4 30.7 all-gather.12
  146.5 31.5 all-gather.14
  193.9 47.7 all-gather.16
  320.3 45.9 all-gather.18

commit v3 on v2

--- a/solution.py
+++ b/solution.py
@@ -16,6 +16,9 @@
 ROWS = 1
 NDOC = 4
 PAIR = 2 * HD
+HELD = HD + 8
+TILE = 256
+HOP = 2
 
 BF = jnp.bfloat16
 F32 = jnp.float32
@@ -114,7 +117,7 @@
     passing = (end == count_starts(starts_ref, row, base - 1)).astype(F32)
     seg = seg_grid(starts_ref, row, base, (half, PAIR), 0)
     key = k[:half] * (seg == end).astype(F32).astype(BF)
-    state = passing * state_in.astype(F32) + compact(dot(key, v[:half], 0, 0), low)
+    state = passing * state_in + compact(dot(key, v[:half], 0, 0), low)
     total = passing * total_in + jnp.sum(key.astype(F32), 0, keepdims=True)
     later = seg_grid(starts_ref, row, base + half, (half, PAIR), 0)
     return state.astype(BF), total, (later == end).astype(F32)
@@ -148,10 +151,16 @@
     return jnp.concatenate([state * first[:HD], state * second[:HD]], 0)
 
 
+def keep_state(state_ref, row, product, summands, low):
+    state_ref[row, 0, :HD] = compact(product, low)
+    total = jnp.sum(summands, 0, keepdims=True)
+    state_ref[row, 0, HD:] = jnp.broadcast_to(total, (HELD - HD, PAIR))
+
+
 def features_kernel(
     starts_ref, place_ref, norm_ref, weight_ref, bias_ref, feat_ref,
     same_ref, down_ref, up_ref, high_ref, low_ref,
-    q_ref, k_ref, v_ref, state_ref, total_ref,
+    q_ref, k_ref, v_ref, state_ref,
 ):
     tokens = same_ref.shape[0]
     base = place_ref[0, 0] * tokens
@@ -174,12 +183,11 @@
         v_ref[here, :] = value
         leaving = leaving_mask(starts_ref, row, base, tokens)
         key_out = out[1] * leaving.astype(BF)
-        state_ref[0, row] = compact(dot(key_out, value, 0, 0), low).astype(BF)
-        total_ref[0, row : row + 1, :] = jnp.sum(key_out.astype(F32), 0, keepdims=True)
+        keep_state(state_ref, row, dot(key_out, value, 0, 0), key_out.astype(F32), low)
 
 
 def attend_kernel(
-    starts_ref, place_ref, q_ref, k_ref, v_ref, state_ref, total_ref, low_ref, out_ref, den_ref
+    starts_ref, place_ref, q_ref, k_ref, v_ref, state_ref, low_ref, out_ref, den_ref
 ):
     tokens = q_ref.shape[0] // (MB * ROWS)
     base = place_ref[0, 0] * tokens
@@ -190,8 +198,9 @@
         q, k, v = q_ref[here, :], k_ref[here, :], v_ref[here, :]
         mask, mask_in = causal_mask(starts_ref, row, base, tokens)
         enter = entering_mask(starts_ref, row, base, tokens)
-        state, total = state_ref[0, row], total_ref[0, row : row + 1, :]
-        middle, _, reach = middle_state(starts_ref, row, base, tokens, k, v, state, total, low)
+        carry, total = state_ref[row, 0, :HD], state_ref[row, 0, HD : HD + 1]
+        state = carry.astype(BF)
+        middle, _, reach = middle_state(starts_ref, row, base, tokens, k, v, carry, total, low)
         half = tokens // 2
         num = jnp.concatenate(
             [
@@ -224,7 +233,7 @@
 
 
 def back_state_kernel(
-    starts_ref, place_ref, q_ref, ga_ref, att_ref, den_ref, state_ref, total_ref
+    starts_ref, place_ref, q_ref, ga_ref, att_ref, den_ref, state_ref
 ):
     tokens = q_ref.shape[0] // (MB * ROWS)
     base = place_ref[0, 0] * tokens
@@ -236,13 +245,12 @@
         grad_den = -split_dot(grad_num.astype(F32) * att_ref[here, :], ones)
         enter = entering_mask(starts_ref, row, base, tokens)
         query = q_ref[here, :] * enter.astype(BF)
-        state_ref[0, row] = compact(dot(query, grad_num, 0, 0), low)
-        total_ref[0, row : row + 1, :] = jnp.sum(grad_den * query.astype(F32), 0, keepdims=True)
+        keep_state(state_ref, row, dot(query, grad_num, 0, 0), grad_den * query.astype(F32), low)
 
 
 def back_kernel(
     starts_ref, place_ref, q_ref, k_ref, v_ref, ga_ref, att_ref, den_ref,
-    state_ref, total_ref, later_ref, later_total_ref, feat_ref,
+    state_ref, later_ref, feat_ref,
     same_ref, down_ref, up_ref, high_ref, low_ref,
     grad_ref, sums_ref,
 ):
@@ -262,9 +270,10 @@
         mask, mask_in = causal_mask(starts_ref, row, base, tokens)
         enter = entering_mask(starts_ref, row, base, tokens)
         leave = leaving_mask(starts_ref, row, base, tokens)
-        state, total = state_ref[0, row], total_ref[0, row : row + 1, :]
+        carry, total = state_ref[row, 0, :HD], state_ref[row, 0, HD : HD + 1]
+        state = carry.astype(BF)
         middle, middle_total, reach = middle_state(
-            starts_ref, row, base, tokens, k, v, state, total, low
+            starts_ref, row, base, tokens, k, v, carry, total, low
         )
         half = tokens // 2
         gq = jnp.concatenate(
@@ -279,12 +288,12 @@
             ],
             0,
         )
-        later = later_ref[0, row]
+        later = later_ref[row, 0, :HD]
         later_high = later.astype(BF)
         later_low = spread((later - later_high.astype(F32)).astype(BF), first, second)
         later_high = spread(later_high, first, second)
         gk = leave * (
-            dot(v, later_high, 1, 1) + dot(v, later_low, 1, 1) + later_total_ref[0, row : row + 1, :]
+            dot(v, later_high, 1, 1) + dot(v, later_low, 1, 1) + later_ref[row, 0, HD : HD + 1]
         )
         gv = leave * (dot(k, later_high) + dot(k, later_low))
         for head, den in zip((first, second), dens):
@@ -549,6 +558,282 @@
     )
 
 
+def exchange(forward, starts_ref, own_ref, got_ref, bufs, tokens):
+    (twin_buf, in_buf, out_buf, back_buf, twin_sem, send_sem, recv_sem, back_send, back_recv) = bufs
+    rows, pairs = own_ref.shape[:2]
+    part = rows // 2
+    chunks, width = in_buf.shape[:2]
+    split = pairs // width
+    place, chips = lax.axis_index("ctx"), lax.axis_size("ctx") // 2
+    core, z = place % 2, place // 2
+    away = z if forward else chips - 1 - z
+    first, last = away == 0, away == chips - 1
+    step = 2 if forward else -2
+    twin = place + 1 - 2 * core
+    leads = core == (0 if forward else 1)
+    lead = 2 * z + (0 if forward else 1)
+    other = 2 * z + (1 if forward else 0)
+
+    def remote(src, dst, send, recv, to):
+        return pltpu.make_async_remote_copy(
+            src_ref=src, dst_ref=dst, send_sem=send, recv_sem=recv,
+            device_id={"ctx": to}, device_id_type=pl.DeviceIdType.MESH,
+        )
+
+    def twin_copy():
+        theirs = own_ref.at[pl.ds((1 - core) * part, part)]
+        return remote(theirs, twin_buf, twin_sem.at[0], twin_sem.at[1], twin)
+
+    def onward(j):
+        return remote(out_buf.at[j], in_buf.at[j], send_sem.at[j], recv_sem.at[j], place + step)
+
+    def where_of(j):
+        return core * part + j // split, pl.ds((j % split) * width, width)
+
+    def back(j):
+        row, cols = where_of(j)
+        return remote(back_buf.at[j], got_ref.at[row, cols], back_send.at[j], back_recv.at[j], twin)
+
+    def passing(row, at):
+        end = count_starts(starts_ref, row, at * tokens + tokens - 1)
+        return (end == count_starts(starts_ref, row, at * tokens - 1)).astype(F32)
+
+    def begin():
+        barrier = pltpu.get_barrier_semaphore()
+
+        def greet(peer):
+            pl.semaphore_signal(
+                barrier, inc=1, device_id={"ctx": peer}, device_id_type=pl.DeviceIdType.MESH
+            )
+
+        greet(twin)
+
+        @pl.when(jnp.logical_not(first))
+        def _():
+            greet(place - step)
+
+        pl.semaphore_wait(barrier, 2 - last.astype(jnp.int32))
+        twin_copy().start()
+
+    def advance(i):
+        @pl.when(i == 0)
+        def _():
+            twin_copy().wait_recv()
+
+        j = i - HOP * away
+
+        @pl.when((j >= 0) & (j < chunks))
+        def _():
+            row, cols = where_of(j)
+
+            @pl.when(first)
+            def _():
+                in_buf[j] = jnp.zeros(in_buf.shape[1:], F32)
+
+            @pl.when(jnp.logical_not(first))
+            def _():
+                onward(j).wait_recv()
+
+            mine, theirs = own_ref[row, cols], twin_buf[j // split, cols]
+            entering_lead = in_buf[j]
+            entering_other = jnp.where(leads, mine, theirs) + passing(row, lead) * entering_lead
+
+            @pl.when(jnp.logical_not(last))
+            def _():
+                out_buf[j] = (
+                    jnp.where(leads, theirs, mine) + passing(row, other) * entering_other
+                )
+                onward(j).start()
+
+            got_ref[row, cols] = jnp.where(leads, entering_lead, entering_other)
+            back_buf[j] = jnp.where(leads, entering_other, entering_lead)
+            back(j).start()
+
+    def finish():
+        twin_copy().wait_send()
+
+        def one(j, carry):
+            back(j).wait_send()
+            back(j).wait_recv()
+
+            @pl.when(jnp.logical_not(last))
+            def _():
+                onward(j).wait_send()
+
+            return carry
+
+        lax.fori_loop(0, chunks, one, 0)
+
+    return begin, advance, finish, (chips - 1) * HOP + chunks
+
+
+def exchange_scratch(rows, pairs):
+    width = pairs // 2 if pairs % 2 == 0 else pairs
+    chunks = rows // 2 * (pairs // width)
+    one = pltpu.VMEM((chunks, width, HELD, PAIR), F32)
+    return [
+        pltpu.VMEM((rows // 2, pairs, HELD, PAIR), F32), one, one, one,
+        pltpu.SemaphoreType.DMA((2,)),
+    ] + [pltpu.SemaphoreType.DMA((chunks,))] * 4
+
+
+def tile(n):
+    return pl.ds(pl.multiple_of(n * TILE, TILE), TILE)
+
+
+def run_tiles(first_count, first_body, second_count, second_body, link):
+    begin, advance, finish, steps = link
+    begin()
+    both = first_count + second_count
+
+    def one(i, carry):
+        @pl.when(i < first_count)
+        def _():
+            first_body(i)
+
+        @pl.when((i >= first_count) & (i < both))
+        def _():
+            second_body(i - first_count)
+
+        advance(i)
+        return carry
+
+    lax.fori_loop(0, max(both, steps), one, 0)
+    finish()
+
+
+def start_all(count, copy):
+    def one(n, carry):
+        copy(n).start()
+        return carry
+
+    lax.fori_loop(0, count, one, 0)
+
+
+def feed_forward_kernel(
+    tokens, starts_ref, own_ref, norm_ref, up_ref, bias_ref, down_ref,
+    pre_ref, hidden_ref, mlp_ref, got_ref,
+    up_buf, down_buf, up_sem, down_sem, *bufs,
+):
+    ups, downs = up_ref.shape[1] // TILE, down_ref.shape[1] // TILE
+
+    def up_copy(n):
+        return pltpu.make_async_copy(up_ref.at[:, tile(n)], up_buf.at[:, tile(n)], up_sem.at[n])
+
+    def down_copy(n):
+        return pltpu.make_async_copy(
+            down_ref.at[:, tile(n)], down_buf.at[:, tile(n)], down_sem.at[n]
+        )
+
+    start_all(ups, up_copy)
+    start_all(downs, down_copy)
+
+    def up(n):
+        up_copy(n).wait()
+        pre = dot(norm_ref[...], up_buf[:, tile(n)]) + bias_ref[:, tile(n)]
+        pre_ref[:, tile(n)] = pre
+        hidden = 0.5 * pre * (1.0 + lax.erf(pre * math.sqrt(0.5)))
+        hidden_ref[:, tile(n)] = hidden.astype(BF)
+
+    def down(n):
+        down_copy(n).wait()
+        mlp_ref[:, tile(n)] = dot(hidden_ref[...], down_buf[:, tile(n)])
+
+    run_tiles(ups, up, downs, down, exchange(True, starts_ref, own_ref, got_ref, bufs, tokens))
+
+
+def feed_backward_kernel(
+    tokens, starts_ref, own_ref, grad_ref, pre_ref, down_ref, up_ref,
+    grad_pre_ref, grad_norm_ref, got_ref,
+    pre_buf, down_buf, up_buf, pre_sem, down_sem, up_sem, *bufs,
+):
+    downs, ups = down_ref.shape[0] // TILE, up_ref.shape[0] // TILE
+
+    def pre_copy(n):
+        return pltpu.make_async_copy(pre_ref.at[:, tile(n)], pre_buf.at[:, tile(n)], pre_sem.at[n])
+
+    def down_copy(n):
+        return pltpu.make_async_copy(down_ref.at[tile(n)], down_buf.at[tile(n)], down_sem.at[n])
+
+    def up_copy(n):
+        return pltpu.make_async_copy(up_ref.at[tile(n)], up_buf.at[tile(n)], up_sem.at[n])
+
+    start_all(downs, down_copy)
+    start_all(downs, pre_copy)
+    start_all(ups, up_copy)
+
+    def down(n):
+        down_copy(n).wait()
+        pre_copy(n).wait()
+        grad = dot(grad_ref[...], down_buf[tile(n), :], 1, 1)
+        pre = pre_buf[:, tile(n)]
+        cdf = 0.5 * (1.0 + lax.erf(pre * math.sqrt(0.5)))
+        slope = cdf + pre * jnp.exp(-0.5 * pre * pre) * (1.0 / math.sqrt(2.0 * math.pi))
+        grad_pre_ref[:, tile(n)] = (grad * slope).astype(BF)
+
+    def up(n):
+        up_copy(n).wait()
+        grad_norm_ref[:, tile(n)] = dot(grad_pre_ref[...], up_buf[tile(n), :], 1, 1)
+
+    run_tiles(downs, down, ups, up, exchange(False, starts_ref, own_ref, got_ref, bufs, tokens))
+
+
+IN_VMEM = pl.BlockSpec(memory_space=pltpu.VMEM)
+ANYWHERE = pl.BlockSpec(memory_space=pl.ANY)
+
+
+def link_call(kernel, number, in_specs, out_shape, scratch, flops):
+    return pl.pallas_call(
+        kernel,
+        in_specs=in_specs,
+        out_specs=[IN_VMEM] * len(out_shape),
+        out_shape=out_shape,
+        scratch_shapes=scratch,
+        compiler_params=pltpu.CompilerParams(
+            collective_id=number, has_side_effects=True, vmem_limit_bytes=VMEM_LIMIT
+        ),
+        cost_estimate=pl.CostEstimate(flops=flops, bytes_accessed=16 << 20, transcendentals=0),
+    )
+
+
+def feed_forward(starts, state, norm, w_up, b_up, w_down):
+    total, units = norm.shape[0], w_up.shape[1]
+    rows, pairs = state.shape[:2]
+    return link_call(
+        partial(feed_forward_kernel, total // rows),
+        1,
+        [SMEM, IN_VMEM, IN_VMEM, ANYWHERE, IN_VMEM, ANYWHERE],
+        [
+            shaped((total, units), F32), shaped((total, units), BF), shaped((total, D), F32),
+            shaped(state.shape, F32),
+        ],
+        [
+            pltpu.VMEM(w_up.shape, BF), pltpu.VMEM(w_down.shape, BF),
+            pltpu.SemaphoreType.DMA((units // TILE,)), pltpu.SemaphoreType.DMA((D // TILE,)),
+        ]
+        + exchange_scratch(rows, pairs),
+        4 * total * units * D,
+    )(starts, state, norm, w_up, b_up.reshape(1, units), w_down)
+
+
+def feed_backward(starts, state, grad, pre, w_down, w_up):
+    total, units = pre.shape
+    rows, pairs = state.shape[:2]
+    return link_call(
+        partial(feed_backward_kernel, total // rows),
+        2,
+        [SMEM, IN_VMEM, IN_VMEM, ANYWHERE, ANYWHERE, ANYWHERE],
+        [shaped((total, units), BF), shaped((total, D), F32), shaped(state.shape, F32)],
+        [
+            pltpu.VMEM(pre.shape, F32), pltpu.VMEM(w_down.shape, BF), pltpu.VMEM(w_up.shape, BF),
+            pltpu.SemaphoreType.DMA((units // TILE,)), pltpu.SemaphoreType.DMA((units // TILE,)),
+            pltpu.SemaphoreType.DMA((D // TILE,)),
+        ]
+        + exchange_scratch(rows, pairs),
+        4 * total * units * D,
+    )(starts, state, grad, pre, w_down, w_up)
+
+
 def gather_tp(value):
     if lax.axis_size("tp") != 2:
         return lax.all_gather(value, "tp", axis=1, tiled=True)
@@ -587,7 +872,6 @@
 ):
     section = lax.axis_index("pipe")
     place = lax.axis_index("ctx")
-    peers = lax.axis_size("ctx")
     width = section_inputs.shape[-1]
     tokens = section_inputs.shape[3]
     rows = MB * ROWS
@@ -605,25 +889,10 @@
     same, down, up = rotary_tables(place, tokens)
     tables = (same, down, up, high, low)
     table_specs = [whole((tokens, PAIR))] * 3 + [whole((PAIR, PAIR))] * 2
-    state_shape = shaped((pairs, rows, HD, PAIR), BF)
-    total_shape = shaped((pairs, 8, PAIR), F32)
-    state_spec, total_spec = stacked(rows, HD, PAIR), stacked(8, PAIR)
+    state_shape = shaped((rows, pairs, HELD, PAIR), F32)
+    state_spec = pl.BlockSpec((rows, 1, HELD, PAIR), lambda p: (0, p, 0, 0))
     low_shape, full_shape = shaped((total, pairs * PAIR), BF), shaped((total, pairs * PAIR), F32)
     unit = 2 * rows * tokens * PAIR * PAIR * pairs
-
-    ends = jnp.arange(peers, dtype=jnp.int32)[:, None, None] * tokens
-    seg_last = jnp.sum((starts[None] <= ends + tokens - 1).astype(jnp.int32), 2)
-    seg_prev = jnp.sum((starts[None] <= ends - 1).astype(jnp.int32), 2)
-    order = jnp.arange(peers)[:, None]
-    from_earlier = ((order < place) & (seg_last == seg_prev[place][None])).astype(F32)
-    from_later = ((order > place) & (seg_prev == seg_last[place][None])).astype(F32)
-
-    def carried(state, totals, weights):
-        states, sums = lax.all_gather((state, totals), "ctx")
-        state_in = jnp.sum(states.astype(F32) * weights[:, None, :, None, None], 0)
-        padded = jnp.concatenate([weights, jnp.zeros((peers, 8 - rows), F32)], 1)
-        total_in = jnp.sum(jnp.where(padded[:, None, :, None] > 0, sums, 0.0), 0)
-        return state_in.astype(state.dtype), total_in
 
     def forward(u_low, own):
         u = u_low.astype(F32)
@@ -632,64 +901,52 @@
         xhat = centered * inv
         first = (xhat * gain[0] + shift[0]).astype(BF)
         second = (xhat * gain[1] + shift[1]).astype(BF)
-        q, k, v, state, totals = call(
+        q, k, v, state = call(
             features_kernel,
             pairs,
             [SMEM, SMEM, whole((total, D)), column(D, 3 * PAIR), stacked(1, 3 * PAIR),
              stacked(1, PAIR)] + table_specs,
-            [column(total, PAIR)] * 3 + [state_spec, total_spec],
-            [low_shape] * 3 + [state_shape, total_shape],
+            [column(total, PAIR)] * 3 + [state_spec],
+            [low_shape] * 3 + [state_shape],
             30 * unit,
         )(starts, place_in, first, w_qkv, b_qkv, feat, *tables)
-        state_in, total_in = carried(state, totals, from_earlier)
-        pre = jnp.dot(second, w_up, preferred_element_type=F32) + b_up
-        hidden = jax.nn.gelu(pre, approximate=False).astype(BF)
-        mlp = jnp.dot(hidden, w_down, preferred_element_type=F32)
+        pre, hidden, mlp, state_in = feed_forward(starts, state, second, w_up, b_up, w_down)
         att_low, att, den = call(
             attend_kernel,
             pairs,
-            [SMEM, SMEM] + [column(total, PAIR)] * 3 + [state_spec, total_spec],
+            [SMEM, SMEM] + [column(total, PAIR)] * 3 + [state_spec],
             [column(total, PAIR)] * 3,
             [low_shape, full_shape, full_shape],
             8 * unit,
-        )(starts, place_in, q, k, v, state_in, total_in)
+        )(starts, place_in, q, k, v, state_in)
         part = jnp.dot(att_low, w_dense, preferred_element_type=F32) + mlp
         out = scatter_tp(part) + own.astype(F32) + b_out
-        kept = (xhat, inv, first, second, q, k, v, pre, hidden, att_low, att, den, state_in, total_in)
+        kept = (xhat, inv, first, second, q, k, v, pre, hidden, att_low, att, den, state_in)
         return out, kept
 
     def backward(dy, own, kept, want):
-        xhat, inv, first, second, q, k, v, pre, hidden, att_low, att, den, state_in, total_in = kept
+        xhat, inv, first, second, q, k, v, pre, hidden, att_low, att, den, state_in = kept
         ga = lax.dot_general(
             dy, w_dense, (((1,), (1,)), ((), ())), preferred_element_type=F32
         ).astype(BF)
-        state, totals = call(
+        (state,) = call(
             back_state_kernel,
             pairs,
             [SMEM, SMEM] + [column(total, PAIR)] * 4,
-            [state_spec, total_spec],
-            [shaped(state_shape.shape, F32), total_shape],
+            [state_spec],
+            [state_shape],
             3 * unit,
         )(starts, place_in, q, ga, att, den)
-        later, later_total = carried(state, totals, from_later)
-        grad_hidden = lax.dot_general(
-            dy, w_down, (((1,), (1,)), ((), ())), preferred_element_type=F32
-        )
-        cdf = 0.5 * (1.0 + lax.erf(pre * math.sqrt(0.5)))
-        slope = cdf + pre * jnp.exp(-0.5 * pre * pre) * (1.0 / math.sqrt(2.0 * math.pi))
-        grad_pre = (grad_hidden * slope).astype(BF)
-        grad_second = lax.dot_general(
-            grad_pre, w_up, (((1,), (1,)), ((), ())), preferred_element_type=F32
-        )
+        grad_pre, grad_second, later = feed_backward(starts, state, dy, pre, w_down, w_up)
         grad_proj, sums = call(
             back_kernel,
             pairs,
             [SMEM, SMEM] + [column(total, PAIR)] * 6
-            + [state_spec, total_spec, state_spec, total_spec, stacked(1, PAIR)] + table_specs,
+            + [state_spec, state_spec, stacked(1, PAIR)] + table_specs,
             [column(total, 3 * PAIR), stacked(8, PAIR)],
             [shaped((total, pairs * 3 * PAIR), BF), shaped((pairs, 8, PAIR), F32)],
             20 * unit,
-        )(starts, place_in, q, k, v, ga, att, den, state_in, total_in, later, later_total, feat, *tables)
+        )(starts, place_in, q, k, v, ga, att, den, state_in, later, feat, *tables)
         grad_first = lax.dot_general(
             grad_proj, w_qkv, (((1,), (1,)), ((), ())), preferred_element_type=F32
         )

time: 610 us -> 510 us (0.84)
  Pallas kernels: 249 us -> 332 us
  blocking collectives: 58.5 us -> 0 us
  matrix products: 70.7 us -> 14.6 us
  waiting for transfers between devices: 123 us -> 85.1 us
  other arithmetic: 54.6 us -> 39.6 us
  between operations: 14.5 us -> 1.4 us
    pallas_call x0 -> x4, Pallas kernels: none -> 85.4 us  [the longest x2 52.7 us: feed_backward(): link_call(partial(feed_backward_kernel, total // rows), 2, [SMEM, IN_VMEM...]
    all_gather x4 -> x0, blocking collectives: 58.5 us -> none  [carried(): states, sums = lax.all_gather((state, totals), 'ctx')]
    dot_general x6 -> x0, matrix products: 55.9 us -> none  [the longest x2 23 us: forward(): mlp = jnp.dot(hidden, w_down, preferred_element_type=F32)]
    all_gather x4 -> x0, waiting for transfers between devices: 33.9 us -> none  [carried(): states, sums = lax.all_gather((state, totals), 'ctx')]
    reduce_sum x9 -> x3, other arithmetic: 17.1 us -> 3.82 us  [the longest x2 3.44 us: backward(): jnp.mean(both, -1, keepdims=True)]
    ppermute x4, waiting for transfers between devices: 25.2 us -> 37.5 us  [scatter_tp(): lax.ppermute(jnp.where(me == 0, right, left).astype(BF), 'tp', [(0, 1), (...]
    ppermute x1, waiting for transfers between devices: 12.1 us -> 0.01 us  [local(): norm_sums = norm_sums + lax.ppermute(away, 'tp', [(0, 1), (1, 0)])]
  transfers between devices with their start and end apart: 14 -> 10, of which waited for: 11 -> 8; matrix products, arithmetic and copies ran while one was open for 13% -> 5% of each run, Pallas kernels for 3% -> 8%
where the time goes in v3:
time: 510 us; the launch traced here: 503 us
  Pallas kernels  332 us (65%)
  waiting for transfers between devices  85.1 us (17%)
  other arithmetic  39.6 us (8%)
  starting transfers between devices  17.1 us (3%)
  matrix products  14.6 us (3%)
  local copies, waits for them, and re-layouts  12.8 us (3%)
    pallas_call x1, Pallas kernels, reduce_over_ctx(): pl.pallas_call(partial(reduce_kernel, (count, terms)), in_specs=[pl.Block...  159 us
    pallas_call x2, Pallas kernels, feed_backward(): link_call(partial(feed_backward_kernel, total // rows), 2, [SMEM, IN_VMEM...  52.7 us
    ppermute x4, waiting for transfers between devices, scatter_tp(): lax.ppermute(jnp.where(me == 0, right, left).astype(BF), 'tp', [(0, 1), (...  37.5 us
    pallas_call x2, Pallas kernels, backward(): call(back_kernel, pairs, [SMEM, SMEM] + [column(total, PAIR)] * 6 + [stat...  36.2 us
    pallas_call x2, Pallas kernels, feed_forward(): link_call(partial(feed_forward_kernel, total // rows), 1, [SMEM, IN_VMEM,...  32.6 us
    pallas_call x2, Pallas kernels, forward(): call(features_kernel, pairs, [SMEM, SMEM, whole((total, D)), column(D, 3...  26 us
    ppermute x3, waiting for transfers between devices, gather_tp(): other = lax.ppermute(value, 'tp', [(0, 1), (1, 0)])  23.4 us
    pallas_call x2, Pallas kernels, forward(): call(attend_kernel, pairs, [SMEM, SMEM] + [column(total, PAIR)] * 3 + [st...  17 us
  transfers between devices with their start and end apart: 10, of which 8 were waited for; matrix products, arithmetic and copies ran while one was open for 5% of the time, Pallas kernels for 8%

profile of v3, /device:TPU:0, one launch (start us, length us, event | category | flops | bytes accessed | tf_op | source)
XLA Modules:
  0.0 503.0 jit_solution(15279128788735450027)
XLA Ops:
  0.7 3.0 collective-permute-start
  5.6 1.3 reshape_squeeze.11.feat_ref
  10.5 5.5 %collective-permute-done = bf16[512,512]{1,0:T(8,128)(2,1)} collective-permute-done((bf16[512,512]{1,0:T(8,128)(2,1)}, bf16[512,512]{1,0:T(8,128)(2,1)}, u32[]{:S(2)}, u32[]{:S(2)}) %collective-permute-start) | collective-permute-done | bytes 524320 | tf_op jit(solution)/shard_map/ppermute | solution.py:840
  15.9 1.5 convert_reduce_fusion.2
  17.9 2.0 fusion.17
  19.9 13.0 %shard_map.203 = (bf16[512,512]{1,0:T(8,128)(2,1)}, bf16[512,512]{1,0:T(8,128)(2,1)}, bf16[512,512]{1,0:T(8,128)(2,1)}, f32[4,4,72,128]{3,2,1,0:T(8,128)}) custom-call(s32[4,4]{1,0:T(4,128)} %bitcast.81, s32[1,1]{1,0:T(1,128)} %bitcast.2.place_ref, bf16[512,1024]{1,0:T(8,128)(2,1)} %get-tuple-element.127.norm_ref, bf16[1024,1536]{1,0:T(8,128)(2,1)} %bitcast.115, ...), custom_call_target="tpu_custom_call" | custom-call | flops 2013265920 | bytes 8388608 | tf_op jit(solution)/shard_map/pallas_call | solution.py:904
  32.8 14.8 %shard_map.204 = (f32[512,2048]{1,0:T(8,128)}, bf16[512,2048]{1,0:T(8,128)(2,1)}, f32[512,1024]{1,0:T(8,128)}, f32[4,4,72,128]{3,2,1,0:T(8,128)}) custom-call(s32[4,4]{1,0:T(4,128)} %bitcast.82, f32[4,4,72,128]{3,2,1,0:T(8,128)} %get-tuple-element.45.own_ref, bf16[512,1024]{1,0:T(8,128)(2,1)} %get-tuple-element.126.norm_ref, bf16[1024,2048]{1,0:T(8,128)(2,1)} %bitcast.107, ...), custom_call_target="tpu_custom_call" | custom-call | flops 4294967296 | bytes 16777216 | tf_op jit(solution)/shard_map/pallas_call | solution.py:802
  47.6 8.5 %shard_map.205 = (bf16[512,512]{1,0:T(8,128)(2,1)}, f32[512,512]{1,0:T(8,128)}, f32[512,512]{1,0:T(8,128)}) custom-call(s32[4,4]{1,0:T(4,128)} %bitcast.83, s32[1,1]{1,0:T(1,128)} %bitcast.2.place_ref, bf16[512,512]{1,0:T(8,128)(2,1)} %get-tuple-element.42.q_ref, bf16[512,512]{1,0:T(8,128)(2,1)} %get-tuple-element.43.k_ref, ...), custom_call_target="tpu_custom_call" | custom-call | flops 536870912 | bytes 8388608 | tf_op jit(solution)/shard_map/pallas_call | solution.py:914
  56.2 1.8 convolution_add_fusion.1
  58.1 1.6 collective-permute-start.1
  59.6 12.9 %collective-permute-done.1 = bf16[512,512]{1,0:T(8,128)(2,1)S(1)} collective-permute-done((bf16[512,512]{1,0:T(8,128)(2,1)S(1)}, bf16[512,512]{1,0:T(8,128)(2,1)S(1)}, u32[]{:S(2)}, u32[]{:S(2)}) %collective-permute-start.1) | collective-permute-done | bytes 524320 | tf_op jit(solution)/shard_map/ppermute | solution.py:855
  72.9 4.0 collective-permute-start.2
  76.9 10.6 %collective-permute-done.2 = bf16[512,512]{1,0:T(8,128)(2,1)S(1)} collective-permute-done((bf16[512,512]{1,0:T(8,128)(2,1)S(1)}, bf16[512,512]{1,0:T(8,128)(2,1)S(1)}, u32[]{:S(2)}, u32[]{:S(2)}) %collective-permute-start.2) | collective-permute-done | bytes 524320 | tf_op jit(solution)/shard_map/ppermute | solution.py:983
  87.5 1.5 collective-permute-start.3
  89.0 1.5 convolution_convert_fusion.1.ga_ref
  90.5 9.8 %collective-permute-done.3 = bf16[512,512]{1,0:T(8,128)(2,1)} collective-permute-done((bf16[512,512]{1,0:T(8,128)(2,1)S(1)}, bf16[512,512]{1,0:T(8,128)(2,1)}, u32[]{:S(2)}, u32[]{:S(2)}) %collective-permute-start.3) | collective-permute-done | bytes 524320 | tf_op jit(solution)/shard_map/ppermute | solution.py:840
  100.4 2.0 convert_reduce_fusion.1
  102.8 2.0 fusion.21
  104.8 13.0 %shard_map.206 = (bf16[512,512]{1,0:T(8,128)(2,1)}, bf16[512,512]{1,0:T(8,128)(2,1)}, bf16[512,512]{1,0:T(8,128)(2,1)}, f32[4,4,72,128]{3,2,1,0:T(8,128)}) custom-call(s32[4,4]{1,0:T(4,128)} %bitcast.84, s32[1,1]{1,0:T(1,128)} %bitcast.2.place_ref, bf16[512,1024]{1,0:T(8,128)(2,1)} %get-tuple-element.125.norm_ref.refs_6_, bf16[1024,1536]{1,0:T(8,128)(2,1)} %bitcast.116, ...), custom_call_target="tpu_custom_call" | custom-call | flops 2013265920 | bytes 8388608 | tf_op jit(solution)/shard_map/pallas_call | solution.py:904
  117.8 17.8 %shard_map.207 = (f32[512,2048]{1,0:T(8,128)}, bf16[512,2048]{1,0:T(8,128)(2,1)}, f32[512,1024]{1,0:T(8,128)}, f32[4,4,72,128]{3,2,1,0:T(8,128)}) custom-call(s32[4,4]{1,0:T(4,128)} %bitcast.85, f32[4,4,72,128]{3,2,1,0:T(8,128)} %get-tuple-element.52.own_ref, bf16[512,1024]{1,0:T(8,128)(2,1)} %get-tuple-element.124.norm_ref.refs_2_, ...), custom_call_target="tpu_custom_call" | custom-call | flops 4294967296 | bytes 16777216 | tf_op jit(solution)/shard_map/pallas_call | solution.py:802
  135.6 8.4 %shard_map.208 = (bf16[512,512]{1,0:T(8,128)(2,1)}, f32[512,512]{1,0:T(8,128)}, f32[512,512]{1,0:T(8,128)}) custom-call(s32[4,4]{1,0:T(4,128)} %bitcast.86, s32[1,1]{1,0:T(1,128)} %bitcast.2.place_ref, bf16[512,512]{1,0:T(8,128)(2,1)} %get-tuple-element.49.q_ref, bf16[512,512]{1,0:T(8,128)(2,1)} %get-tuple-element.50.k_ref, ...), custom_call_target="tpu_custom_call" | custom-call | flops 536870912 | bytes 8388608 | tf_op jit(solution)/shard_map/pallas_call | solution.py:914
  144.0 4.5 shard_map.209.own_ref
  148.5 34.2 %shard_map.210 = (bf16[512,2048]{1,0:T(8,128)(2,1)}, f32[512,1024]{1,0:T(8,128)}, f32[4,4,72,128]{3,2,1,0:T(8,128)}) custom-call(s32[4,4]{1,0:T(4,128)} %bitcast.88, f32[4,4,72,128]{3,2,1,0:T(8,128)} %shard_map.209.own_ref, bf16[512,1024]{1,0:T(8,128)(2,1)} %copy-done.2, f32[512,2048]{1,0:T(8,128)} %get-tuple-element.56.pre_ref, ...), custom_call_target="tpu_custom_call" | custom-call | flops 4294967296 | bytes 16777216 | tf_op jit(solution)/shard_map/pallas_call | solution.py:822
  182.8 18.1 %shard_map.211 = (bf16[512,1536]{1,0:T(8,128)(2,1)}, f32[4,8,128]{2,1,0:T(8,128)}) custom-call(s32[4,4]{1,0:T(4,128)} %bitcast.89, s32[1,1]{1,0:T(1,128)} %bitcast.2.place_ref, bf16[512,512]{1,0:T(8,128)(2,1)} %get-tuple-element.49.q_ref, bf16[512,512]{1,0:T(8,128)(2,1)} %get-tuple-element.50.k_ref, bf16[512,512]{1,0:T(8,128)(2,1)} %get-tuple-element.51.v_ref, ...), custom_call_target="tpu_custom_call" | custom-call | flops 1342177280 | bytes 8388608 | tf_op jit(solution)/shard_map/pallas_call | solution.py:941
  200.9 3.4 fusion.69
  205.9 1.6 collective-permute-start.4
  207.5 12.0 %collective-permute-done.4 = bf16[512,512]{1,0:T(8,128)(2,1)S(1)} collective-permute-done((bf16[512,512]{1,0:T(8,128)(2,1)S(1)}, bf16[512,512]{1,0:T(8,128)(2,1)S(1)}, u32[]{:S(2)}, u32[]{:S(2)}) %collective-permute-start.4) | collective-permute-done | bytes 524320 | tf_op jit(solution)/shard_map/ppermute | solution.py:855
  220.7 1.3 collective-permute-start.5
  222.0 13.6 %collective-permute-done.5 = bf16[512,512]{1,0:T(8,128)(2,1)S(1)} collective-permute-done((bf16[512,512]{1,0:T(8,128)(2,1)}, bf16[512,512]{1,0:T(8,128)(2,1)S(1)}, u32[]{:S(2)}, u32[]{:S(2)}) %collective-permute-start.5) | collective-permute-done | bytes 524320 | tf_op jit(solution)/shard_map/ppermute | solution.py:988
  235.6 1.5 collective-permute-start.6
  237.1 2.5 convolution_add_fusion
  239.6 1.3 copy-done.4
  242.3 8.1 %collective-permute-done.6 = bf16[512,512]{1,0:T(8,128)(2,1)S(1)} collective-permute-done((bf16[512,512]{1,0:T(8,128)(2,1)S(1)}, bf16[512,512]{1,0:T(8,128)(2,1)S(1)}, u32[]{:S(2)}, u32[]{:S(2)}) %collective-permute-start.6) | collective-permute-done | bytes 524320 | tf_op jit(solution)/shard_map/ppermute | solution.py:840
  250.9 1.6 convolution_convert_fusion.ga_ref
  252.5 4.5 shard_map.212.own_ref
  257.0 18.5 %shard_map.213 = (bf16[512,2048]{1,0:T(8,128)(2,1)}, f32[512,1024]{1,0:T(8,128)}, f32[4,4,72,128]{3,2,1,0:T(8,128)}) custom-call(s32[4,4]{1,0:T(4,128)} %bitcast.91, f32[4,4,72,128]{3,2,1,0:T(8,128)} %shard_map.212.own_ref, bf16[512,1024]{1,0:T(8,128)(2,1)} %copy-done.17, f32[512,2048]{1,0:T(8,128)} %get-tuple-element.56.pre_ref, ...), custom_call_target="tpu_custom_call" | custom-call | flops 4294967296 | bytes 16777216 | tf_op jit(solution)/shard_map/pallas_call | solution.py:822
  275.5 18.1 %shard_map.214 = (bf16[512,1536]{1,0:T(8,128)(2,1)}, f32[4,8,128]{2,1,0:T(8,128)}) custom-call(s32[4,4]{1,0:T(4,128)} %bitcast.92, s32[1,1]{1,0:T(1,128)} %bitcast.2.place_ref, bf16[512,512]{1,0:T(8,128)(2,1)} %get-tuple-element.49.q_ref, bf16[512,512]{1,0:T(8,128)(2,1)} %get-tuple-element.50.k_ref, bf16[512,512]{1,0:T(8,128)(2,1)} %get-tuple-element.51.v_ref, ...), custom_call_target="tpu_custom_call" | custom-call | flops 1342177280 | bytes 8388608 | tf_op jit(solution)/shard_map/pallas_call | solution.py:941
  295.1 3.4 fusion.67
  298.5 2.6 fusion.75
  301.1 1.6 collective-permute-start.9
  302.7 2.3 fusion.27
  306.1 12.6 %collective-permute-done.7 = bf16[512,512]{1,0:T(8,128)(2,1)S(1)} collective-permute-done((bf16[512,512]{1,0:T(8,128)(2,1)S(1)}, bf16[512,512]{1,0:T(8,128)(2,1)S(1)}, u32[]{:S(2)}, u32[]{:S(2)}) %collective-permute-start.7) | collective-permute-done | bytes 524320 | tf_op jit(solution)/shard_map/ppermute | solution.py:855
  318.8 2.8 convert_reduce_fusion.3
  322.6 158.9 %shard_map.215 = (bf16[2048,1024]{1,0:T(8,128)(2,1)}, bf16[1024,2048]{1,0:T(8,128)(2,1)}, bf16[512,1024]{1,0:T(8,128)(2,1)}, bf16[1024,1536]{1,0:T(8,128)(2,1)}, bf16[256,512]{1,0:T(8,128)(2,1)}) custom-call(bf16[512,2048]{1,0:T(8,128)(2,1)} %get-tuple-element.65.refs_0_, bf16[512,1024]{1,0:T(8,128)(2,1)} %copy-done.17, ...), custom_call_target="tpu_custom_call" | custom-call | flops 6576668672 | bytes 41943040 | tf_op jit(solution)/shard_map/pallas_call | solution.py:535
  484.5 6.8 %bitcast_convert_fusion = f32[1,2048,1024]{2,1,0:T(8,128)} fusion(bf16[2048,1024]{1,0:T(8,128)(2,1)} %get-tuple-element.72), kind=kLoop, calls=%fused_computation | loop fusion | flops 2097152 | bytes 12582912 | tf_op jit(solution)/shard_map/broadcast_in_dim | solution.py:1018
  491.3 4.4 bitcast_convert_fusion.1
  495.7 3.6 bitcast_convert_fusion.2
  499.3 1.6 bitcast_convert_fusion.3
  (105 shorter events, 19.7 us)
Async XLA Ops:
  0.6 55.5 %copy-start = (bf16[1,512,1024]{2,1,0:T(8,128)(2,1)S(1)}, bf16[1,512,1024]{2,1,0:T(8,128)(2,1)}, u32[]{:S(2)}) copy-start(bf16[1,512,1024]{2,1,0:T(8,128)(2,1)} %param.19) | copy-start | bytes 3145732
  0.7 15.3 %copy-start.6 = (bf16[1,4,1,128,512]{4,3,2,1,0:T(8,128)(2,1)S(1)}, bf16[1,4,1,128,512]{4,3,2,1,0:T(8,128)(2,1)}, u32[]{:S(2)}) copy-start(bf16[1,4,1,128,512]{4,3,2,1,0:T(8,128)(2,1)} %param.12) | copy-start | bytes 1572868
  0.7 15.2 %collective-permute-start = (bf16[512,512]{1,0:T(8,128)(2,1)}, bf16[512,512]{1,0:T(8,128)(2,1)}, u32[]{:S(2)}, u32[]{:S(2)}) collective-permute-start(bf16[512,512]{1,0:T(8,128)(2,1)} %bitcast.70), channel_id=1, source_target_pairs={{0,1},{1,0},{2,3},{3,2},{4,5},{5,4},{6,7},{7,6},{8,9},{9,8},{10,11... | collective-permute-start | bytes 1572872 | tf_op jit(solution)/shard_map/ppermute | solution.py:840
  17.5 82.9 %copy-start.2 = (bf16[512,1024]{1,0:T(8,128)(2,1)}, bf16[512,1024]{1,0:T(8,128)(2,1)S(1)}, u32[]{:S(2)}) copy-start(bf16[512,1024]{1,0:T(8,128)(2,1)S(1)} %get-tuple-element.123.grad_ref) | copy-start | bytes 3145732
  47.6 8.6 %copy-start.13 = (f32[512,1024]{1,0:T(8,128)S(1)}, f32[512,1024]{1,0:T(8,128)}, u32[]{:S(2)}) copy-start(f32[512,1024]{1,0:T(8,128)} %get-tuple-element.48) | copy-start | bytes 6291460
  56.2 16.4 %copy-start.18 = (f32[1,512]{1,0:T(1,128)S(1)}, f32[1,512]{1,0:T(1,128)}, u32[]{:S(2)}) copy-start(f32[1,512]{1,0:T(1,128)} %param.20) | copy-start | bytes 6148
  58.1 14.5 %collective-permute-start.1 = (bf16[512,512]{1,0:T(8,128)(2,1)S(1)}, bf16[512,512]{1,0:T(8,128)(2,1)S(1)}, u32[]{:S(2)}, u32[]{:S(2)}) collective-permute-start(bf16[512,512]{1,0:T(8,128)(2,1)S(1)} %select_convert_fusion.3), channel_id=1, source_target_pairs={{0,1},{1,0},{2,3},{3,2},{4,5},{5,4},{6,7},{7,6},{8,9},{9,8},{10,11... | collective-permute-start | bytes 1572872 | tf_op jit(solution)/shard_map/ppermute | solution.py:855
  72.9 14.6 %collective-permute-start.2 = (bf16[512,512]{1,0:T(8,128)(2,1)S(1)}, bf16[512,512]{1,0:T(8,128)(2,1)S(1)}, u32[]{:S(2)}, u32[]{:S(2)}) collective-permute-start(bf16[512,512]{1,0:T(8,128)(2,1)S(1)} %fusion.33), channel_id=1, source_target_pairs={{0,2},{1,3},{4,6},{5,7},{8,10},{9,11},{12,14},{13,15},{16,18},{17,... | collective-permute-start | bytes 1572872 | tf_op jit(solution)/shard_map/ppermute | solution.py:983
  87.5 3.0 copy-start.14
  87.5 12.9 %collective-permute-start.3 = (bf16[512,512]{1,0:T(8,128)(2,1)S(1)}, bf16[512,512]{1,0:T(8,128)(2,1)}, u32[]{:S(2)}, u32[]{:S(2)}) collective-permute-start(bf16[512,512]{1,0:T(8,128)(2,1)S(1)} %collective-permute-done.2), channel_id=1, source_target_pairs={{0,1},{1,0},{2,3},{3,2},{4,5},{5,4},{6,7},{7,6},{8,9},{9,8},{10,11... | collective-permute-start | bytes 1572872 | tf_op jit(solution)/shard_map/ppermute | solution.py:840
  182.8 18.1 %copy-start.19 = (bf16[1,1024,1536]{2,1,0:T(8,128)(2,1)S(1)}, bf16[1,1024,1536]{2,1,0:T(8,128)(2,1)}, u32[]{:S(2)}) copy-start(bf16[1,1024,1536]{2,1,0:T(8,128)(2,1)} %param.16) | copy-start | bytes 9437188
  200.9 3.4 copy-start.11
  205.2 14.3 %copy-start.7 = (bf16[1,4,1,128,512]{4,3,2,1,0:T(8,128)(2,1)S(1)}, bf16[1,4,1,128,512]{4,3,2,1,0:T(8,128)(2,1)}, u32[]{:S(2)}) copy-start(bf16[1,4,1,128,512]{4,3,2,1,0:T(8,128)(2,1)} %param.12) | copy-start | bytes 1572868
  205.9 13.6 %collective-permute-start.4 = (bf16[512,512]{1,0:T(8,128)(2,1)S(1)}, bf16[512,512]{1,0:T(8,128)(2,1)S(1)}, u32[]{:S(2)}, u32[]{:S(2)}) collective-permute-start(bf16[512,512]{1,0:T(8,128)(2,1)S(1)} %select_convert_fusion.2), channel_id=1, source_target_pairs={{0,1},{1,0},{2,3},{3,2},{4,5},{5,4},{6,7},{7,6},{8,9},{9,8},{10,11... | collective-permute-start | bytes 1572872 | tf_op jit(solution)/shard_map/ppermute | solution.py:855
  220.7 14.9 %collective-permute-start.5 = (bf16[512,512]{1,0:T(8,128)(2,1)}, bf16[512,512]{1,0:T(8,128)(2,1)S(1)}, u32[]{:S(2)}, u32[]{:S(2)}) collective-permute-start(bf16[512,512]{1,0:T(8,128)(2,1)} %fusion.34), channel_id=1, source_target_pairs={{2,0},{3,1},{6,4},{7,5},{10,8},{11,9},{14,12},{15,13},{18,16},{19,... | collective-permute-start | bytes 1572872 | tf_op jit(solution)/shard_map/ppermute | solution.py:988
  235.6 14.9 %collective-permute-start.6 = (bf16[512,512]{1,0:T(8,128)(2,1)S(1)}, bf16[512,512]{1,0:T(8,128)(2,1)S(1)}, u32[]{:S(2)}, u32[]{:S(2)}) collective-permute-start(bf16[512,512]{1,0:T(8,128)(2,1)S(1)} %collective-permute-done.5), channel_id=1, source_target_pairs={{0,1},{1,0},{2,3},{3,2},{4,5},{5,4},{6,7},{7,6},{8,9},{9,8},{10,11... | collective-permute-start | bytes 1572872 | tf_op jit(solution)/shard_map/ppermute | solution.py:840
  239.6 1.3 copy-start.4
  240.9 9.5 %copy-start.3 = (bf16[512,1024]{1,0:T(8,128)(2,1)S(1)}, bf16[512,1024]{1,0:T(8,128)(2,1)}, u32[]{:S(2)}) copy-start(bf16[512,1024]{1,0:T(8,128)(2,1)} %copy-done.2) | copy-start | bytes 3145732
  241.8 64.3 %collective-permute-start.8 = (bf16[512,512]{1,0:T(8,128)(2,1)}, bf16[512,512]{1,0:T(8,128)(2,1)}, u32[]{:S(2)}, u32[]{:S(2)}) collective-permute-start(bf16[512,512]{1,0:T(8,128)(2,1)} %select_convert_fusion), channel_id=1, source_target_pairs={{0,1},{1,0},{2,3},{3,2},{4,5},{5,4},{6,7},{7,6},{8,9},{9,8},{10,11... | collective-permute-start | bytes 1572872 | tf_op jit(solution)/shard_map/ppermute | solution.py:855
  250.9 6.1 %copy-start.17 = (bf16[512,1024]{1,0:T(8,128)(2,1)}, bf16[512,1024]{1,0:T(8,128)(2,1)S(1)}, u32[]{:S(2)}) copy-start(bf16[512,1024]{1,0:T(8,128)(2,1)S(1)} %fusion.37.grad_ref.refs_1_.refs_5_) | copy-start | bytes 3145732
  275.5 19.6 %copy-start.20 = (bf16[1,1024,1536]{2,1,0:T(8,128)(2,1)S(1)}, bf16[1,1024,1536]{2,1,0:T(8,128)(2,1)}, u32[]{:S(2)}) copy-start(bf16[1,1024,1536]{2,1,0:T(8,128)(2,1)} %param.16) | copy-start | bytes 9437188
  295.1 3.4 copy-start.10
  301.1 5.0 collective-permute-start.9
  302.7 3.0 copy-start.12
  305.0 13.8 %copy-start.5 = (f32[512,1024]{1,0:T(8,128)S(1)}, f32[512,1024]{1,0:T(8,128)}, u32[]{:S(2)}) copy-start(f32[512,1024]{1,0:T(8,128)} %copy-done.4) | copy-start | bytes 6291460
  305.0 13.8 %copy-start.15 = (bf16[512,512]{1,0:T(8,128)(2,1)S(1)}, bf16[512,512]{1,0:T(8,128)(2,1)}, u32[]{:S(2)}) copy-start(bf16[512,512]{1,0:T(8,128)(2,1)} %copy-done.14) | copy-start | bytes 1572868
  305.1 13.7 %collective-permute-start.7 = (bf16[512,512]{1,0:T(8,128)(2,1)S(1)}, bf16[512,512]{1,0:T(8,128)(2,1)S(1)}, u32[]{:S(2)}, u32[]{:S(2)}) collective-permute-start(bf16[512,512]{1,0:T(8,128)(2,1)S(1)} %select_convert_fusion.1), channel_id=1, source_target_pairs={{0,1},{1,0},{2,3},{3,2},{4,5},{5,4},{6,7},{7,6},{8,9},{9,8},{10,11... | collective-permute-start | bytes 1572872 | tf_op jit(solution)/shard_map/ppermute | solution.py:855
  484.5 6.8 %copy-start.8 = (bf16[1024,2048]{1,0:T(8,128)(2,1)S(1)}, bf16[1024,2048]{1,0:T(8,128)(2,1)}, u32[]{:S(2)}) copy-start(bf16[1024,2048]{1,0:T(8,128)(2,1)} %get-tuple-element.71) | copy-start | bytes 12582916
  491.3 4.5 copy-start.9
  495.7 3.6 copy-start.16
  495.7 7.0 %copy-start.1 = (bf16[1,512,1024]{2,1,0:T(8,128)(2,1)S(1)}, bf16[1,512,1024]{2,1,0:T(8,128)(2,1)}, u32[]{:S(2)}) copy-start(bf16[1,512,1024]{2,1,0:T(8,128)(2,1)} %param.19) | copy-start | bytes 3145732

commit v4 on v3

--- a/solution.py
+++ b/solution.py
@@ -832,6 +832,95 @@
         + exchange_scratch(rows, pairs),
         4 * total * units * D,
     )(starts, state, grad, pre, w_down, w_up)
+
+
+STEPS = 8
+
+
+def hand_over_kernel(sender, part_ref, base_ref, full_ref, out_ref, *bufs):
+    (
+        away_buf, sum_buf, pass_buf,
+        sum_send, sum_recv, pass_send, pass_recv, spread_send, spread_recv,
+    ) = bufs
+    width = base_ref.shape[1]
+    height = base_ref.shape[0] // STEPS
+    pipe, tp = lax.axis_index("pipe"), lax.axis_index("tp")
+    sends = pipe == sender
+    own = pl.ds(pl.multiple_of(tp * width, width), width)
+    away = pl.ds(pl.multiple_of((1 - tp) * width, width), width)
+
+    def rows(c):
+        return slice(c * height, (c + 1) * height)
+
+    def remote(src, dst, send, recv, to):
+        return pltpu.make_async_remote_copy(
+            src_ref=src, dst_ref=dst, send_sem=send, recv_sem=recv,
+            device_id=to, device_id_type=pl.DeviceIdType.MESH,
+        )
+
+    def sum_copy(c):
+        return remote(away_buf.at[c], sum_buf.at[c], sum_send.at[c], sum_recv.at[c], {"tp": 1 - tp})
+
+    def pass_copy(c):
+        target = out_ref.at[rows(c), own]
+        return remote(pass_buf.at[c], target, pass_send.at[c], pass_recv.at[c], {"pipe": 1 - pipe})
+
+    def spread_copy(c):
+        piece = out_ref.at[rows(c), own]
+        return remote(piece, piece, spread_send.at[c], spread_recv.at[c], {"tp": 1 - tp})
+
+    barrier = pltpu.get_barrier_semaphore()
+
+    def greet(to):
+        pl.semaphore_signal(barrier, inc=1, device_id=to, device_id_type=pl.DeviceIdType.MESH)
+
+    greet({"tp": 1 - tp})
+
+    @pl.when(jnp.logical_not(sends))
+    def _():
+        greet({"pipe": 1 - pipe})
+
+    pl.semaphore_wait(barrier, 1 + sends.astype(jnp.int32))
+
+    @pl.when(sends)
+    def _():
+        for c in range(STEPS):
+            away_buf[c] = part_ref[rows(c), away].astype(BF)
+            sum_copy(c).start()
+        for c in range(STEPS):
+            out_ref[rows(c), :] = full_ref[rows(c), :]
+            sum_copy(c).wait_recv()
+            total = part_ref[rows(c), own] + sum_buf[c].astype(F32) + base_ref[rows(c), :]
+            pass_buf[c] = total.astype(BF)
+            pass_copy(c).start()
+        for c in range(STEPS):
+            sum_copy(c).wait_send()
+            pass_copy(c).wait_send()
+
+    @pl.when(jnp.logical_not(sends))
+    def _():
+        for c in range(STEPS):
+            pass_copy(c).wait_recv()
+            spread_copy(c).start()
+        for c in range(STEPS):
+            spread_copy(c).wait_send()
+            spread_copy(c).wait_recv()
+
+
+def hand_over(sender, part, base, full):
+    total, width = base.shape
+    piece = pltpu.VMEM((STEPS, total // STEPS, width), BF)
+    return pl.pallas_call(
+        partial(hand_over_kernel, sender),
+        in_specs=[IN_VMEM] * 3,
+        out_specs=IN_VMEM,
+        out_shape=shaped(full.shape, BF),
+        scratch_shapes=[piece] * 3 + [pltpu.SemaphoreType.DMA((STEPS,))] * 6,
+        compiler_params=pltpu.CompilerParams(
+            collective_id=3 + sender, has_side_effects=True, vmem_limit_bytes=VMEM_LIMIT
+        ),
+        cost_estimate=pl.CostEstimate(flops=1 << 20, bytes_accessed=8 << 20, transcendentals=0),
+    )(part, base, full)
 
 
 def gather_tp(value):
@@ -894,7 +983,7 @@
     low_shape, full_shape = shaped((total, pairs * PAIR), BF), shaped((total, pairs * PAIR), F32)
     unit = 2 * rows * tokens * PAIR * PAIR * pairs
 
-    def forward(u_low, own):
+    def forward(u_low):
         u = u_low.astype(F32)
         centered = u - jnp.mean(u, -1, keepdims=True)
         inv = lax.rsqrt(jnp.mean(centered * centered, -1, keepdims=True) + norm_eps)
@@ -920,9 +1009,8 @@
             8 * unit,
         )(starts, place_in, q, k, v, state_in)
         part = jnp.dot(att_low, w_dense, preferred_element_type=F32) + mlp
-        out = scatter_tp(part) + own.astype(F32) + b_out
         kept = (xhat, inv, first, second, q, k, v, pre, hidden, att_low, att, den, state_in)
-        return out, kept
+        return part, kept
 
     def backward(dy, own, kept, want):
         xhat, inv, first, second, q, k, v, pre, hidden, att_low, att, den, state_in = kept
@@ -956,9 +1044,8 @@
             - jnp.mean(both, -1, keepdims=True)
             - xhat * jnp.mean(both * xhat, -1, keepdims=True)
         )
-        grad_input = scatter_tp(part) + own.astype(F32)
         if not want:
-            return grad_input, None
+            return part, None
 
         large = ((hidden, dy), (second, grad_pre), (att_low, dy), (first, grad_proj))
         norm_sums = jnp.stack(
@@ -975,20 +1062,33 @@
             jnp.sum(own.astype(F32), 0),
             jnp.sum(grad_pre.astype(F32), 0),
         )
-        return grad_input, (large, norm_sums, small)
+        return part, (large, norm_sums, small)
 
     mine = section_inputs[0].reshape(total, width)
     mine_full = gather_tp(mine)
-    y0, _ = forward(mine_full, mine)
-    sent = lax.ppermute(y0.astype(BF), "pipe", [(0, 1)])
-    own_in = jnp.where(section == 0, mine, sent)
-    full_in = jnp.where(section == 0, mine_full, gather_tp(sent))
-    y1, kept = forward(full_in, own_in)
-    du1, _ = backward(mine_full, mine, kept, False)
-    sent = lax.ppermute(du1.astype(BF), "pipe", [(1, 0)])
-    own_grad = jnp.where(section == 1, mine, sent)
-    full_grad = jnp.where(section == 1, mine_full, gather_tp(sent))
-    du0, (large, norm_sums, small) = backward(full_grad, own_grad, kept, True)
+    tp_place = lax.axis_index("tp")
+
+    def own_part(full):
+        return lax.dynamic_slice_in_dim(full, tp_place * width, width, 1)
+
+    def next_section(sender, part, base):
+        if lax.axis_size("tp") == 2 and total % (16 * STEPS) == 0:
+            return hand_over(sender, part, base, mine_full)
+        sent = (scatter_tp(part) + base).astype(BF)
+        sent = lax.ppermute(sent, "pipe", [(sender, 1 - sender)])
+        return jnp.where(section == sender, mine_full, gather_tp(sent))
+
+    wide = mine.astype(F32)
+    part, _ = forward(mine_full)
+    full_in = next_section(0, part, wide + b_out)
+    part, kept = forward(full_in)
+    y1 = scatter_tp(part) + own_part(full_in).astype(F32) + b_out
+    part, _ = backward(mine_full, mine, kept, False)
+    full_grad = next_section(1, part, wide)
+    y1, full_grad = lax.optimization_barrier((y1, full_grad))
+    own_grad = own_part(full_grad)
+    part, (large, norm_sums, small) = backward(full_grad, own_grad, kept, True)
+    du0 = scatter_tp(part) + own_grad.astype(F32)
     if lax.axis_size("tp") == 2:
         me = lax.axis_index("tp")
         away = lax.dynamic_slice_in_dim(norm_sums, (1 - me) * width, width, 1)

time: 510 us -> 480 us (0.941); the launches traced: 503 us -> 479 us
  waiting for transfers between devices: 85.1 us -> 14.4 us
  Pallas kernels: 332 us -> 392 us
  starting transfers between devices: 17.1 us -> 5.76 us
    pallas_call x0 -> x2, Pallas kernels: none -> 56.9 us  [hand_over(): pl.pallas_call(partial(hand_over_kernel, sender), in_specs=[IN_VMEM] * 3,...]
    ppermute x4 -> x2, waiting for transfers between devices: 37.5 us -> 11.3 us  [scatter_tp(): lax.ppermute(jnp.where(me == 0, right, left).astype(BF), 'tp', [(0, 1), (...]
    ppermute x2 -> x0, waiting for transfers between devices: 24.2 us -> none  [the longest x1 13.6 us: local(): sent = lax.ppermute(du1.astype(BF), 'pipe', [(1, 0)])]
    ppermute x3 -> x1, waiting for transfers between devices: 23.4 us -> 3.01 us  [gather_tp(): other = lax.ppermute(value, 'tp', [(0, 1), (1, 0)])]
    ppermute x2 -> x0, starting transfers between devices: 5.27 us -> none  [the longest x1 3.99 us: local(): sent = lax.ppermute(y0.astype(BF), 'pipe', [(0, 1)])]
  transfers between devices with their start and end apart: 10 -> 4, of which waited for: 8 -> 2; matrix products, arithmetic and copies ran while one was open for 5% -> 3% of each run, Pallas kernels for 8% -> 7%
where the time goes in v4:
time: 480 us; the launch traced here: 479 us
  Pallas kernels  392 us (82%)
  other arithmetic  36 us (8%)
  matrix products  16.5 us (3%)
  waiting for transfers between devices  14.4 us (3%)
  local copies, waits for them, and re-layouts  13.1 us (3%)
  starting transfers between devices  5.76 us (1%)
    pallas_call x1, Pallas kernels, reduce_over_ctx(): pl.pallas_call(partial(reduce_kernel, (count, terms)), in_specs=[pl.Block...  159 us
    pallas_call x2, Pallas kernels, hand_over(): pl.pallas_call(partial(hand_over_kernel, sender), in_specs=[IN_VMEM] * 3,...  56.9 us
    pallas_call x2, Pallas kernels, feed_backward(): link_call(partial(feed_backward_kernel, total // rows), 2, [SMEM, IN_VMEM...  53.7 us
    pallas_call x2, Pallas kernels, backward(): call(back_kernel, pairs, [SMEM, SMEM] + [column(total, PAIR)] * 6 + [stat...  36.2 us
    pallas_call x2, Pallas kernels, feed_forward(): link_call(partial(feed_forward_kernel, total // rows), 1, [SMEM, IN_VMEM,...  33.6 us
    pallas_call x2, Pallas kernels, forward(): call(features_kernel, pairs, [SMEM, SMEM, whole((total, D)), column(D, 3...  26 us
    pallas_call x2, Pallas kernels, forward(): call(attend_kernel, pairs, [SMEM, SMEM] + [column(total, PAIR)] * 3 + [st...  17 us
    broadcast_in_dim x4, other arithmetic, local(): return (section_ends,) + tuple((g[None] for g in grads))  16.4 us
  transfers between devices with their start and end apart: 4, of which 2 were waited for; matrix products, arithmetic and copies ran while one was open for 3% of the time, Pallas kernels for 7%

profile of v4, /device:TPU:0, one launch (start us, length us, event | category | flops | bytes accessed | tf_op | source)
XLA Modules:
  0.0 478.6 jit_solution(7092217982773393191)
XLA Ops:
  0.7 3.0 collective-permute-start
  3.7 0.8 fusion.72
  4.5 0.8 fusion.73
  5.7 0.8 concatenate.36.down_ref
  6.4 0.8 concatenate.37.up_ref
  8.4 1.3 reshape_squeeze.11.feat_ref
  9.7 0.8 concatenate.35.same_ref
  10.5 1.1 bitcast_convert_fusion.4.base_ref
  11.7 1.1 broadcast_add_fusion.base_ref
  12.8 3.0 collective-permute-done
  16.6 1.5 convolution_convert_fusion.1.ga_ref
  18.1 1.9 fusion.17
  20.1 13.0 %shard_map.203 = (bf16[512,512]{1,0:T(8,128)(2,1)}, bf16[512,512]{1,0:T(8,128)(2,1)}, bf16[512,512]{1,0:T(8,128)(2,1)}, f32[4,4,72,128]{3,2,1,0:T(8,128)}) custom-call(s32[4,4]{1,0:T(4,128)} %bitcast.73, s32[1,1]{1,0:T(1,128)} %bitcast.1.place_ref, bf16[512,1024]{1,0:T(8,128)(2,1)} %get-tuple-element.129.norm_ref, bf16[1024,1536]{1,0:T(8,128)(2,1)} %bitcast.115, ...), custom_call_target="tpu_custom_call" | custom-call | flops 2013265920 | bytes 8388608 | tf_op jit(solution)/shard_map/pallas_call | solution.py:993
  33.0 14.8 %shard_map.204 = (f32[512,2048]{1,0:T(8,128)}, bf16[512,2048]{1,0:T(8,128)(2,1)}, f32[512,1024]{1,0:T(8,128)}, f32[4,4,72,128]{3,2,1,0:T(8,128)}) custom-call(s32[4,4]{1,0:T(4,128)} %bitcast.74, f32[4,4,72,128]{3,2,1,0:T(8,128)} %get-tuple-element.47.own_ref, bf16[512,1024]{1,0:T(8,128)(2,1)} %get-tuple-element.128.norm_ref, bf16[1024,2048]{1,0:T(8,128)(2,1)} %bitcast.107, ...), custom_call_target="tpu_custom_call" | custom-call | flops 4294967296 | bytes 16777216 | tf_op jit(solution)/shard_map/pallas_call | solution.py:802
  47.8 8.5 %shard_map.205 = (bf16[512,512]{1,0:T(8,128)(2,1)}, f32[512,512]{1,0:T(8,128)}, f32[512,512]{1,0:T(8,128)}) custom-call(s32[4,4]{1,0:T(4,128)} %bitcast.75, s32[1,1]{1,0:T(1,128)} %bitcast.1.place_ref, bf16[512,512]{1,0:T(8,128)(2,1)} %get-tuple-element.44.q_ref, bf16[512,512]{1,0:T(8,128)(2,1)} %get-tuple-element.45.k_ref, ...), custom_call_target="tpu_custom_call" | custom-call | flops 536870912 | bytes 8388608 | tf_op jit(solution)/shard_map/pallas_call | solution.py:1003
  56.4 3.1 convolution_add_fusion.1.part_ref
  59.5 21.1 %shard_map.206 = bf16[512,1024]{1,0:T(8,128)(2,1)} custom-call(f32[512,1024]{1,0:T(8,128)} %convolution_add_fusion.1.part_ref, f32[512,512]{1,0:T(8,128)} %broadcast_add_fusion.base_ref, bf16[512,1024]{1,0:T(8,128)(2,1)} %copy-done.3), custom_call_target="tpu_custom_call" | custom-call | flops 1048576 | bytes 8388608 | tf_op jit(solution)/shard_map/pallas_call | solution.py:913
  80.6 1.5 convert_reduce_fusion.1
  82.1 1.6 fusion.30
  83.7 2.0 fusion.21
  85.7 13.0 %shard_map.207 = (bf16[512,512]{1,0:T(8,128)(2,1)}, bf16[512,512]{1,0:T(8,128)(2,1)}, bf16[512,512]{1,0:T(8,128)(2,1)}, f32[4,4,72,128]{3,2,1,0:T(8,128)}) custom-call(s32[4,4]{1,0:T(4,128)} %bitcast.76, s32[1,1]{1,0:T(1,128)} %bitcast.1.place_ref, bf16[512,1024]{1,0:T(8,128)(2,1)} %get-tuple-element.127.norm_ref.refs_6_, bf16[1024,1536]{1,0:T(8,128)(2,1)} %bitcast.116, ...), custom_call_target="tpu_custom_call" | custom-call | flops 2013265920 | bytes 8388608 | tf_op jit(solution)/shard_map/pallas_call | solution.py:993
  98.7 18.8 %shard_map.208 = (f32[512,2048]{1,0:T(8,128)}, bf16[512,2048]{1,0:T(8,128)(2,1)}, f32[512,1024]{1,0:T(8,128)}, f32[4,4,72,128]{3,2,1,0:T(8,128)}) custom-call(s32[4,4]{1,0:T(4,128)} %bitcast.77, f32[4,4,72,128]{3,2,1,0:T(8,128)} %get-tuple-element.54.own_ref, bf16[512,1024]{1,0:T(8,128)(2,1)} %get-tuple-element.126.norm_ref.refs_2_, ...), custom_call_target="tpu_custom_call" | custom-call | flops 4294967296 | bytes 16777216 | tf_op jit(solution)/shard_map/pallas_call | solution.py:802
  117.5 8.4 %shard_map.209 = (bf16[512,512]{1,0:T(8,128)(2,1)}, f32[512,512]{1,0:T(8,128)}, f32[512,512]{1,0:T(8,128)}) custom-call(s32[4,4]{1,0:T(4,128)} %bitcast.78, s32[1,1]{1,0:T(1,128)} %bitcast.1.place_ref, bf16[512,512]{1,0:T(8,128)(2,1)} %get-tuple-element.51.q_ref, bf16[512,512]{1,0:T(8,128)(2,1)} %get-tuple-element.52.k_ref, ...), custom_call_target="tpu_custom_call" | custom-call | flops 536870912 | bytes 8388608 | tf_op jit(solution)/shard_map/pallas_call | solution.py:1003
  125.9 4.5 shard_map.210.own_ref
  130.4 35.0 %shard_map.211 = (bf16[512,2048]{1,0:T(8,128)(2,1)}, f32[512,1024]{1,0:T(8,128)}, f32[4,4,72,128]{3,2,1,0:T(8,128)}) custom-call(s32[4,4]{1,0:T(4,128)} %bitcast.80, f32[4,4,72,128]{3,2,1,0:T(8,128)} %shard_map.210.own_ref, bf16[512,1024]{1,0:T(8,128)(2,1)} %copy-done.3, f32[512,2048]{1,0:T(8,128)} %get-tuple-element.60.pre_ref, ...), custom_call_target="tpu_custom_call" | custom-call | flops 4294967296 | bytes 16777216 | tf_op jit(solution)/shard_map/pallas_call | solution.py:822
  165.4 18.1 %shard_map.212 = (bf16[512,1536]{1,0:T(8,128)(2,1)}, f32[4,8,128]{2,1,0:T(8,128)}) custom-call(s32[4,4]{1,0:T(4,128)} %bitcast.81, s32[1,1]{1,0:T(1,128)} %bitcast.1.place_ref, bf16[512,512]{1,0:T(8,128)(2,1)} %get-tuple-element.51.q_ref, bf16[512,512]{1,0:T(8,128)(2,1)} %get-tuple-element.52.k_ref, bf16[512,512]{1,0:T(8,128)(2,1)} %get-tuple-element.53.v_ref, ...), custom_call_target="tpu_custom_call" | custom-call | flops 1342177280 | bytes 8388608 | tf_op jit(solution)/shard_map/pallas_call | solution.py:1029
  183.5 3.4 fusion.64
  186.9 0.9 fusion.71
  190.0 1.9 fusion.24.part_ref
  191.9 35.8 %shard_map.213.grad_ref.refs_1_.refs_5_ = bf16[512,1024]{1,0:T(8,128)(2,1)} custom-call(f32[512,1024]{1,0:T(8,128)} %fusion.24.part_ref, f32[512,512]{1,0:T(8,128)} %bitcast_convert_fusion.4.base_ref, bf16[512,1024]{1,0:T(8,128)(2,1)} %copy-done.3), custom_call_target="tpu_custom_call" | custom-call | flops 1048576 | bytes 8388608 | tf_op jit(solution)/shard_map/pallas_call | solution.py:913
  228.1 0.8 copy-done.7
  228.9 1.5 convolution_convert_fusion.ga_ref
  230.4 4.5 shard_map.214.own_ref
  234.9 18.8 %shard_map.215 = (bf16[512,2048]{1,0:T(8,128)(2,1)}, f32[512,1024]{1,0:T(8,128)}, f32[4,4,72,128]{3,2,1,0:T(8,128)}) custom-call(s32[4,4]{1,0:T(4,128)} %bitcast.83, f32[4,4,72,128]{3,2,1,0:T(8,128)} %shard_map.214.own_ref, bf16[512,1024]{1,0:T(8,128)(2,1)} %shard_map.213.grad_ref.refs_1_.refs_5_, f32[512,2048]{1,0:T(8,128)} %get-tuple-element.60.pre_ref, ...), custom_call_target="tpu_custom_call" | custom-call | flops 4294967296 | bytes 16777216 | tf_op jit(solution)/shard_map/pallas_call | solution.py:822
  253.7 18.1 %shard_map.216 = (bf16[512,1536]{1,0:T(8,128)(2,1)}, f32[4,8,128]{2,1,0:T(8,128)}) custom-call(s32[4,4]{1,0:T(4,128)} %bitcast.84, s32[1,1]{1,0:T(1,128)} %bitcast.1.place_ref, bf16[512,512]{1,0:T(8,128)(2,1)} %get-tuple-element.51.q_ref, bf16[512,512]{1,0:T(8,128)(2,1)} %get-tuple-element.52.k_ref, bf16[512,512]{1,0:T(8,128)(2,1)} %get-tuple-element.53.v_ref, ...), custom_call_target="tpu_custom_call" | custom-call | flops 1342177280 | bytes 8388608 | tf_op jit(solution)/shard_map/pallas_call | solution.py:1029
  273.3 5.8 %fusion.70 = (f32[512]{0:T(512)S(1)}, f32[512]{0:T(512)S(1)}, f32[1024]{0:T(1024)S(1)}, f32[1024]{0:T(1024)S(1)}, f32[1024]{0:T(1024)S(1)}, /*index=5*/f32[1024]{0:T(1024)S(1)}, f32[512,1024]{1,0:T(8,128)}) fusion(f32[512]{0:T(512)S(1)} %add_rsqrt_fusion, f32[512]{0:T(512)S(1)} %broadcast_multiply_fusion.4, bf16[512,1024]{1,0:T(8,128)(2,1)S(1)} %copy-done.2, ...), kind=kOutput, calls=%fused_computation.129 | convolution fusion | flops 1618471936 | bytes 9994240 | tf_op jit(solution)/shard_map/dot_general | solution.py:1038
  279.8 2.3 fusion.27
  282.2 1.6 collective-permute-start.2
  284.2 11.3 %collective-permute-done.2 = bf16[512,512]{1,0:T(8,128)(2,1)S(1)} collective-permute-done((bf16[512,512]{1,0:T(8,128)(2,1)S(1)}, bf16[512,512]{1,0:T(8,128)(2,1)S(1)}, u32[]{:S(2)}, u32[]{:S(2)}) %collective-permute-start.2) | collective-permute-done | bytes 524320 | tf_op jit(solution)/shard_map/ppermute | solution.py:944
  295.5 1.4 convert_reduce_fusion.3
  297.0 0.9 reshape.153.refs_8_
  297.9 159.5 %shard_map.217 = (bf16[2048,1024]{1,0:T(8,128)(2,1)}, bf16[1024,2048]{1,0:T(8,128)(2,1)}, bf16[512,1024]{1,0:T(8,128)(2,1)}, bf16[1024,1536]{1,0:T(8,128)(2,1)}, bf16[256,512]{1,0:T(8,128)(2,1)}) custom-call(bf16[512,2048]{1,0:T(8,128)(2,1)} %get-tuple-element.69.refs_0_, bf16[512,1024]{1,0:T(8,128)(2,1)} %shard_map.213.grad_ref.refs_1_.refs_5_, ...), custom_call_target="tpu_custom_call" | custom-call | flops 6576668672 | bytes 41943040 | tf_op jit(solution)/shard_map/pallas_call | solution.py:535
  457.4 1.0 convert_element_type.121
  459.1 1.3 slice.93
  460.3 6.8 %bitcast_convert_fusion = f32[1,2048,1024]{2,1,0:T(8,128)} fusion(bf16[2048,1024]{1,0:T(8,128)(2,1)} %get-tuple-element.76), kind=kLoop, calls=%fused_computation | loop fusion | flops 2097152 | bytes 12582912 | tf_op jit(solution)/shard_map/broadcast_in_dim | solution.py:1118
  467.1 4.5 bitcast_convert_fusion.1
  471.6 3.6 bitcast_convert_fusion.2
  475.2 1.6 bitcast_convert_fusion.3
  (86 shorter events, 10.0 us)
Async XLA Ops:
  0.6 15.9 %copy-start = (bf16[1,512,1024]{2,1,0:T(8,128)(2,1)S(1)}, bf16[1,512,1024]{2,1,0:T(8,128)(2,1)}, u32[]{:S(2)}) copy-start(bf16[1,512,1024]{2,1,0:T(8,128)(2,1)} %param.19) | copy-start | bytes 3145732
  0.7 9.9 %copy-start.4 = (bf16[1,4,1,128,512]{4,3,2,1,0:T(8,128)(2,1)S(1)}, bf16[1,4,1,128,512]{4,3,2,1,0:T(8,128)(2,1)}, u32[]{:S(2)}) copy-start(bf16[1,4,1,128,512]{4,3,2,1,0:T(8,128)(2,1)} %param.12) | copy-start | bytes 1572868
  0.7 11.0 %copy-start.15 = (f32[1,512]{1,0:T(1,128)S(1)}, f32[1,512]{1,0:T(1,128)}, u32[]{:S(2)}) copy-start(f32[1,512]{1,0:T(1,128)} %param.20) | copy-start | bytes 6148
  0.7 15.1 %collective-permute-start = (bf16[512,512]{1,0:T(8,128)(2,1)}, bf16[512,512]{1,0:T(8,128)(2,1)S(1)}, u32[]{:S(2)}, u32[]{:S(2)}) collective-permute-start(bf16[512,512]{1,0:T(8,128)(2,1)} %bitcast.70), channel_id=1, source_target_pairs={{0,1},{1,0},{2,3},{3,2},{4,5},{5,4},{6,7},{7,6},{8,9},{9,8},{10,11... | collective-permute-start | bytes 1572872 | tf_op jit(solution)/shard_map/ppermute | solution.py:929
  16.1 2.0 copy-start.3
  47.8 8.6 %copy-start.12 = (f32[512,1024]{1,0:T(8,128)S(1)}, f32[512,1024]{1,0:T(8,128)}, u32[]{:S(2)}) copy-start(f32[512,1024]{1,0:T(8,128)} %get-tuple-element.50) | copy-start | bytes 6291460
  80.6 3.2 copy-start.2
  165.4 18.1 %copy-start.16 = (bf16[1,1024,1536]{2,1,0:T(8,128)(2,1)S(1)}, bf16[1,1024,1536]{2,1,0:T(8,128)(2,1)}, u32[]{:S(2)}) copy-start(bf16[1,1024,1536]{2,1,0:T(8,128)(2,1)} %param.16) | copy-start | bytes 9437188
  183.5 3.4 copy-start.9
  186.9 1.6 copy-start.11
  186.9 1.7 copy-start.14
  189.4 38.3 %collective-permute-start.1 = (bf16[512,512]{1,0:T(8,128)(2,1)S(1)}, bf16[512,512]{1,0:T(8,128)(2,1)S(1)}, u32[]{:S(2)}, u32[]{:S(2)}) collective-permute-start(bf16[512,512]{1,0:T(8,128)(2,1)S(1)} %select_convert_fusion.1), channel_id=1, source_target_pairs={{0,1},{1,0},{2,3},{3,2},{4,5},{5,4},{6,7},{7,6},{8,9},{9,8},{10,11... | collective-permute-start | bytes 1572872 | tf_op jit(solution)/shard_map/ppermute | solution.py:944
  227.7 1.2 copy-start.7
  253.7 19.6 %copy-start.17 = (bf16[1,1024,1536]{2,1,0:T(8,128)(2,1)S(1)}, bf16[1,1024,1536]{2,1,0:T(8,128)(2,1)}, u32[]{:S(2)}) copy-start(bf16[1,1024,1536]{2,1,0:T(8,128)(2,1)} %param.16) | copy-start | bytes 9437188
  279.2 5.0 %collective-permute-start.3 = (f32[4,512]{1,0:T(4,128)S(1)}, f32[4,512]{1,0:T(4,128)S(1)}, u32[]{:S(2)}, u32[]{:S(2)}) collective-permute-start(f32[4,512]{1,0:T(4,128)S(1)} %constant_dynamic-slice_fusion), channel_id=1, source_target_pairs={{0,1},{1,0},{2,3},{3,2},{4,5},{5,4},{6,7},{7,6},{8,9},{9,8},{10,11... | collective-permute-start | bytes 24584 | tf_op jit(solution)/shard_map/ppermute | solution.py:1096
  279.8 4.0 copy-start.10
  282.1 13.4 %copy-start.8 = (bf16[512,1024]{1,0:T(8,128)(2,1)S(1)}, bf16[512,1024]{1,0:T(8,128)(2,1)}, u32[]{:S(2)}) copy-start(bf16[512,1024]{1,0:T(8,128)(2,1)} %shard_map.213.grad_ref.refs_1_.refs_5_) | copy-start | bytes 3145732
  282.2 13.3 %collective-permute-start.2 = (bf16[512,512]{1,0:T(8,128)(2,1)S(1)}, bf16[512,512]{1,0:T(8,128)(2,1)S(1)}, u32[]{:S(2)}, u32[]{:S(2)}) collective-permute-start(bf16[512,512]{1,0:T(8,128)(2,1)S(1)} %select_convert_fusion), channel_id=1, source_target_pairs={{0,1},{1,0},{2,3},{3,2},{4,5},{5,4},{6,7},{7,6},{8,9},{9,8},{10,11... | collective-permute-start | bytes 1572872 | tf_op jit(solution)/shard_map/ppermute | solution.py:944
  460.3 6.8 %copy-start.5 = (bf16[1024,2048]{1,0:T(8,128)(2,1)S(1)}, bf16[1024,2048]{1,0:T(8,128)(2,1)}, u32[]{:S(2)}) copy-start(bf16[1024,2048]{1,0:T(8,128)(2,1)} %get-tuple-element.75) | copy-start | bytes 12582916
  467.1 4.5 copy-start.6
  471.6 3.6 copy-start.13
  471.6 7.0 %copy-start.1 = (bf16[1,512,1024]{2,1,0:T(8,128)(2,1)S(1)}, bf16[1,512,1024]{2,1,0:T(8,128)(2,1)}, u32[]{:S(2)}) copy-start(bf16[1,512,1024]{2,1,0:T(8,128)(2,1)} %param.19) | copy-start | bytes 3145732

commit v5 on v4

--- a/solution.py
+++ b/solution.py
@@ -248,6 +248,56 @@
         keep_state(state_ref, row, dot(query, grad_num, 0, 0), grad_den * query.astype(F32), low)
 
 
+def back_unit(starts_ref, row, base, q, k, v, ga, att, den, held, later_held, tables):
+    same, down, up, high, low_table = tables
+    tokens = q.shape[0]
+    half = tokens // 2
+    low, first, second = lane_masks(tokens)
+    grad_num = (ga.astype(F32) / den).astype(BF)
+    both = -split_dot(grad_num.astype(F32) * att, head_spread())
+    dens = (both[:, :PAIR], both[:, PAIR:])
+    grad_den = jnp.where(low, dens[0], dens[1])
+    mask, mask_in = causal_mask(starts_ref, row, base, tokens)
+    enter = entering_mask(starts_ref, row, base, tokens)
+    leave = leaving_mask(starts_ref, row, base, tokens)
+    carry, total = held[:HD], held[HD : HD + 1]
+    middle, middle_total, reach = middle_state(
+        starts_ref, row, base, tokens, k, v, carry, total, low
+    )
+    state, middle = spread(carry.astype(BF), first, second), spread(middle, first, second)
+    gq = jnp.concatenate(
+        [
+            enter[:half] * (dot(grad_num[:half], state, 1, 1) + grad_den[:half] * total),
+            reach * (dot(grad_num[half:], middle, 1, 1) + grad_den[half:] * middle_total),
+        ],
+        0,
+    )
+    later = later_held[:HD]
+    later_high = later.astype(BF)
+    later_low = spread((later - later_high.astype(F32)).astype(BF), first, second)
+    later_high = spread(later_high, first, second)
+    gk = leave * (
+        dot(v, later_high, 1, 1) + dot(v, later_low, 1, 1) + later_held[HD : HD + 1]
+    )
+    gv = leave * (dot(k, later_high) + dot(k, later_low))
+    for head, grad_head_den in zip((first, second), dens):
+        q_head, grad_head = q * head, grad_num * head
+        scores = (dot(q_head, k, 1, 1) * mask).astype(BF)
+        grad_scores = dot(grad_head, v, 1, 1) + grad_head_den
+        gq = gq + dot((grad_scores * mask_in).astype(BF), k * head)
+        gk = gk + dot((grad_scores * mask).astype(BF), q_head, 0, 0)
+        gv = gv + dot(scores, grad_head, 0, 0)
+    arg_grads = (gq * q.astype(F32), gk * k.astype(F32))
+    feat_sum = jnp.sum(arg_grads[0] + arg_grads[1], 0, keepdims=True)
+    turned = []
+    for x in arg_grads:
+        x = split_dot(x, high, 1) + dot(x.astype(BF), low_table, 1, 1)
+        turned.append(rotate_back(x, same, down, up))
+    dq, dk = turned[0], pltpu.roll(turned[1], HD, 1)
+    parts = (jnp.where(low, dq, dk), jnp.where(low, gv, dq), jnp.where(low, dk, gv))
+    return tuple(part.astype(BF) for part in parts), feat_sum
+
+
 def back_kernel(
     starts_ref, place_ref, q_ref, k_ref, v_ref, ga_ref, att_ref, den_ref,
     state_ref, later_ref, feat_ref,
@@ -256,68 +306,18 @@
 ):
     tokens = q_ref.shape[0] // (MB * ROWS)
     base = place_ref[0, 0] * tokens
-    low, first, second = lane_masks(tokens)
-    spreading = head_spread()
-    feat_sum = jnp.zeros((1, PAIR), F32)
-    bias_sum = [jnp.zeros((1, PAIR), F32) for _ in range(3)]
+    tables = tuple(t[...] for t in (same_ref, down_ref, up_ref, high_ref, low_ref))
+    sums_ref[...] = jnp.zeros_like(sums_ref)
     for row in range(MB * ROWS):
         here = slice(row * tokens, (row + 1) * tokens)
-        q, k, v = q_ref[here, :], k_ref[here, :], v_ref[here, :]
-        grad_num = (ga_ref[here, :].astype(F32) / den_ref[here, :]).astype(BF)
-        both = -split_dot(grad_num.astype(F32) * att_ref[here, :], spreading)
-        dens = (both[:, :PAIR], both[:, PAIR:])
-        grad_den = jnp.where(low, dens[0], dens[1])
-        mask, mask_in = causal_mask(starts_ref, row, base, tokens)
-        enter = entering_mask(starts_ref, row, base, tokens)
-        leave = leaving_mask(starts_ref, row, base, tokens)
-        carry, total = state_ref[row, 0, :HD], state_ref[row, 0, HD : HD + 1]
-        state = carry.astype(BF)
-        middle, middle_total, reach = middle_state(
-            starts_ref, row, base, tokens, k, v, carry, total, low
-        )
-        half = tokens // 2
-        gq = jnp.concatenate(
-            [
-                enter[:half]
-                * (dot(grad_num[:half], spread(state, first, second), 1, 1) + grad_den[:half] * total),
-                reach
-                * (
-                    dot(grad_num[half:], spread(middle, first, second), 1, 1)
-                    + grad_den[half:] * middle_total
-                ),
-            ],
-            0,
-        )
-        later = later_ref[row, 0, :HD]
-        later_high = later.astype(BF)
-        later_low = spread((later - later_high.astype(F32)).astype(BF), first, second)
-        later_high = spread(later_high, first, second)
-        gk = leave * (
-            dot(v, later_high, 1, 1) + dot(v, later_low, 1, 1) + later_ref[row, 0, HD : HD + 1]
-        )
-        gv = leave * (dot(k, later_high) + dot(k, later_low))
-        for head, den in zip((first, second), dens):
-            q_head, grad_head = q * head, grad_num * head
-            scores = (dot(q_head, k, 1, 1) * mask).astype(BF)
-            grad_scores = dot(grad_head, v, 1, 1) + den
-            gq = gq + dot((grad_scores * mask_in).astype(BF), k * head)
-            gk = gk + dot((grad_scores * mask).astype(BF), q_head, 0, 0)
-            gv = gv + dot(scores, grad_head, 0, 0)
-        arg_grads = (gq * q.astype(F32), gk * k.astype(F32))
-        feat_sum = feat_sum + jnp.sum(arg_grads[0] + arg_grads[1], 0, keepdims=True)
-        turned = []
-        for x in arg_grads:
-            x = split_dot(x, high_ref[...], 1) + dot(x.astype(BF), low_ref[...], 1, 1)
-            turned.append(rotate_back(x, same_ref[...], down_ref[...], up_ref[...]))
-        dq, dk = turned[0], pltpu.roll(turned[1], HD, 1)
-        parts = (jnp.where(low, dq, dk), jnp.where(low, gv, dq), jnp.where(low, dk, gv))
+        values = [r[here, :] for r in (q_ref, k_ref, v_ref, ga_ref, att_ref, den_ref)]
+        parts, feat_sum = back_unit(
+            starts_ref, row, base, *values, state_ref[row, 0], later_ref[row, 0], tables
+        )
+        sums_ref[0, 0:1, :] += feat_sum / feat_ref[0]
         for n, part in enumerate(parts):
-            part = part.astype(BF)
             grad_ref[here, n * PAIR : (n + 1) * PAIR] = part
-            bias_sum[n] = bias_sum[n] + jnp.sum(part.astype(F32), 0, keepdims=True)
-    sums_ref[0, 0:1, :] = feat_sum / feat_ref[0]
-    for n in range(3):
-        sums_ref[0, n + 1 : n + 2, :] = bias_sum[n]
+            sums_ref[0, n + 1 : n + 2, :] += jnp.sum(part.astype(F32), 0, keepdims=True)
 
 
 SMEM = pl.BlockSpec(memory_space=pltpu.SMEM)
@@ -357,15 +357,31 @@
 LAG = 6
 
 
-def reduce_kernel(plan, *refs):
+def last_kernel(plan, *refs):
     count, terms = plan
-    factors, small_ref = refs[: 2 * len(terms)], refs[2 * len(terms)]
-    outs = refs[2 * len(terms) + 1 : 3 * len(terms) + 2]
     (
-        work, give, take, part, outside, inside,
+        starts_ref, hidden_ref, dy_ref, second_ref, grad_pre_ref, low_ref, first_ref,
+        q_ref, k_ref, v_ref, ga_ref, att_ref, den_ref, state_ref, later_ref, feat_ref,
+        same_ref, down_ref, up_ref, high_table_ref, low_table_ref,
+        qkv_ref, grad_second_ref, xhat_ref, inv_ref, gain_ref, small_in_ref,
+    ) = refs[:27]
+    outs, du_ref = refs[27:32], refs[32]
+    (
+        proj, small_ref, away_buf, come_buf, norm_sum, norm_away, norm_come,
+        sum_send, sum_recv, norm_sem,
+        work, give, take, outside, inside,
         give_send, give_recv, part_send, outer_recv, inner_recv, total_send,
         final_send, final_recv, own_sem,
-    ) = refs[3 * len(terms) + 2 :]
+    ) = refs[33:]
+    part = give
+    factors = (
+        hidden_ref, dy_ref, second_ref, grad_pre_ref, low_ref, dy_ref, first_ref, proj
+    )
+    rows, pairs = state_ref.shape[:2]
+    tokens, width = q_ref.shape[0] // rows, du_ref.shape[1]
+    units = rows * pairs
+    tp = lax.axis_index("tp")
+    my_cols = pl.ds(pl.multiple_of(tp * width, width), width)
     half = CHUNK // 2
     place, peers = lax.axis_index("ctx"), lax.axis_size("ctx")
     core, z, chips = place % 2, place // 2, peers // 2
@@ -383,6 +399,87 @@
             device_id={"ctx": to}, device_id_type=pl.DeviceIdType.MESH,
         )
 
+    def to_tp(src, dst, send, recv):
+        return pltpu.make_async_remote_copy(
+            src_ref=src, dst_ref=dst, send_sem=send, recv_sem=recv,
+            device_id={"tp": 1 - tp}, device_id_type=pl.DeviceIdType.MESH,
+        )
+
+    def sum_copy(m):
+        return to_tp(away_buf.at[m], come_buf.at[m], sum_send.at[m], sum_recv.at[m])
+
+    def norm_copy():
+        return to_tp(norm_away, norm_come, norm_sem.at[0], norm_sem.at[1])
+
+    def split_cols(x):
+        left, right = x[:, :width], x[:, width:]
+        return jnp.where(tp == 0, left, right), jnp.where(tp == 0, right, left)
+
+    def row_block(m):
+        return pl.ds(pl.multiple_of(m * tokens, tokens), tokens)
+
+    def attention_step(i):
+        p, row = i // rows, i % rows
+        here, cols = row_block(row), pl.ds(pl.multiple_of(p * PAIR, PAIR), PAIR)
+        tables = tuple(
+            t[...] for t in (same_ref, down_ref, up_ref, high_table_ref, low_table_ref)
+        )
+        values = [r[here, cols] for r in (q_ref, k_ref, v_ref, ga_ref, att_ref, den_ref)]
+        parts, feat_sum = back_unit(
+            starts_ref, row, place * tokens, *values, state_ref[row, p], later_ref[row, p], tables
+        )
+        line = (lax.broadcasted_iota(jnp.int32, (8, PAIR), 0) == p).astype(F32)
+        small_ref[:8, 3 * PAIR : 4 * PAIR] += line * (feat_sum / feat_ref[p])
+        for n, piece in enumerate(parts):
+            proj[here, pl.ds(pl.multiple_of((3 * p + n) * PAIR, PAIR), PAIR)] = piece
+            small_ref[:8, n * PAIR : (n + 1) * PAIR] += line * jnp.sum(
+                piece.astype(F32), 0, keepdims=True
+            )
+
+    def norm_step(m):
+        here = row_block(m)
+        one, two, xhat = dot(proj[here, :], qkv_ref[...], 1, 1), grad_second_ref[here, :], xhat_ref[here, :]
+        for n, x in enumerate((one * xhat, two * xhat, one, two)):
+            norm_sum[n : n + 1, :] += jnp.sum(x, 0, keepdims=True)
+        both = one * gain_ref[0:1, :] + two * gain_ref[1:2, :]
+        leaving = inv_ref[here, :] * (
+            both
+            - jnp.mean(both, -1, keepdims=True)
+            - xhat * jnp.mean(both * xhat, -1, keepdims=True)
+        )
+        kept, sent = split_cols(leaving)
+        away_buf[m] = sent.astype(BF)
+        sum_copy(m).start()
+        du_ref[here, :] = kept + dy_ref[here, my_cols].astype(F32)
+
+    def other_work(i):
+        @pl.when(i < units)
+        def _():
+            attention_step(i)
+
+        @pl.when((i >= units) & (i < units + rows))
+        def _():
+            norm_step(i - units)
+
+        @pl.when(i == units + rows)
+        def _():
+            kept, sent = split_cols(norm_sum[...])
+            norm_away[...] = sent
+            norm_copy().start()
+            small_ref[16:24, :] = kept
+
+        late = i - (units + rows + 3)
+
+        @pl.when((late >= 0) & (late < rows))
+        def _():
+            sum_copy(late).wait()
+            du_ref[row_block(late), :] += come_buf[late].astype(F32)
+
+        @pl.when(late == rows)
+        def _():
+            norm_copy().wait()
+            small_ref[16:24, :] += norm_come[...]
+
     def give_copy(t):
         return remote(give.at[t], take.at[t], give_send.at[t], give_recv.at[t], twin)
 
@@ -412,10 +509,8 @@
     some_target = outs[-1].at[mine]
 
     barrier = pltpu.get_barrier_semaphore()
-    for peer in (inner, twin):
-        pl.semaphore_signal(
-            barrier, inc=1, device_id={"ctx": peer}, device_id_type=pl.DeviceIdType.MESH
-        )
+    for peer in ({"ctx": inner}, {"ctx": twin}, {"tp": 1 - tp}):
+        pl.semaphore_signal(barrier, inc=1, device_id=peer, device_id_type=pl.DeviceIdType.MESH)
 
     @pl.when(has_outer)
     def _():
@@ -423,7 +518,10 @@
             barrier, inc=1, device_id={"ctx": outer}, device_id_type=pl.DeviceIdType.MESH
         )
 
-    pl.semaphore_wait(barrier, 2 + has_outer.astype(jnp.int32))
+    pl.semaphore_wait(barrier, 3 + has_outer.astype(jnp.int32))
+    small_ref[...] = jnp.zeros_like(small_ref)
+    small_ref[8:16, :] = small_in_ref[...]
+    norm_sum[...] = jnp.zeros_like(norm_sum)
     lag = jnp.where(middle, 2, LAG)
 
     def one(t, carry):
@@ -453,7 +551,7 @@
 
         @pl.when((tb >= 0) & (tb < count))
         def _():
-            give_copy(tb).wait_recv()
+            give_copy(tb).wait()
             total = work[(t + RING - 1) % RING, mine, :] + take[tb].astype(F32)
 
             @pl.when(has_outer)
@@ -506,12 +604,12 @@
             def _():
                 deliver(tc, some_target)
 
+        other_work(t)
         return carry
 
     lax.fori_loop(0, count + LAG, one, 0)
 
     def drain(t, carry):
-        give_copy(t).wait_send()
         across(t).wait_send()
         final_copy(t, some_target).wait_send()
         final_copy(t, some_target).wait_recv()
@@ -526,36 +624,54 @@
     lax.fori_loop(0, count, drain, 0)
 
 
-def reduce_over_ctx(factors, small):
-    terms = tuple((a.shape[1] // CHUNK, b.shape[1] // PANEL) for a, b in factors)
+def last_call(starts, factors, attention, norms, small):
+    shapes = [(a.shape[1], b.shape[1]) for a, b in factors[:3]]
+    first, qkv = factors[3][0], norms[0]
+    shapes.append((first.shape[1], qkv.shape[1]))
+    terms = tuple((x // CHUNK, y // PANEL) for x, y in shapes)
     count = sum(x * y for x, y in terms) + 1
-    half = CHUNK // 2
-    flat = [x for pair in factors for x in pair] + [small]
-    slots = pltpu.VMEM((count, half, PANEL), BF)
-    sums = pl.pallas_call(
-        partial(reduce_kernel, (count, terms)),
-        in_specs=[pl.BlockSpec(memory_space=pltpu.VMEM)] * len(flat),
-        out_specs=[pl.BlockSpec(memory_space=pl.ANY)] * (len(terms) + 1),
-        out_shape=[shaped((a.shape[1], b.shape[1]), BF) for a, b in factors]
-        + [shaped((CHUNK, PANEL), BF)],
-        scratch_shapes=[pltpu.VMEM((RING, CHUNK, PANEL), F32)]
-        + [slots] * 5
-        + [pltpu.SemaphoreType.DMA((count,))] * 9,
+    total, width = first.shape[0], D // 2
+    rows, tokens = MB * ROWS, total // (MB * ROWS)
+    slots = pltpu.VMEM((count, CHUNK // 2, PANEL), BF)
+    flat = [factors[0][0], factors[0][1], factors[1][0], factors[1][1], factors[2][0], first]
+    flat = flat + list(attention) + list(norms) + [small]
+    dma = pltpu.SemaphoreType.DMA
+    *sums, du = pl.pallas_call(
+        partial(last_kernel, (count, terms)),
+        in_specs=[SMEM] + [IN_VMEM] * len(flat),
+        out_specs=[ANYWHERE] * 5 + [IN_VMEM],
+        out_shape=[shaped(x, BF) for x in shapes]
+        + [shaped((CHUNK, PANEL), BF), shaped((total, width), F32)],
+        scratch_shapes=[
+            pltpu.VMEM((total, qkv.shape[1]), BF),
+            pltpu.VMEM((CHUNK, PANEL), F32),
+            pltpu.VMEM((rows, tokens, width), BF),
+            pltpu.VMEM((rows, tokens, width), BF),
+            pltpu.VMEM((8, D), F32),
+            pltpu.VMEM((8, width), F32),
+            pltpu.VMEM((8, width), F32),
+            dma((rows,)), dma((rows,)), dma((2,)),
+            pltpu.VMEM((RING, CHUNK, PANEL), F32),
+        ]
+        + [slots] * 4
+        + [dma((count,))] * 9,
         compiler_params=pltpu.CompilerParams(
             collective_id=0, has_side_effects=True, vmem_limit_bytes=REDUCE_LIMIT
         ),
         cost_estimate=pl.CostEstimate(
             flops=count * 2 * CHUNK * PANEL * 512, bytes_accessed=40 << 20, transcendentals=0
         ),
-    )(*flat)
-    return [g.astype(F32) for g in sums[:-1]], sums[-1].astype(F32)
-
-
-def fits_reduce(factors):
-    even = lax.axis_size("ctx") % 4 == 0
-    return even and all(
-        a.shape[1] % CHUNK == 0 and b.shape[1] % PANEL == 0 for a, b in factors
-    )
+    )(starts, *flat)
+    return [g.astype(F32) for g in sums[:-1]], sums[-1].astype(F32), du
+
+
+def fits_last(factors, qkv, pairs):
+    sizes = [(a.shape[1], b.shape[1]) for a, b in factors] + [qkv.shape]
+    even = all(x % CHUNK == 0 and y % PANEL == 0 for x, y in sizes)
+    ahead = sum(x // CHUNK * (y // PANEL) for x, y in sizes[:-1])
+    units = MB * ROWS * (pairs + 2) + 8
+    line = lax.axis_size("ctx") % 4 == 0 and lax.axis_size("tp") == 2
+    return even and line and units <= ahead and pairs <= 8
 
 
 def exchange(forward, starts_ref, own_ref, got_ref, bufs, tokens):
@@ -1026,6 +1142,28 @@
             3 * unit,
         )(starts, place_in, q, ga, att, den)
         grad_pre, grad_second, later = feed_backward(starts, state, dy, pre, w_down, w_up)
+        large = ((hidden, dy), (second, grad_pre), (att_low, dy))
+        up_sum = jnp.sum(grad_pre.astype(F32), 0) if want else None
+        out_sum = jnp.sum(own.astype(F32), 0)
+        if want and fits_last(large, w_qkv, pairs):
+            extra = jnp.concatenate([up_sum, out_sum])
+            extra = jnp.pad(extra, (0, 8 * PANEL - extra.size)).reshape(8, PANEL)
+            weights, flat, du = last_call(
+                starts,
+                large + ((first, None),),
+                (q, k, v, ga, att, den, state_in, later, feat) + tables,
+                (w_qkv, grad_second, xhat, inv, gain),
+                extra,
+            )
+            ends = up_sum.size // PANEL
+            little = (
+                flat[:pairs, : 3 * PAIR].reshape(-1),
+                flat[:pairs, 3 * PAIR :].reshape(heads, FEAT),
+                flat[8 + ends : 8 + ends + out_sum.size // PANEL].reshape(-1),
+                flat[8 : 8 + ends].reshape(-1),
+                flat[16:20],
+            )
+            return du, (weights, little)
         grad_proj, sums = call(
             back_kernel,
             pairs,
@@ -1046,8 +1184,6 @@
         )
         if not want:
             return part, None
-
-        large = ((hidden, dy), (second, grad_pre), (att_low, dy), (first, grad_proj))
         norm_sums = jnp.stack(
             [
                 jnp.sum(grad_first * xhat, 0),
@@ -1056,13 +1192,17 @@
                 jnp.sum(grad_second, 0),
             ]
         )
-        small = (
+        norm_sums = lax.psum_scatter(norm_sums, "tp", scatter_dimension=1, tiled=True)
+        little = (
             sums[:, 1:4, :].reshape(pairs * 3 * PAIR),
             sums[:, 0, :].reshape(heads, FEAT),
-            jnp.sum(own.astype(F32), 0),
-            jnp.sum(grad_pre.astype(F32), 0),
-        )
-        return part, (large, norm_sums, small)
+            out_sum,
+            up_sum,
+            norm_sums,
+        )
+        products = tuple(dot(a, b, 0, 0).astype(BF) for a, b in large + ((first, grad_proj),))
+        weights = [g.astype(F32) for g in lax.psum(products, "ctx")]
+        return scatter_tp(part) + own.astype(F32), (weights, lax.psum(little, "ctx"))
 
     mine = section_inputs[0].reshape(total, width)
     mine_full = gather_tp(mine)
@@ -1087,29 +1227,9 @@
     full_grad = next_section(1, part, wide)
     y1, full_grad = lax.optimization_barrier((y1, full_grad))
     own_grad = own_part(full_grad)
-    part, (large, norm_sums, small) = backward(full_grad, own_grad, kept, True)
-    du0 = scatter_tp(part) + own_grad.astype(F32)
-    if lax.axis_size("tp") == 2:
-        me = lax.axis_index("tp")
-        away = lax.dynamic_slice_in_dim(norm_sums, (1 - me) * width, width, 1)
-        norm_sums = lax.dynamic_slice_in_dim(norm_sums, me * width, width, 1)
-        norm_sums = norm_sums + lax.ppermute(away, "tp", [(0, 1), (1, 0)])
-    else:
-        norm_sums = lax.psum_scatter(norm_sums, "tp", scatter_dimension=1, tiled=True)
-    small = small + (norm_sums,)
-    if fits_reduce(large):
-        flat = jnp.concatenate([x.reshape(-1) for x in small])
-        flat = jnp.pad(flat, (0, CHUNK * PANEL - flat.size)).reshape(CHUNK, PANEL)
-        (g_down, g_up, g_dense, g_qkv), flat = reduce_over_ctx(large, flat)
-        flat, summed, begin = flat.reshape(-1), [], 0
-        for x in small:
-            summed.append(flat[begin : begin + x.size].reshape(x.shape))
-            begin += x.size
-    else:
-        products = tuple(dot(a, b, 0, 0).astype(BF) for a, b in large)
-        g_down, g_up, g_dense, g_qkv = (g.astype(F32) for g in lax.psum(products, "ctx"))
-        summed = lax.psum(small, "ctx")
-    g_qkv_bias, g_feat, g_out_bias, g_up_bias, norm_sums = summed
+    du0, (weights, little) = backward(full_grad, own_grad, kept, True)
+    g_down, g_up, g_dense, g_qkv = weights
+    g_qkv_bias, g_feat, g_out_bias, g_up_bias, norm_sums = little
     section_ends = jnp.where(section == 0, du0, y1).reshape(1, MB, ROWS, tokens, width)
     grads = (
         norm_sums[:2], norm_sums[2:], g_qkv, g_qkv_bias, g_feat, g_dense, g_out_bias,

time: 480 us -> 452 us (0.942)
  waiting for transfers between devices: 14.4 us -> 3.05 us
  Pallas kernels: 392 us -> 383 us
    pallas_call x2 -> x1, Pallas kernels: 36.2 us -> 18 us  [backward(): call(back_kernel, pairs, [SMEM, SMEM] + [column(total, PAIR)] * 6 + [stat...]
    pallas_call x1, Pallas kernels: 159 us -> 175 us  [last_call(): pl.pallas_call(partial(last_kernel, (count, terms)), in_specs=[SMEM] + [I...]
    ppermute x2 -> x1, waiting for transfers between devices: 11.3 us -> 0.01 us  [scatter_tp(): lax.ppermute(jnp.where(me == 0, right, left).astype(BF), 'tp', [(0, 1), (...]
    pallas_call x2, Pallas kernels: 56.9 us -> 49.8 us  [hand_over(): pl.pallas_call(partial(hand_over_kernel, sender), in_specs=[IN_VMEM] * 3,...]
    dot_general x2 -> x1, matrix products: 9.18 us -> 4.33 us  [backward(): lax.dot_general(grad_proj, w_qkv, (((1,), (1,)), ((), ())), preferred_ele...]
  transfers between devices with their start and end apart: 4 -> 2, of which waited for: 2 -> 1; matrix products, arithmetic and copies ran while one was open for 3% -> 4% of each run, Pallas kernels for 7% -> 19%
where the time goes in v5:
time: 452 us; the launch traced here: 451 us
  Pallas kernels  383 us (85%)
  other arithmetic  35.8 us (8%)
  matrix products  12.7 us (3%)
  local copies, waits for them, and re-layouts  12.1 us (3%)
    pallas_call x1, Pallas kernels, last_call(): pl.pallas_call(partial(last_kernel, (count, terms)), in_specs=[SMEM] + [I...  175 us
    pallas_call x2, Pallas kernels, feed_backward(): link_call(partial(feed_backward_kernel, total // rows), 2, [SMEM, IN_VMEM...  53.9 us
    pallas_call x2, Pallas kernels, hand_over(): pl.pallas_call(partial(hand_over_kernel, sender), in_specs=[IN_VMEM] * 3,...  49.8 us
    pallas_call x2, Pallas kernels, feed_forward(): link_call(partial(feed_forward_kernel, total // rows), 1, [SMEM, IN_VMEM,...  33.5 us
    pallas_call x2, Pallas kernels, forward(): call(features_kernel, pairs, [SMEM, SMEM, whole((total, D)), column(D, 3...  26 us
    pallas_call x1, Pallas kernels, backward(): call(back_kernel, pairs, [SMEM, SMEM] + [column(total, PAIR)] * 6 + [stat...  18 us
    pallas_call x2, Pallas kernels, forward(): call(attend_kernel, pairs, [SMEM, SMEM] + [column(total, PAIR)] * 3 + [st...  17.2 us
    broadcast_in_dim x4, other arithmetic, local(): return (section_ends,) + tuple((g[None] for g in grads))  15.2 us
  transfers between devices with their start and end apart: 2, of which 1 were waited for; matrix products, arithmetic and copies ran while one was open for 4% of the time, Pallas kernels for 19%

profile of v5, /device:TPU:0, one launch (start us, length us, event | category | flops | bytes accessed | tf_op | source)
XLA Modules:
  0.0 450.8 jit_solution(4827053656567824669)
XLA Ops:
  0.7 3.0 collective-permute-start
  3.7 1.3 reshape_squeeze.11.feat_ref.refs_15_
  5.1 0.8 fusion.49
  5.9 0.8 fusion.48
  7.1 0.7 subtract_convert_fusion
  8.2 0.8 concatenate.37.up_ref.refs_18_
  8.9 0.8 concatenate.36.down_ref.refs_17_
  9.7 0.8 concatenate.35.same_ref.refs_16_
  10.5 1.2 bitcast_convert_fusion.4.base_ref
  11.7 1.1 broadcast_add_fusion.base_ref
  12.9 3.0 collective-permute-done
  15.9 1.5 convert_reduce_fusion.2
  17.9 1.5 convolution_convert_fusion.1.ga_ref
  19.5 1.9 fusion.9
  21.4 13.0 %shard_map.203 = (bf16[512,512]{1,0:T(8,128)(2,1)}, bf16[512,512]{1,0:T(8,128)(2,1)}, bf16[512,512]{1,0:T(8,128)(2,1)}, f32[4,4,72,128]{3,2,1,0:T(8,128)}) custom-call(s32[4,4]{1,0:T(4,128)} %bitcast.68, s32[1,1]{1,0:T(1,128)} %bitcast.1.place_ref, bf16[512,1024]{1,0:T(8,128)(2,1)} %get-tuple-element.117.norm_ref, bf16[1024,1536]{1,0:T(8,128)(2,1)} %bitcast.98, ...), custom_call_target="tpu_custom_call" | custom-call | flops 2013265920 | bytes 8388608 | tf_op jit(solution)/shard_map/pallas_call | solution.py:1109
  34.4 14.7 %shard_map.204 = (f32[512,2048]{1,0:T(8,128)}, bf16[512,2048]{1,0:T(8,128)(2,1)}, f32[512,1024]{1,0:T(8,128)}, f32[4,4,72,128]{3,2,1,0:T(8,128)}) custom-call(s32[4,4]{1,0:T(4,128)} %bitcast.69, f32[4,4,72,128]{3,2,1,0:T(8,128)} %get-tuple-element.46.own_ref, bf16[512,1024]{1,0:T(8,128)(2,1)} %get-tuple-element.116.norm_ref, bf16[1024,2048]{1,0:T(8,128)(2,1)} %bitcast.90, ...), custom_call_target="tpu_custom_call" | custom-call | flops 4294967296 | bytes 16777216 | tf_op jit(solution)/shard_map/pallas_call | solution.py:918
  49.1 8.5 %shard_map.205 = (bf16[512,512]{1,0:T(8,128)(2,1)}, f32[512,512]{1,0:T(8,128)}, f32[512,512]{1,0:T(8,128)}) custom-call(s32[4,4]{1,0:T(4,128)} %bitcast.70, s32[1,1]{1,0:T(1,128)} %bitcast.1.place_ref, bf16[512,512]{1,0:T(8,128)(2,1)} %get-tuple-element.43.q_ref, bf16[512,512]{1,0:T(8,128)(2,1)} %get-tuple-element.44.k_ref, ...), custom_call_target="tpu_custom_call" | custom-call | flops 536870912 | bytes 8388608 | tf_op jit(solution)/shard_map/pallas_call | solution.py:1119
  57.7 3.1 convolution_add_fusion.1.part_ref
  60.7 21.1 %shard_map.206 = bf16[512,1024]{1,0:T(8,128)(2,1)} custom-call(f32[512,1024]{1,0:T(8,128)} %convolution_add_fusion.1.part_ref, f32[512,512]{1,0:T(8,128)} %broadcast_add_fusion.base_ref, bf16[512,1024]{1,0:T(8,128)(2,1)} %copy-done.2), custom_call_target="tpu_custom_call" | custom-call | flops 1048576 | bytes 8388608 | tf_op jit(solution)/shard_map/pallas_call | solution.py:1029
  81.8 1.5 convert_reduce_fusion.1
  83.4 1.6 fusion.10
  85.0 2.7 fusion.2
  87.7 0.9 copy.27.refs_24_
  88.5 13.0 %shard_map.207 = (bf16[512,512]{1,0:T(8,128)(2,1)}, bf16[512,512]{1,0:T(8,128)(2,1)}, bf16[512,512]{1,0:T(8,128)(2,1)}, f32[4,4,72,128]{3,2,1,0:T(8,128)}) custom-call(s32[4,4]{1,0:T(4,128)} %bitcast.71, s32[1,1]{1,0:T(1,128)} %bitcast.1.place_ref, bf16[512,1024]{1,0:T(8,128)(2,1)} %get-tuple-element.114.norm_ref.refs_6_, bf16[1024,1536]{1,0:T(8,128)(2,1)} %bitcast.99, ...), custom_call_target="tpu_custom_call" | custom-call | flops 2013265920 | bytes 8388608 | tf_op jit(solution)/shard_map/pallas_call | solution.py:1109
  101.5 18.8 %shard_map.208 = (f32[512,2048]{1,0:T(8,128)}, bf16[512,2048]{1,0:T(8,128)(2,1)}, f32[512,1024]{1,0:T(8,128)}, f32[4,4,72,128]{3,2,1,0:T(8,128)}) custom-call(s32[4,4]{1,0:T(4,128)} %bitcast.72, f32[4,4,72,128]{3,2,1,0:T(8,128)} %get-tuple-element.50.own_ref, bf16[512,1024]{1,0:T(8,128)(2,1)} %get-tuple-element.115.norm_ref.refs_3_, ...), custom_call_target="tpu_custom_call" | custom-call | flops 4294967296 | bytes 16777216 | tf_op jit(solution)/shard_map/pallas_call | solution.py:918
  120.3 8.6 %shard_map.209 = (bf16[512,512]{1,0:T(8,128)(2,1)}, f32[512,512]{1,0:T(8,128)}, f32[512,512]{1,0:T(8,128)}) custom-call(s32[4,4]{1,0:T(4,128)} %bitcast.73, s32[1,1]{1,0:T(1,128)} %bitcast.1.place_ref, bf16[512,512]{1,0:T(8,128)(2,1)} %get-tuple-element.52.q_ref.refs_7_, bf16[512,512]{1,0:T(8,128)(2,1)} %get-tuple-element.53.k_ref.refs_8_, ...), custom_call_target="tpu_custom_call" | custom-call | flops 536870912 | bytes 8388608 | tf_op jit(solution)/shard_map/pallas_call | solution.py:1119
  128.9 1.8 convolution_add_fusion
  131.4 4.5 shard_map.210.own_ref
  135.9 34.8 %shard_map.211 = (bf16[512,2048]{1,0:T(8,128)(2,1)}, f32[512,1024]{1,0:T(8,128)}, f32[4,4,72,128]{3,2,1,0:T(8,128)}) custom-call(s32[4,4]{1,0:T(4,128)} %bitcast.75, f32[4,4,72,128]{3,2,1,0:T(8,128)} %shard_map.210.own_ref, bf16[512,1024]{1,0:T(8,128)(2,1)} %copy-done.2, f32[512,2048]{1,0:T(8,128)} %get-tuple-element.60.pre_ref, ...), custom_call_target="tpu_custom_call" | custom-call | flops 4294967296 | bytes 16777216 | tf_op jit(solution)/shard_map/pallas_call | solution.py:938
  170.7 18.0 %shard_map.212 = (bf16[512,1536]{1,0:T(8,128)(2,1)}, f32[4,8,128]{2,1,0:T(8,128)}) custom-call(s32[4,4]{1,0:T(4,128)} %bitcast.76, s32[1,1]{1,0:T(1,128)} %bitcast.1.place_ref, bf16[512,512]{1,0:T(8,128)(2,1)} %get-tuple-element.52.q_ref.refs_7_, bf16[512,512]{1,0:T(8,128)(2,1)} %get-tuple-element.53.k_ref.refs_8_, ...), custom_call_target="tpu_custom_call" | custom-call | flops 1342177280 | bytes 8388608 | tf_op jit(solution)/shard_map/pallas_call | solution.py:1167
  188.8 4.3 fusion.41
  193.1 0.8 fusion.47
  193.9 1.9 subtract_multiply_fusion.part_ref
  195.8 28.7 %shard_map.213.grad_ref.refs_2_ = bf16[512,1024]{1,0:T(8,128)(2,1)} custom-call(f32[512,1024]{1,0:T(8,128)} %subtract_multiply_fusion.part_ref, f32[512,512]{1,0:T(8,128)} %bitcast_convert_fusion.4.base_ref, bf16[512,1024]{1,0:T(8,128)(2,1)} %copy-done.2), custom_call_target="tpu_custom_call" | custom-call | flops 1048576 | bytes 8388608 | tf_op jit(solution)/shard_map/pallas_call | solution.py:1029
  224.9 0.9 copy-done.7
  225.8 1.5 convolution_convert_fusion.ga_ref.refs_10_
  227.4 4.5 shard_map.214.own_ref
  231.9 19.1 %shard_map.215 = (bf16[512,2048]{1,0:T(8,128)(2,1)}, f32[512,1024]{1,0:T(8,128)}, f32[4,4,72,128]{3,2,1,0:T(8,128)}) custom-call(s32[4,4]{1,0:T(4,128)} %bitcast.78, f32[4,4,72,128]{3,2,1,0:T(8,128)} %shard_map.214.own_ref, bf16[512,1024]{1,0:T(8,128)(2,1)} %shard_map.213.grad_ref.refs_2_, f32[512,2048]{1,0:T(8,128)} %get-tuple-element.60.pre_ref, ...), custom_call_target="tpu_custom_call" | custom-call | flops 4294967296 | bytes 16777216 | tf_op jit(solution)/shard_map/pallas_call | solution.py:938
  251.0 2.0 convert_reduce_fusion
  253.6 175.3 %shard_map.216 = (bf16[2048,1024]{1,0:T(8,128)(2,1)}, bf16[1024,2048]{1,0:T(8,128)(2,1)}, bf16[512,1024]{1,0:T(8,128)(2,1)}, bf16[1024,1536]{1,0:T(8,128)(2,1)},...) custom-call(s32[4,4]{1,0:T(4,128)} %bitcast.79, bf16[512,2048]{1,0:T(8,128)(2,1)} %get-tuple-element.51.refs_1_, ...), custom_call_target="tpu_custom_call" | custom-call | flops 6576668672 | bytes 41943040 | tf_op jit(solution)/shard_map/pallas_call | solution.py:639
  428.9 1.3 slice.67
  430.8 1.0 convert_element_type.112
  432.4 0.7 broadcast_in_dim_reshape.10
  434.3 2.8 bitcast_convert_fusion.3
  437.1 3.6 bitcast_convert_fusion.2
  440.7 4.4 bitcast_convert_fusion.1
  445.1 4.4 bitcast_convert_fusion
  449.6 1.2 broadcast_select_fusion
  (55 shorter events, 5.6 us)
Async XLA Ops:
  0.6 17.3 %copy-start = (bf16[1,512,1024]{2,1,0:T(8,128)(2,1)S(1)}, bf16[1,512,1024]{2,1,0:T(8,128)(2,1)}, u32[]{:S(2)}) copy-start(bf16[1,512,1024]{2,1,0:T(8,128)(2,1)} %param.19) | copy-start | bytes 3145732
  0.7 9.8 %copy-start.3 = (bf16[1,4,1,128,512]{4,3,2,1,0:T(8,128)(2,1)S(1)}, bf16[1,4,1,128,512]{4,3,2,1,0:T(8,128)(2,1)}, u32[]{:S(2)}) copy-start(bf16[1,4,1,128,512]{4,3,2,1,0:T(8,128)(2,1)} %param.12) | copy-start | bytes 1572868
  0.7 11.1 %copy-start.12 = (f32[1,512]{1,0:T(1,128)S(1)}, f32[1,512]{1,0:T(1,128)}, u32[]{:S(2)}) copy-start(f32[1,512]{1,0:T(1,128)} %param.20) | copy-start | bytes 6148
  0.7 15.2 %collective-permute-start = (bf16[512,512]{1,0:T(8,128)(2,1)}, bf16[512,512]{1,0:T(8,128)(2,1)}, u32[]{:S(2)}, u32[]{:S(2)}) collective-permute-start(bf16[512,512]{1,0:T(8,128)(2,1)} %bitcast.59), channel_id=1, source_target_pairs={{0,1},{1,0},{2,3},{3,2},{4,5},{5,4},{6,7},{7,6},{8,9},{9,8},{10,11... | collective-permute-start | bytes 1572872 | tf_op jit(solution)/shard_map/ppermute | solution.py:1045
  17.5 2.0 copy-start.2
  49.1 8.6 %copy-start.9 = (f32[512,1024]{1,0:T(8,128)S(1)}, f32[512,1024]{1,0:T(8,128)}, u32[]{:S(2)}) copy-start(f32[512,1024]{1,0:T(8,128)} %get-tuple-element.49) | copy-start | bytes 6291460
  81.8 3.2 copy-start.1
  120.3 8.6 %copy-start.10 = (f32[512,1024]{1,0:T(8,128)S(1)}, f32[512,1024]{1,0:T(8,128)}, u32[]{:S(2)}) copy-start(f32[512,1024]{1,0:T(8,128)} %get-tuple-element.57) | copy-start | bytes 6291460
  130.8 93.7 %collective-permute-start.1 = (bf16[512,512]{1,0:T(8,128)(2,1)S(1)}, bf16[512,512]{1,0:T(8,128)(2,1)S(1)}, u32[]{:S(2)}, u32[]{:S(2)}) collective-permute-start(bf16[512,512]{1,0:T(8,128)(2,1)S(1)} %select_convert_fusion), channel_id=1, source_target_pairs={{0,1},{1,0},{2,3},{3,2},{4,5},{5,4},{6,7},{7,6},{8,9},{9,8},{10,11... | collective-permute-start | bytes 1572872 | tf_op jit(solution)/shard_map/ppermute | solution.py:1060
  188.8 4.3 copy-start.8
  224.5 1.2 copy-start.7
  433.1 4.0 copy-start.6
  437.1 3.6 copy-start.5
  440.7 4.5 copy-start.4
  445.1 4.4 copy-start.11

commit v6 on v5

--- a/solution.py
+++ b/solution.py
@@ -18,7 +18,7 @@
 PAIR = 2 * HD
 HELD = HD + 8
 TILE = 256
-HOP = 2
+HOP = 3
 
 BF = jnp.bfloat16
 F32 = jnp.float32
@@ -166,24 +166,23 @@
     base = place_ref[0, 0] * tokens
     low, first, second = lane_masks(tokens)
     feat = feat_ref[0]
+    proj = dot(norm_ref[...], weight_ref[...]) + bias_ref[0]
+    c0, c1, c2 = proj[:, :PAIR], proj[:, PAIR : 2 * PAIR], proj[:, 2 * PAIR :]
+    left = lane_masks(proj.shape[0])[0]
+    v_ref[...] = jnp.where(left, c1, c2).astype(BF)
+    same, down, up = (
+        jnp.concatenate([t[...]] * (MB * ROWS), 0) for t in (same_ref, down_ref, up_ref)
+    )
+    query, key = jnp.where(left, c0, c1), pltpu.roll(jnp.where(left, c2, c0), HD, 1)
+    for x, out_ref in ((query, q_ref), (key, k_ref)):
+        x = rotate(x, same, down, up)
+        arg = split_dot(x, high_ref[...]) + dot(x.astype(BF), low_ref[...])
+        out_ref[...] = (feat * jnp.exp(arg)).astype(BF)
     for row in range(MB * ROWS):
         here = slice(row * tokens, (row + 1) * tokens)
-        proj = dot(norm_ref[here, :], weight_ref[...]) + bias_ref[0]
-        c0, c1, c2 = proj[:, :PAIR], proj[:, PAIR : 2 * PAIR], proj[:, 2 * PAIR :]
-        query = jnp.where(low, c0, c1)
-        key = pltpu.roll(jnp.where(low, c2, c0), HD, 1)
-        value = jnp.where(low, c1, c2).astype(BF)
-        out = []
-        for x in (query, key):
-            x = rotate(x, same_ref[...], down_ref[...], up_ref[...])
-            arg = split_dot(x, high_ref[...]) + dot(x.astype(BF), low_ref[...])
-            out.append((feat * jnp.exp(arg)).astype(BF))
-        q_ref[here, :] = out[0]
-        k_ref[here, :] = out[1]
-        v_ref[here, :] = value
         leaving = leaving_mask(starts_ref, row, base, tokens)
-        key_out = out[1] * leaving.astype(BF)
-        keep_state(state_ref, row, dot(key_out, value, 0, 0), key_out.astype(F32), low)
+        key_out = k_ref[here, :] * leaving.astype(BF)
+        keep_state(state_ref, row, dot(key_out, v_ref[here, :], 0, 0), key_out.astype(F32), low)
 
 
 def attend_kernel(
@@ -354,16 +353,17 @@
 CHUNK = 256
 PANEL = 512
 RING = 4
-LAG = 6
+LATER = (2, 3, 5, 20, 21, 22)
+LAG = 7
 
 
 def last_kernel(plan, *refs):
     count, terms = plan
     (
-        starts_ref, hidden_ref, dy_ref, second_ref, grad_pre_ref, low_ref, first_ref,
+        starts_ref, hidden_ref, dy_ref, second_any, grad_pre_any, low_ref, first_any,
         q_ref, k_ref, v_ref, ga_ref, att_ref, den_ref, state_ref, later_ref, feat_ref,
         same_ref, down_ref, up_ref, high_table_ref, low_table_ref,
-        qkv_ref, grad_second_ref, xhat_ref, inv_ref, gain_ref, small_in_ref,
+        qkv_any, grad_second_any, xhat_any, inv_ref, gain_ref, small_in_ref,
     ) = refs[:27]
     outs, du_ref = refs[27:32], refs[32]
     (
@@ -372,8 +372,18 @@
         work, give, take, outside, inside,
         give_send, give_recv, part_send, outer_recv, inner_recv, total_send,
         final_send, final_recv, own_sem,
+        second_ref, grad_pre_ref, first_ref, qkv_ref, grad_second_ref, xhat_ref, load_sem,
     ) = refs[33:]
     part = give
+    later_loads = [
+        pltpu.make_async_copy(source, buffer, load_sem.at[n])
+        for n, (source, buffer) in enumerate(
+            (
+                (second_any, second_ref), (grad_pre_any, grad_pre_ref), (qkv_any, qkv_ref),
+                (grad_second_any, grad_second_ref), (xhat_any, xhat_ref), (first_any, first_ref),
+            )
+        )
+    ]
     factors = (
         hidden_ref, dy_ref, second_ref, grad_pre_ref, low_ref, dy_ref, first_ref, proj
     )
@@ -519,14 +529,22 @@
         )
 
     pl.semaphore_wait(barrier, 3 + has_outer.astype(jnp.int32))
+    for copy in later_loads:
+        copy.start()
     small_ref[...] = jnp.zeros_like(small_ref)
     small_ref[8:16, :] = small_in_ref[...]
     norm_sum[...] = jnp.zeros_like(norm_sum)
-    lag = jnp.where(middle, 2, LAG)
+    lag = jnp.where(middle, 3, LAG)
 
     def one(t, carry):
         slot = t % RING
         begin = 0
+
+        @pl.when(t == terms[0][0] * terms[0][1] - 1)
+        def _():
+            for copy in later_loads:
+                copy.wait()
+
         for n, (blocks, panels) in enumerate(terms):
             left, right = factors[2 * n], factors[2 * n + 1]
 
@@ -547,12 +565,12 @@
             give[t] = work[slot, theirs, :].astype(BF)
             give_copy(t).start()
 
-        tb = t - 1
+        tb = t - 2
 
         @pl.when((tb >= 0) & (tb < count))
         def _():
             give_copy(tb).wait()
-            total = work[(t + RING - 1) % RING, mine, :] + take[tb].astype(F32)
+            total = work[(t + RING - 2) % RING, mine, :] + take[tb].astype(F32)
 
             @pl.when(has_outer)
             def _():
@@ -638,7 +656,7 @@
     dma = pltpu.SemaphoreType.DMA
     *sums, du = pl.pallas_call(
         partial(last_kernel, (count, terms)),
-        in_specs=[SMEM] + [IN_VMEM] * len(flat),
+        in_specs=[SMEM] + [ANYWHERE if n in LATER else IN_VMEM for n in range(len(flat))],
         out_specs=[ANYWHERE] * 5 + [IN_VMEM],
         out_shape=[shaped(x, BF) for x in shapes]
         + [shaped((CHUNK, PANEL), BF), shaped((total, width), F32)],
@@ -654,7 +672,8 @@
             pltpu.VMEM((RING, CHUNK, PANEL), F32),
         ]
         + [slots] * 4
-        + [dma((count,))] * 9,
+        + [dma((count,))] * 9
+        + [pltpu.VMEM(flat[n].shape, flat[n].dtype) for n in LATER] + [dma((len(LATER),))],
         compiler_params=pltpu.CompilerParams(
             collective_id=0, has_side_effects=True, vmem_limit_bytes=REDUCE_LIMIT
         ),
@@ -797,9 +816,13 @@
     return pl.ds(pl.multiple_of(n * TILE, TILE), TILE)
 
 
-def run_tiles(first_count, first_body, second_count, second_body, link):
+def run_tiles(first_count, first_body, second_count, second_body, loads, link):
     begin, advance, finish, steps = link
+    for _, copy in loads[:-1]:
+        copy(0).start()
     begin()
+    for n, (count, copy) in enumerate(loads):
+        start_all(0 if n == len(loads) - 1 else 1, count, copy)
     both = first_count + second_count
 
     def one(i, carry):
@@ -818,12 +841,12 @@
     finish()
 
 
-def start_all(count, copy):
+def start_all(begin, count, copy):
     def one(n, carry):
         copy(n).start()
         return carry
 
-    lax.fori_loop(0, count, one, 0)
+    lax.fori_loop(begin, count, one, 0)
 
 
 def feed_forward_kernel(
@@ -841,8 +864,7 @@
             down_ref.at[:, tile(n)], down_buf.at[:, tile(n)], down_sem.at[n]
         )
 
-    start_all(ups, up_copy)
-    start_all(downs, down_copy)
+    loads = ((ups, up_copy), (downs, down_copy))
 
     def up(n):
         up_copy(n).wait()
@@ -855,7 +877,8 @@
         down_copy(n).wait()
         mlp_ref[:, tile(n)] = dot(hidden_ref[...], down_buf[:, tile(n)])
 
-    run_tiles(ups, up, downs, down, exchange(True, starts_ref, own_ref, got_ref, bufs, tokens))
+    link = exchange(True, starts_ref, own_ref, got_ref, bufs, tokens)
+    run_tiles(ups, up, downs, down, loads, link)
 
 
 def feed_backward_kernel(
@@ -874,9 +897,7 @@
     def up_copy(n):
         return pltpu.make_async_copy(up_ref.at[tile(n)], up_buf.at[tile(n)], up_sem.at[n])
 
-    start_all(downs, down_copy)
-    start_all(downs, pre_copy)
-    start_all(ups, up_copy)
+    loads = ((downs, down_copy), (downs, pre_copy), (ups, up_copy))
 
     def down(n):
         down_copy(n).wait()
@@ -891,7 +912,8 @@
         up_copy(n).wait()
         grad_norm_ref[:, tile(n)] = dot(grad_pre_ref[...], up_buf[tile(n), :], 1, 1)
 
-    run_tiles(downs, down, ups, up, exchange(False, starts_ref, own_ref, got_ref, bufs, tokens))
+    link = exchange(False, starts_ref, own_ref, got_ref, bufs, tokens)
+    run_tiles(downs, down, ups, up, loads, link)
 
 
 IN_VMEM = pl.BlockSpec(memory_space=pltpu.VMEM)

time: 452 us -> 436 us (0.965)
  Pallas kernels: 383 us -> 367 us
    pallas_call x2, Pallas kernels: 26 us -> 16.1 us  [forward(): call(features_kernel, pairs, [SMEM, SMEM, whole((total, D)), column(D, 3...]
  transfers between devices with their start and end apart: 2 -> 2, of which waited for: 1 -> 1; matrix products, arithmetic and copies ran while one was open for 4% -> 4% of each run, Pallas kernels for 19% -> 20%
where the time goes in v6:
time: 436 us; the launch traced here: 435 us
  Pallas kernels  367 us (84%)
  other arithmetic  35.8 us (8%)
  matrix products  12.7 us (3%)
  local copies, waits for them, and re-layouts  12.1 us (3%)
    pallas_call x1, Pallas kernels, last_call(): pl.pallas_call(partial(last_kernel, (count, terms)), in_specs=[SMEM] + [A...  171 us
    pallas_call x2, Pallas kernels, feed_backward(): link_call(partial(feed_backward_kernel, total // rows), 2, [SMEM, IN_VMEM...  52.7 us
    pallas_call x2, Pallas kernels, hand_over(): pl.pallas_call(partial(hand_over_kernel, sender), in_specs=[IN_VMEM] * 3,...  50.4 us
    pallas_call x2, Pallas kernels, feed_forward(): link_call(partial(feed_forward_kernel, total // rows), 1, [SMEM, IN_VMEM,...  32.8 us
    pallas_call x1, Pallas kernels, backward(): call(back_kernel, pairs, [SMEM, SMEM] + [column(total, PAIR)] * 6 + [stat...  18 us
    pallas_call x2, Pallas kernels, forward(): call(attend_kernel, pairs, [SMEM, SMEM] + [column(total, PAIR)] * 3 + [st...  17.2 us
    pallas_call x2, Pallas kernels, forward(): call(features_kernel, pairs, [SMEM, SMEM, whole((total, D)), column(D, 3...  16.1 us
    broadcast_in_dim x4, other arithmetic, local(): return (section_ends,) + tuple((g[None] for g in grads))  15.2 us
  transfers between devices with their start and end apart: 2, of which 1 were waited for; matrix products, arithmetic and copies ran while one was open for 4% of the time, Pallas kernels for 20%

profile of v6, /device:TPU:0, one launch (start us, length us, event | category | flops | bytes accessed | tf_op | source)
XLA Modules:
  0.0 435.5 jit_solution(4100834561577892305)
XLA Ops:
  0.7 3.0 collective-permute-start
  3.7 1.3 reshape_squeeze.11.feat_ref.refs_15_
  5.1 0.8 fusion.49
  5.9 0.8 fusion.48
  7.1 0.7 subtract_convert_fusion
  8.2 0.8 concatenate.37.up_ref.refs_18_
  8.9 0.8 concatenate.36.down_ref.refs_17_
  9.7 0.8 concatenate.35.same_ref.refs_16_
  10.5 1.2 bitcast_convert_fusion.4.base_ref
  11.7 1.1 broadcast_add_fusion.base_ref
  12.9 3.0 collective-permute-done
  15.9 1.5 convert_reduce_fusion.2
  17.9 1.5 convolution_convert_fusion.1.ga_ref
  19.5 1.9 fusion.9
  21.4 8.1 %shard_map.203 = (bf16[512,512]{1,0:T(8,128)(2,1)}, bf16[512,512]{1,0:T(8,128)(2,1)}, bf16[512,512]{1,0:T(8,128)(2,1)}, f32[4,4,72,128]{3,2,1,0:T(8,128)}) custom-call(s32[4,4]{1,0:T(4,128)} %bitcast.68, s32[1,1]{1,0:T(1,128)} %bitcast.1.place_ref, bf16[512,1024]{1,0:T(8,128)(2,1)} %get-tuple-element.117.norm_ref, bf16[1024,1536]{1,0:T(8,128)(2,1)} %bitcast.98, ...), custom_call_target="tpu_custom_call" | custom-call | flops 2013265920 | bytes 8388608 | tf_op jit(solution)/shard_map/pallas_call | solution.py:1131
  29.5 14.6 %shard_map.204 = (f32[512,2048]{1,0:T(8,128)}, bf16[512,2048]{1,0:T(8,128)(2,1)}, f32[512,1024]{1,0:T(8,128)}, f32[4,4,72,128]{3,2,1,0:T(8,128)}) custom-call(s32[4,4]{1,0:T(4,128)} %bitcast.69, f32[4,4,72,128]{3,2,1,0:T(8,128)} %get-tuple-element.46.own_ref, bf16[512,1024]{1,0:T(8,128)(2,1)} %get-tuple-element.116.norm_ref, bf16[1024,2048]{1,0:T(8,128)(2,1)} %bitcast.90, ...), custom_call_target="tpu_custom_call" | custom-call | flops 4294967296 | bytes 16777216 | tf_op jit(solution)/shard_map/pallas_call | solution.py:940
  44.1 8.5 %shard_map.205 = (bf16[512,512]{1,0:T(8,128)(2,1)}, f32[512,512]{1,0:T(8,128)}, f32[512,512]{1,0:T(8,128)}) custom-call(s32[4,4]{1,0:T(4,128)} %bitcast.70, s32[1,1]{1,0:T(1,128)} %bitcast.1.place_ref, bf16[512,512]{1,0:T(8,128)(2,1)} %get-tuple-element.43.q_ref, bf16[512,512]{1,0:T(8,128)(2,1)} %get-tuple-element.44.k_ref, ...), custom_call_target="tpu_custom_call" | custom-call | flops 536870912 | bytes 8388608 | tf_op jit(solution)/shard_map/pallas_call | solution.py:1141
  52.7 3.1 convolution_add_fusion.1.part_ref
  55.7 21.1 %shard_map.206 = bf16[512,1024]{1,0:T(8,128)(2,1)} custom-call(f32[512,1024]{1,0:T(8,128)} %convolution_add_fusion.1.part_ref, f32[512,512]{1,0:T(8,128)} %broadcast_add_fusion.base_ref, bf16[512,1024]{1,0:T(8,128)(2,1)} %copy-done.2), custom_call_target="tpu_custom_call" | custom-call | flops 1048576 | bytes 8388608 | tf_op jit(solution)/shard_map/pallas_call | solution.py:1051
  76.8 1.5 convert_reduce_fusion.1
  78.4 1.6 fusion.10
  80.0 2.7 fusion.2
  82.7 0.9 copy.27.refs_24_
  83.5 8.1 %shard_map.207 = (bf16[512,512]{1,0:T(8,128)(2,1)}, bf16[512,512]{1,0:T(8,128)(2,1)}, bf16[512,512]{1,0:T(8,128)(2,1)}, f32[4,4,72,128]{3,2,1,0:T(8,128)}) custom-call(s32[4,4]{1,0:T(4,128)} %bitcast.71, s32[1,1]{1,0:T(1,128)} %bitcast.1.place_ref, bf16[512,1024]{1,0:T(8,128)(2,1)} %get-tuple-element.114.norm_ref.refs_6_, bf16[1024,1536]{1,0:T(8,128)(2,1)} %bitcast.99, ...), custom_call_target="tpu_custom_call" | custom-call | flops 2013265920 | bytes 8388608 | tf_op jit(solution)/shard_map/pallas_call | solution.py:1131
  91.6 18.2 %shard_map.208 = (f32[512,2048]{1,0:T(8,128)}, bf16[512,2048]{1,0:T(8,128)(2,1)}, f32[512,1024]{1,0:T(8,128)}, f32[4,4,72,128]{3,2,1,0:T(8,128)}) custom-call(s32[4,4]{1,0:T(4,128)} %bitcast.72, f32[4,4,72,128]{3,2,1,0:T(8,128)} %get-tuple-element.50.own_ref, bf16[512,1024]{1,0:T(8,128)(2,1)} %get-tuple-element.115.norm_ref.refs_3_, ...), custom_call_target="tpu_custom_call" | custom-call | flops 4294967296 | bytes 16777216 | tf_op jit(solution)/shard_map/pallas_call | solution.py:940
  109.8 8.6 %shard_map.209 = (bf16[512,512]{1,0:T(8,128)(2,1)}, f32[512,512]{1,0:T(8,128)}, f32[512,512]{1,0:T(8,128)}) custom-call(s32[4,4]{1,0:T(4,128)} %bitcast.73, s32[1,1]{1,0:T(1,128)} %bitcast.1.place_ref, bf16[512,512]{1,0:T(8,128)(2,1)} %get-tuple-element.52.q_ref.refs_7_, bf16[512,512]{1,0:T(8,128)(2,1)} %get-tuple-element.53.k_ref.refs_8_, ...), custom_call_target="tpu_custom_call" | custom-call | flops 536870912 | bytes 8388608 | tf_op jit(solution)/shard_map/pallas_call | solution.py:1141
  118.5 1.8 convolution_add_fusion
  120.9 4.5 %shard_map.210.own_ref = f32[4,4,72,128]{3,2,1,0:T(8,128)} custom-call(s32[4,4]{1,0:T(4,128)} %bitcast.74, s32[1,1]{1,0:T(1,128)} %bitcast.1.place_ref, bf16[512,512]{1,0:T(8,128)(2,1)} %get-tuple-element.52.q_ref.refs_7_, bf16[512,512]{1,0:T(8,128)(2,1)} %convolution_convert_fusion.1.ga_ref, f32[512,512]{1,0:T(8,128)} %get-tuple-element.58.att_ref.refs_11_, ...), custom_call_target="tpu_custom_call" | custom-call | flops 201326592 | bytes 8388608 | tf_op jit(solution)/shard_map/pallas_call | solution.py:1158
  125.4 33.8 %shard_map.211 = (bf16[512,2048]{1,0:T(8,128)(2,1)}, f32[512,1024]{1,0:T(8,128)}, f32[4,4,72,128]{3,2,1,0:T(8,128)}) custom-call(s32[4,4]{1,0:T(4,128)} %bitcast.75, f32[4,4,72,128]{3,2,1,0:T(8,128)} %shard_map.210.own_ref, bf16[512,1024]{1,0:T(8,128)(2,1)} %copy-done.2, f32[512,2048]{1,0:T(8,128)} %get-tuple-element.60.pre_ref, ...), custom_call_target="tpu_custom_call" | custom-call | flops 4294967296 | bytes 16777216 | tf_op jit(solution)/shard_map/pallas_call | solution.py:960
  159.3 18.0 %shard_map.212 = (bf16[512,1536]{1,0:T(8,128)(2,1)}, f32[4,8,128]{2,1,0:T(8,128)}) custom-call(s32[4,4]{1,0:T(4,128)} %bitcast.76, s32[1,1]{1,0:T(1,128)} %bitcast.1.place_ref, bf16[512,512]{1,0:T(8,128)(2,1)} %get-tuple-element.52.q_ref.refs_7_, bf16[512,512]{1,0:T(8,128)(2,1)} %get-tuple-element.53.k_ref.refs_8_, ...), custom_call_target="tpu_custom_call" | custom-call | flops 1342177280 | bytes 8388608 | tf_op jit(solution)/shard_map/pallas_call | solution.py:1189
  177.3 4.3 fusion.41
  181.7 0.8 fusion.47
  182.5 1.9 subtract_multiply_fusion.part_ref
  184.4 29.3 %shard_map.213.grad_ref.refs_2_ = bf16[512,1024]{1,0:T(8,128)(2,1)} custom-call(f32[512,1024]{1,0:T(8,128)} %subtract_multiply_fusion.part_ref, f32[512,512]{1,0:T(8,128)} %bitcast_convert_fusion.4.base_ref, bf16[512,1024]{1,0:T(8,128)(2,1)} %copy-done.2), custom_call_target="tpu_custom_call" | custom-call | flops 1048576 | bytes 8388608 | tf_op jit(solution)/shard_map/pallas_call | solution.py:1051
  214.0 0.9 copy-done.7
  215.0 1.5 convolution_convert_fusion.ga_ref.refs_10_
  216.6 4.5 %shard_map.214.own_ref = f32[4,4,72,128]{3,2,1,0:T(8,128)} custom-call(s32[4,4]{1,0:T(4,128)} %bitcast.77, s32[1,1]{1,0:T(1,128)} %bitcast.1.place_ref, bf16[512,512]{1,0:T(8,128)(2,1)} %get-tuple-element.52.q_ref.refs_7_, bf16[512,512]{1,0:T(8,128)(2,1)} %convolution_convert_fusion.ga_ref.refs_10_, f32[512,512]{1,0:T(8,128)} %get-tuple-element.58.att_ref.refs_11_, ...), custom_call_target="tpu_custom_call" | custom-call | flops 201326592 | bytes 8388608 | tf_op jit(solution)/shard_map/pallas_call | solution.py:1158
  221.1 18.9 %shard_map.215 = (bf16[512,2048]{1,0:T(8,128)(2,1)}, f32[512,1024]{1,0:T(8,128)}, f32[4,4,72,128]{3,2,1,0:T(8,128)}) custom-call(s32[4,4]{1,0:T(4,128)} %bitcast.78, f32[4,4,72,128]{3,2,1,0:T(8,128)} %shard_map.214.own_ref, bf16[512,1024]{1,0:T(8,128)(2,1)} %shard_map.213.grad_ref.refs_2_, f32[512,2048]{1,0:T(8,128)} %get-tuple-element.60.pre_ref, ...), custom_call_target="tpu_custom_call" | custom-call | flops 4294967296 | bytes 16777216 | tf_op jit(solution)/shard_map/pallas_call | solution.py:960
  240.0 2.0 convert_reduce_fusion
  242.5 171.0 %shard_map.216 = (bf16[2048,1024]{1,0:T(8,128)(2,1)}, bf16[1024,2048]{1,0:T(8,128)(2,1)}, bf16[512,1024]{1,0:T(8,128)(2,1)}, bf16[1024,1536]{1,0:T(8,128)(2,1)},...) custom-call(s32[4,4]{1,0:T(4,128)} %bitcast.79, bf16[512,2048]{1,0:T(8,128)(2,1)} %get-tuple-element.51.refs_1_, ...), custom_call_target="tpu_custom_call" | custom-call | flops 6576668672 | bytes 41943040 | tf_op jit(solution)/shard_map/pallas_call | solution.py:657
  413.6 1.3 slice.67
  415.5 1.0 convert_element_type.112
  417.1 0.7 broadcast_in_dim_reshape.10
  419.0 2.8 bitcast_convert_fusion.3
  421.8 3.6 bitcast_convert_fusion.2
  425.4 4.4 %bitcast_convert_fusion.1 = f32[1,1024,2048]{2,1,0:T(8,128)} fusion(bf16[1024,2048]{1,0:T(8,128)(2,1)S(1)} %copy-done.5), kind=kLoop, calls=%fused_computation.1 | loop fusion | flops 2097152 | bytes 12582912 | tf_op jit(solution)/shard_map/broadcast_in_dim | solution.py:1260
  429.9 4.4 %bitcast_convert_fusion = f32[1,2048,1024]{2,1,0:T(8,128)} fusion(bf16[2048,1024]{1,0:T(8,128)(2,1)S(1)} %copy-done.4), kind=kLoop, calls=%fused_computation | loop fusion | flops 2097152 | bytes 12582912 | tf_op jit(solution)/shard_map/broadcast_in_dim | solution.py:1260
  434.3 1.2 broadcast_select_fusion
  (55 shorter events, 5.6 us)
Async XLA Ops:
  0.6 17.3 %copy-start = (bf16[1,512,1024]{2,1,0:T(8,128)(2,1)S(1)}, bf16[1,512,1024]{2,1,0:T(8,128)(2,1)}, u32[]{:S(2)}) copy-start(bf16[1,512,1024]{2,1,0:T(8,128)(2,1)} %param.19) | copy-start | bytes 3145732
  0.7 9.8 %copy-start.3 = (bf16[1,4,1,128,512]{4,3,2,1,0:T(8,128)(2,1)S(1)}, bf16[1,4,1,128,512]{4,3,2,1,0:T(8,128)(2,1)}, u32[]{:S(2)}) copy-start(bf16[1,4,1,128,512]{4,3,2,1,0:T(8,128)(2,1)} %param.12) | copy-start | bytes 1572868
  0.7 11.1 %copy-start.12 = (f32[1,512]{1,0:T(1,128)S(1)}, f32[1,512]{1,0:T(1,128)}, u32[]{:S(2)}) copy-start(f32[1,512]{1,0:T(1,128)} %param.20) | copy-start | bytes 6148
  0.7 15.2 %collective-permute-start = (bf16[512,512]{1,0:T(8,128)(2,1)}, bf16[512,512]{1,0:T(8,128)(2,1)}, u32[]{:S(2)}, u32[]{:S(2)}) collective-permute-start(bf16[512,512]{1,0:T(8,128)(2,1)} %bitcast.59), channel_id=1, source_target_pairs={{0,1},{1,0},{2,3},{3,2},{4,5},{5,4},{6,7},{7,6},{8,9},{9,8},{10,11... | collective-permute-start | bytes 1572872 | tf_op jit(solution)/shard_map/ppermute | solution.py:1067
  17.5 2.0 copy-start.2
  44.1 8.6 %copy-start.9 = (f32[512,1024]{1,0:T(8,128)S(1)}, f32[512,1024]{1,0:T(8,128)}, u32[]{:S(2)}) copy-start(f32[512,1024]{1,0:T(8,128)} %get-tuple-element.49) | copy-start | bytes 6291460
  76.8 3.2 copy-start.1
  109.8 8.6 %copy-start.10 = (f32[512,1024]{1,0:T(8,128)S(1)}, f32[512,1024]{1,0:T(8,128)}, u32[]{:S(2)}) copy-start(f32[512,1024]{1,0:T(8,128)} %get-tuple-element.57) | copy-start | bytes 6291460
  120.3 93.3 %collective-permute-start.1 = (bf16[512,512]{1,0:T(8,128)(2,1)S(1)}, bf16[512,512]{1,0:T(8,128)(2,1)S(1)}, u32[]{:S(2)}, u32[]{:S(2)}) collective-permute-start(bf16[512,512]{1,0:T(8,128)(2,1)S(1)} %select_convert_fusion), channel_id=1, source_target_pairs={{0,1},{1,0},{2,3},{3,2},{4,5},{5,4},{6,7},{7,6},{8,9},{9,8},{10,11... | collective-permute-start | bytes 1572872 | tf_op jit(solution)/shard_map/ppermute | solution.py:1082
  177.3 4.3 copy-start.8
  213.7 1.2 copy-start.7
  417.8 4.0 copy-start.6
  421.8 3.6 copy-start.5
  425.4 4.5 %copy-start.4 = (bf16[2048,1024]{1,0:T(8,128)(2,1)S(1)}, bf16[2048,1024]{1,0:T(8,128)(2,1)}, u32[]{:S(2)}) copy-start(bf16[2048,1024]{1,0:T(8,128)(2,1)} %get-tuple-element.74) | copy-start | bytes 12582916
  429.9 4.4 %copy-start.11 = (f32[512,512]{1,0:T(8,128)S(1)}, f32[512,512]{1,0:T(8,128)}, u32[]{:S(2)}) copy-start(f32[512,512]{1,0:T(8,128)} %get-tuple-element.68) | copy-start | bytes 3145732

commit v7 on v6

--- a/solution.py
+++ b/solution.py
@@ -353,39 +353,40 @@
 CHUNK = 256
 PANEL = 512
 RING = 4
-LATER = (2, 3, 5, 20, 21, 22)
 LAG = 7
 
 
 def last_kernel(plan, *refs):
     count, terms = plan
     (
-        starts_ref, hidden_ref, dy_ref, second_any, grad_pre_any, low_ref, first_any,
-        q_ref, k_ref, v_ref, ga_ref, att_ref, den_ref, state_ref, later_ref, feat_ref,
+        starts_ref, hidden_ref, dy_ref, low_ref, second_any, first_any,
+        q_ref, k_ref, v_ref, ga_ref, att_ref, den_ref, state_ref, own_ref, feat_ref,
         same_ref, down_ref, up_ref, high_table_ref, low_table_ref,
-        qkv_any, grad_second_any, xhat_any, inv_ref, gain_ref, small_in_ref,
-    ) = refs[:27]
-    outs, du_ref = refs[27:32], refs[32]
+        qkv_any, xhat_any, inv_ref, gain_ref, pre_any, w_down_any, w_up_any, small_in_ref,
+    ) = refs[:28]
+    outs, du_ref = refs[28:33], refs[33]
     (
         proj, small_ref, away_buf, come_buf, norm_sum, norm_away, norm_come,
         sum_send, sum_recv, norm_sem,
         work, give, take, outside, inside,
         give_send, give_recv, part_send, outer_recv, inner_recv, total_send,
         final_send, final_recv, own_sem,
-        second_ref, grad_pre_ref, first_ref, qkv_ref, grad_second_ref, xhat_ref, load_sem,
-    ) = refs[33:]
+        second_ref, first_ref, qkv_ref, xhat_ref, load_sem,
+        grad_pre_ref, grad_second_ref, later_ref, pre_ring, down_ring, up_ring,
+        pre_sem, down_sem, up_sem, *link_bufs,
+    ) = refs[34:]
     part = give
     later_loads = [
         pltpu.make_async_copy(source, buffer, load_sem.at[n])
         for n, (source, buffer) in enumerate(
             (
-                (second_any, second_ref), (grad_pre_any, grad_pre_ref), (qkv_any, qkv_ref),
-                (grad_second_any, grad_second_ref), (xhat_any, xhat_ref), (first_any, first_ref),
+                (second_any, second_ref), (first_any, first_ref), (qkv_any, qkv_ref),
+                (xhat_any, xhat_ref),
             )
         )
     ]
     factors = (
-        hidden_ref, dy_ref, second_ref, grad_pre_ref, low_ref, dy_ref, first_ref, proj
+        hidden_ref, dy_ref, low_ref, dy_ref, second_ref, grad_pre_ref, first_ref, proj
     )
     rows, pairs = state_ref.shape[:2]
     tokens, width = q_ref.shape[0] // rows, du_ref.shape[1]
@@ -428,6 +429,47 @@
     def row_block(m):
         return pl.ds(pl.multiple_of(m * tokens, tokens), tokens)
 
+    downs, ups = w_down_any.shape[0] // TILE, w_up_any.shape[0] // TILE
+    begin_link, advance, finish_link, _ = exchange(
+        False, starts_ref, own_ref, later_ref, link_bufs, tokens, 1, False
+    )
+
+    def down_copies(n):
+        return (
+            pltpu.make_async_copy(w_down_any.at[tile(n)], down_ring.at[n % 2], down_sem.at[n % 2]),
+            pltpu.make_async_copy(pre_any.at[:, tile(n)], pre_ring.at[n % 2], pre_sem.at[n % 2]),
+        )
+
+    def up_copy(n):
+        return pltpu.make_async_copy(w_up_any.at[tile(n)], up_ring.at[n % 2], up_sem.at[n % 2])
+
+    def down_step(n):
+        for copy in down_copies(n):
+            copy.wait()
+        pre = pre_ring[n % 2]
+        grad = dot(dy_ref[...], down_ring[n % 2], 1, 1)
+        cdf = 0.5 * (1.0 + lax.erf(pre * math.sqrt(0.5)))
+        slope = cdf + pre * jnp.exp(-0.5 * pre * pre) * (1.0 / math.sqrt(2.0 * math.pi))
+        grad = (grad * slope).astype(BF)
+        grad_pre_ref[:, tile(n)] = grad
+        per_row = PANEL // TILE
+        line = (lax.broadcasted_iota(jnp.int32, (8, TILE), 0) == n // per_row).astype(F32)
+        cols = pl.ds(pl.multiple_of(n % per_row * TILE, TILE), TILE)
+        small_ref[8:16, cols] += line * jnp.sum(grad.astype(F32), 0, keepdims=True)
+
+        @pl.when(n + 2 < downs)
+        def _():
+            for copy in down_copies(n + 2):
+                copy.start()
+
+    def up_step(n):
+        up_copy(n).wait()
+        grad_second_ref[:, tile(n)] = dot(grad_pre_ref[...], up_ring[n % 2], 1, 1)
+
+        @pl.when(n + 2 < ups)
+        def _():
+            up_copy(n + 2).start()
+
     def attention_step(i):
         p, row = i // rows, i % rows
         here, cols = row_block(row), pl.ds(pl.multiple_of(p * PAIR, PAIR), PAIR)
@@ -462,8 +504,23 @@
         sum_copy(m).start()
         du_ref[here, :] = kept + dy_ref[here, my_cols].astype(F32)
 
-    def other_work(i):
-        @pl.when(i < units)
+    def other_work(step):
+        @pl.when(step < downs)
+        def _():
+            down_step(step)
+
+        @pl.when((step >= downs) & (step < downs + ups))
+        def _():
+            up_step(step - downs)
+
+        advance(step)
+        i = step - downs - ups
+
+        @pl.when(i == 0)
+        def _():
+            finish_link()
+
+        @pl.when((i >= 0) & (i < units))
         def _():
             attention_step(i)
 
@@ -529,6 +586,11 @@
         )
 
     pl.semaphore_wait(barrier, 3 + has_outer.astype(jnp.int32))
+    begin_link()
+    for n in range(2):
+        for copy in down_copies(n):
+            copy.start()
+        up_copy(n).start()
     for copy in later_loads:
         copy.start()
     small_ref[...] = jnp.zeros_like(small_ref)
@@ -540,7 +602,7 @@
         slot = t % RING
         begin = 0
 
-        @pl.when(t == terms[0][0] * terms[0][1] - 1)
+        @pl.when(t == downs)
         def _():
             for copy in later_loads:
                 copy.wait()
@@ -642,21 +704,26 @@
     lax.fori_loop(0, count, drain, 0)
 
 
-def last_call(starts, factors, attention, norms, small):
-    shapes = [(a.shape[1], b.shape[1]) for a, b in factors[:3]]
-    first, qkv = factors[3][0], norms[0]
-    shapes.append((first.shape[1], qkv.shape[1]))
+def last_call(starts, factors, attention, norms, feed, small):
+    second, first = factors[4:]
+    own, qkv = attention[7], norms[0]
+    pre, w_down, w_up = feed
+    total, width = first.shape[0], D // 2
+    rows, tokens = MB * ROWS, total // (MB * ROWS)
+    shapes = [
+        (factors[0].shape[1], D), (factors[3].shape[1], D), (D, pre.shape[1]), (D, qkv.shape[1])
+    ]
     terms = tuple((x // CHUNK, y // PANEL) for x, y in shapes)
     count = sum(x * y for x, y in terms) + 1
-    total, width = first.shape[0], D // 2
-    rows, tokens = MB * ROWS, total // (MB * ROWS)
     slots = pltpu.VMEM((count, CHUNK // 2, PANEL), BF)
-    flat = [factors[0][0], factors[0][1], factors[1][0], factors[1][1], factors[2][0], first]
-    flat = flat + list(attention) + list(norms) + [small]
+    flat = [factors[0], factors[1], factors[3], second, first]
+    flat = flat + list(attention) + list(norms) + list(feed) + [small]
+    later = [n for n, x in enumerate(flat) if any(x is y for y in (second, first, qkv, norms[1]))]
+    outside = later + [n for n, x in enumerate(flat) if any(x is y for y in feed)]
     dma = pltpu.SemaphoreType.DMA
     *sums, du = pl.pallas_call(
         partial(last_kernel, (count, terms)),
-        in_specs=[SMEM] + [ANYWHERE if n in LATER else IN_VMEM for n in range(len(flat))],
+        in_specs=[SMEM] + [ANYWHERE if n in outside else IN_VMEM for n in range(len(flat))],
         out_specs=[ANYWHERE] * 5 + [IN_VMEM],
         out_shape=[shaped(x, BF) for x in shapes]
         + [shaped((CHUNK, PANEL), BF), shaped((total, width), F32)],
@@ -673,7 +740,15 @@
         ]
         + [slots] * 4
         + [dma((count,))] * 9
-        + [pltpu.VMEM(flat[n].shape, flat[n].dtype) for n in LATER] + [dma((len(LATER),))],
+        + [pltpu.VMEM(flat[n].shape, flat[n].dtype) for n in later]
+        + [dma((len(later),))]
+        + [
+            pltpu.VMEM(pre.shape, BF), pltpu.VMEM((total, D), F32), pltpu.VMEM(own.shape, F32),
+            pltpu.VMEM((2, total, TILE), F32), pltpu.VMEM((2, TILE, D), BF),
+            pltpu.VMEM((2, TILE, w_up.shape[1]), BF),
+            dma((2,)), dma((2,)), dma((2,)),
+        ]
+        + exchange_scratch(rows, own.shape[1]),
         compiler_params=pltpu.CompilerParams(
             collective_id=0, has_side_effects=True, vmem_limit_bytes=REDUCE_LIMIT
         ),
@@ -684,16 +759,19 @@
     return [g.astype(F32) for g in sums[:-1]], sums[-1].astype(F32), du
 
 
-def fits_last(factors, qkv, pairs):
-    sizes = [(a.shape[1], b.shape[1]) for a, b in factors] + [qkv.shape]
+def fits_last(units, qkv, pairs):
+    sizes = [(units, D), (pairs * PAIR, D), (D, units), qkv.shape]
     even = all(x % CHUNK == 0 and y % PANEL == 0 for x, y in sizes)
-    ahead = sum(x // CHUNK * (y // PANEL) for x, y in sizes[:-1])
-    units = MB * ROWS * (pairs + 2) + 8
-    line = lax.axis_size("ctx") % 4 == 0 and lax.axis_size("tp") == 2
-    return even and line and units <= ahead and pairs <= 8
-
-
-def exchange(forward, starts_ref, own_ref, got_ref, bufs, tokens):
+    chunks = [x // CHUNK * (y // PANEL) for x, y in sizes]
+    ahead = sum(chunks[:-1])
+    rows, chips = MB * ROWS, lax.axis_size("ctx") // 2
+    feed = units // TILE + D // TILE
+    line = chips % 2 == 0 and lax.axis_size("tp") == 2 and pairs % 2 == 0 and pairs <= 8
+    fits = feed + rows * pairs <= ahead and feed + rows * (pairs + 2) + 3 < sum(chunks)
+    return even and line and fits and chips + 4 <= feed and units < 8 * PANEL
+
+
+def exchange(forward, starts_ref, own_ref, got_ref, bufs, tokens, hop=HOP, greeting=True):
     (twin_buf, in_buf, out_buf, back_buf, twin_sem, send_sem, recv_sem, back_send, back_recv) = bufs
     rows, pairs = own_ref.shape[:2]
     part = rows // 2
@@ -734,6 +812,9 @@
         return (end == count_starts(starts_ref, row, at * tokens - 1)).astype(F32)
 
     def begin():
+        if not greeting:
+            twin_copy().start()
+            return
         barrier = pltpu.get_barrier_semaphore()
 
         def greet(peer):
@@ -755,7 +836,7 @@
         def _():
             twin_copy().wait_recv()
 
-        j = i - HOP * away
+        j = i - hop * away
 
         @pl.when((j >= 0) & (j < chunks))
         def _():
@@ -799,7 +880,7 @@
 
         lax.fori_loop(0, chunks, one, 0)
 
-    return begin, advance, finish, (chips - 1) * HOP + chunks
+    return begin, advance, finish, (chips - 1) * hop + chunks
 
 
 def exchange_scratch(rows, pairs):
@@ -1163,21 +1244,22 @@
             [state_shape],
             3 * unit,
         )(starts, place_in, q, ga, att, den)
-        grad_pre, grad_second, later = feed_backward(starts, state, dy, pre, w_down, w_up)
-        large = ((hidden, dy), (second, grad_pre), (att_low, dy))
-        up_sum = jnp.sum(grad_pre.astype(F32), 0) if want else None
         out_sum = jnp.sum(own.astype(F32), 0)
-        if want and fits_last(large, w_qkv, pairs):
-            extra = jnp.concatenate([up_sum, out_sum])
+        up_size = w_up.shape[1]
+        if want and fits_last(up_size, w_qkv, pairs):
+            extra = jnp.concatenate([jnp.zeros((up_size,), F32), out_sum])
             extra = jnp.pad(extra, (0, 8 * PANEL - extra.size)).reshape(8, PANEL)
             weights, flat, du = last_call(
                 starts,
-                large + ((first, None),),
-                (q, k, v, ga, att, den, state_in, later, feat) + tables,
-                (w_qkv, grad_second, xhat, inv, gain),
+                (hidden, dy, None, att_low, second, first),
+                (q, k, v, ga, att, den, state_in, state, feat) + tables,
+                (w_qkv, xhat, inv, gain),
+                (pre, w_down, w_up),
                 extra,
             )
-            ends = up_sum.size // PANEL
+            g_down, g_dense, g_up, g_qkv = weights
+            weights = (g_down, g_up, g_dense, g_qkv)
+            ends = up_size // PANEL
             little = (
                 flat[:pairs, : 3 * PAIR].reshape(-1),
                 flat[:pairs, 3 * PAIR :].reshape(heads, FEAT),
@@ -1186,6 +1268,9 @@
                 flat[16:20],
             )
             return du, (weights, little)
+        grad_pre, grad_second, later = feed_backward(starts, state, dy, pre, w_down, w_up)
+        large = ((hidden, dy), (second, grad_pre), (att_low, dy))
+        up_sum = jnp.sum(grad_pre.astype(F32), 0) if want else None
         grad_proj, sums = call(
             back_kernel,
             pairs,

time: 436 us -> 429 us (0.984)
    pallas_call x2 -> x1, Pallas kernels: 52.7 us -> 33.8 us  [feed_backward(): link_call(partial(feed_backward_kernel, total // rows), 2, [SMEM, IN_VMEM...]
    pallas_call x1, Pallas kernels: 171 us -> 186 us  [last_call(): pl.pallas_call(partial(last_kernel, (count, terms)), in_specs=[SMEM] + [A...]
where the time goes in v7:
time: 429 us; the launch traced here: 428 us
  Pallas kernels  363 us (85%)
  other arithmetic  33.6 us (8%)
  matrix products  12.7 us (3%)
  local copies, waits for them, and re-layouts  11.2 us (3%)
    pallas_call x1, Pallas kernels, last_call(): pl.pallas_call(partial(last_kernel, (count, terms)), in_specs=[SMEM] + [A...  186 us
    pallas_call x2, Pallas kernels, hand_over(): pl.pallas_call(partial(hand_over_kernel, sender), in_specs=[IN_VMEM] * 3,...  50.3 us
    pallas_call x1, Pallas kernels, feed_backward(): link_call(partial(feed_backward_kernel, total // rows), 2, [SMEM, IN_VMEM...  33.8 us
    pallas_call x2, Pallas kernels, feed_forward(): link_call(partial(feed_forward_kernel, total // rows), 1, [SMEM, IN_VMEM,...  32.8 us
    pallas_call x1, Pallas kernels, backward(): call(back_kernel, pairs, [SMEM, SMEM] + [column(total, PAIR)] * 6 + [stat...  18 us
    pallas_call x2, Pallas kernels, forward(): call(attend_kernel, pairs, [SMEM, SMEM] + [column(total, PAIR)] * 3 + [st...  17.2 us
    pallas_call x2, Pallas kernels, forward(): call(features_kernel, pairs, [SMEM, SMEM, whole((total, D)), column(D, 3...  16.1 us
    broadcast_in_dim x4, other arithmetic, local(): return (section_ends,) + tuple((g[None] for g in grads))  15.3 us
  transfers between devices with their start and end apart: 2, of which 1 were waited for; matrix products, arithmetic and copies ran while one was open for 4% of the time, Pallas kernels for 20%

profile of v7, /device:TPU:0, one launch (start us, length us, event | category | flops | bytes accessed | tf_op | source)
XLA Modules:
  0.0 428.0 jit_solution(4127096222474348651)
XLA Ops:
  0.7 3.0 collective-permute-start
  3.7 1.3 reshape_squeeze.11.feat_ref.refs_14_
  5.1 0.8 fusion.49
  5.9 0.8 fusion.48
  7.1 0.7 subtract_convert_fusion
  8.2 0.8 concatenate.37.up_ref.refs_17_
  8.9 0.8 concatenate.36.down_ref.refs_16_
  9.7 0.8 concatenate.35.same_ref.refs_15_
  10.5 1.2 bitcast_convert_fusion.4.base_ref
  11.7 1.1 broadcast_add_fusion.base_ref
  12.8 3.0 collective-permute-done
  16.6 1.5 convolution_convert_fusion.1.ga_ref
  18.1 1.9 fusion.9
  20.1 8.1 %shard_map.203 = (bf16[512,512]{1,0:T(8,128)(2,1)}, bf16[512,512]{1,0:T(8,128)(2,1)}, bf16[512,512]{1,0:T(8,128)(2,1)}, f32[4,4,72,128]{3,2,1,0:T(8,128)}) custom-call(s32[4,4]{1,0:T(4,128)} %bitcast.73, s32[1,1]{1,0:T(1,128)} %bitcast.1.place_ref, bf16[512,1024]{1,0:T(8,128)(2,1)} %get-tuple-element.111.norm_ref, bf16[1024,1536]{1,0:T(8,128)(2,1)} %bitcast.69, ...), custom_call_target="tpu_custom_call" | custom-call | flops 2013265920 | bytes 8388608 | tf_op jit(solution)/shard_map/pallas_call | solution.py:1212
  28.1 14.6 %shard_map.204 = (f32[512,2048]{1,0:T(8,128)}, bf16[512,2048]{1,0:T(8,128)(2,1)}, f32[512,1024]{1,0:T(8,128)}, f32[4,4,72,128]{3,2,1,0:T(8,128)}) custom-call(s32[4,4]{1,0:T(4,128)} %bitcast.74, f32[4,4,72,128]{3,2,1,0:T(8,128)} %get-tuple-element.43.own_ref, bf16[512,1024]{1,0:T(8,128)(2,1)} %get-tuple-element.110.norm_ref, bf16[1024,2048]{1,0:T(8,128)(2,1)} %bitcast.61, ...), custom_call_target="tpu_custom_call" | custom-call | flops 4294967296 | bytes 16777216 | tf_op jit(solution)/shard_map/pallas_call | solution.py:1021
  42.8 8.5 %shard_map.205 = (bf16[512,512]{1,0:T(8,128)(2,1)}, f32[512,512]{1,0:T(8,128)}, f32[512,512]{1,0:T(8,128)}) custom-call(s32[4,4]{1,0:T(4,128)} %bitcast.75, s32[1,1]{1,0:T(1,128)} %bitcast.1.place_ref, bf16[512,512]{1,0:T(8,128)(2,1)} %get-tuple-element.40.q_ref, bf16[512,512]{1,0:T(8,128)(2,1)} %get-tuple-element.41.k_ref, ...), custom_call_target="tpu_custom_call" | custom-call | flops 536870912 | bytes 8388608 | tf_op jit(solution)/shard_map/pallas_call | solution.py:1222
  51.3 3.1 convolution_add_fusion.1.part_ref
  54.4 21.1 %shard_map.206 = bf16[512,1024]{1,0:T(8,128)(2,1)} custom-call(f32[512,1024]{1,0:T(8,128)} %convolution_add_fusion.1.part_ref, f32[512,512]{1,0:T(8,128)} %broadcast_add_fusion.base_ref, bf16[512,1024]{1,0:T(8,128)(2,1)} %copy-done.2), custom_call_target="tpu_custom_call" | custom-call | flops 1048576 | bytes 8388608 | tf_op jit(solution)/shard_map/pallas_call | solution.py:1132
  75.5 1.5 convert_reduce_fusion
  77.0 1.6 fusion.10
  78.7 2.7 fusion.2
  81.3 0.9 copy.27.refs_22_
  82.2 8.1 %shard_map.207 = (bf16[512,512]{1,0:T(8,128)(2,1)}, bf16[512,512]{1,0:T(8,128)(2,1)}, bf16[512,512]{1,0:T(8,128)(2,1)}, f32[4,4,72,128]{3,2,1,0:T(8,128)}) custom-call(s32[4,4]{1,0:T(4,128)} %bitcast.76, s32[1,1]{1,0:T(1,128)} %bitcast.1.place_ref, bf16[512,1024]{1,0:T(8,128)(2,1)} %get-tuple-element.108.norm_ref.refs_5_, bf16[1024,1536]{1,0:T(8,128)(2,1)} %bitcast.70, ...), custom_call_target="tpu_custom_call" | custom-call | flops 2013265920 | bytes 8388608 | tf_op jit(solution)/shard_map/pallas_call | solution.py:1212
  90.3 18.2 %shard_map.208 = (f32[512,2048]{1,0:T(8,128)}, bf16[512,2048]{1,0:T(8,128)(2,1)}, f32[512,1024]{1,0:T(8,128)}, f32[4,4,72,128]{3,2,1,0:T(8,128)}) custom-call(s32[4,4]{1,0:T(4,128)} %bitcast.77, f32[4,4,72,128]{3,2,1,0:T(8,128)} %get-tuple-element.47.own_ref, bf16[512,1024]{1,0:T(8,128)(2,1)} %get-tuple-element.109.norm_ref.refs_4_, ...), custom_call_target="tpu_custom_call" | custom-call | flops 4294967296 | bytes 16777216 | tf_op jit(solution)/shard_map/pallas_call | solution.py:1021
  108.5 8.6 %shard_map.209 = (bf16[512,512]{1,0:T(8,128)(2,1)}, f32[512,512]{1,0:T(8,128)}, f32[512,512]{1,0:T(8,128)}) custom-call(s32[4,4]{1,0:T(4,128)} %bitcast.78, s32[1,1]{1,0:T(1,128)} %bitcast.1.place_ref, bf16[512,512]{1,0:T(8,128)(2,1)} %get-tuple-element.49.q_ref.refs_6_, bf16[512,512]{1,0:T(8,128)(2,1)} %get-tuple-element.50.k_ref.refs_7_, ...), custom_call_target="tpu_custom_call" | custom-call | flops 536870912 | bytes 8388608 | tf_op jit(solution)/shard_map/pallas_call | solution.py:1222
  117.1 1.8 convolution_add_fusion
  119.0 0.6 collective-permute-start.1
  119.6 4.5 %shard_map.210.own_ref = f32[4,4,72,128]{3,2,1,0:T(8,128)} custom-call(s32[4,4]{1,0:T(4,128)} %bitcast.79, s32[1,1]{1,0:T(1,128)} %bitcast.1.place_ref, bf16[512,512]{1,0:T(8,128)(2,1)} %get-tuple-element.49.q_ref.refs_6_, bf16[512,512]{1,0:T(8,128)(2,1)} %convolution_convert_fusion.1.ga_ref, f32[512,512]{1,0:T(8,128)} %get-tuple-element.55.att_ref.refs_10_, ...), custom_call_target="tpu_custom_call" | custom-call | flops 201326592 | bytes 8388608 | tf_op jit(solution)/shard_map/pallas_call | solution.py:1239
  124.1 33.8 %shard_map.211 = (bf16[512,2048]{1,0:T(8,128)(2,1)}, f32[512,1024]{1,0:T(8,128)}, f32[4,4,72,128]{3,2,1,0:T(8,128)}) custom-call(s32[4,4]{1,0:T(4,128)} %bitcast.80, f32[4,4,72,128]{3,2,1,0:T(8,128)} %shard_map.210.own_ref, bf16[512,1024]{1,0:T(8,128)(2,1)} %copy-done.2, f32[512,2048]{1,0:T(8,128)} %get-tuple-element.57.pre_ref.refs_24_, ...), custom_call_target="tpu_custom_call" | custom-call | flops 4294967296 | bytes 16777216 | tf_op jit(solution)/shard_map/pallas_call | solution.py:1041
  157.9 18.0 %shard_map.212 = (bf16[512,1536]{1,0:T(8,128)(2,1)}, f32[4,8,128]{2,1,0:T(8,128)}) custom-call(s32[4,4]{1,0:T(4,128)} %bitcast.81, s32[1,1]{1,0:T(1,128)} %bitcast.1.place_ref, bf16[512,512]{1,0:T(8,128)(2,1)} %get-tuple-element.49.q_ref.refs_6_, bf16[512,512]{1,0:T(8,128)(2,1)} %get-tuple-element.50.k_ref.refs_7_, ...), custom_call_target="tpu_custom_call" | custom-call | flops 1342177280 | bytes 8388608 | tf_op jit(solution)/shard_map/pallas_call | solution.py:1274
  176.0 4.3 %fusion.41 = f32[512,1024]{1,0:T(8,128)S(1)} fusion(bf16[512,1536]{1,0:T(8,128)(2,1)} %get-tuple-element.59, bf16[1,1024,1536]{2,1,0:T(8,128)(2,1)} %param.16), kind=kOutput, calls=%fused_computation.89 | convolution fusion | flops 1610612736 | bytes 6815744 | tf_op jit(solution)/shard_map/dot_general | solution.py:1283
  180.3 0.8 fusion.47
  181.1 1.9 subtract_multiply_fusion.part_ref
  183.0 29.3 %shard_map.213.refs_2_ = bf16[512,1024]{1,0:T(8,128)(2,1)} custom-call(f32[512,1024]{1,0:T(8,128)} %subtract_multiply_fusion.part_ref, f32[512,512]{1,0:T(8,128)} %bitcast_convert_fusion.4.base_ref, bf16[512,1024]{1,0:T(8,128)(2,1)} %copy-done.2), custom_call_target="tpu_custom_call" | custom-call | flops 1048576 | bytes 8388608 | tf_op jit(solution)/shard_map/pallas_call | solution.py:1132
  212.3 1.3 add_add_fusion
  213.8 1.5 convolution_convert_fusion.ga_ref.refs_9_
  215.9 4.5 %shard_map.214.refs_13_ = f32[4,4,72,128]{3,2,1,0:T(8,128)} custom-call(s32[4,4]{1,0:T(4,128)} %bitcast.82, s32[1,1]{1,0:T(1,128)} %bitcast.1.place_ref, bf16[512,512]{1,0:T(8,128)(2,1)} %get-tuple-element.49.q_ref.refs_6_, bf16[512,512]{1,0:T(8,128)(2,1)} %convolution_convert_fusion.ga_ref.refs_9_, f32[512,512]{1,0:T(8,128)} %get-tuple-element.55.att_ref.refs_10_, ...), custom_call_target="tpu_custom_call" | custom-call | flops 201326592 | bytes 8388608 | tf_op jit(solution)/shard_map/pallas_call | solution.py:1239
  220.4 185.7 %shard_map.215 = (bf16[2048,1024]{1,0:T(8,128)(2,1)}, bf16[512,1024]{1,0:T(8,128)(2,1)}, bf16[1024,2048]{1,0:T(8,128)(2,1)}, bf16[1024,1536]{1,0:T(8,128)(2,1)},...) custom-call(s32[4,4]{1,0:T(4,128)} %bitcast.83, bf16[512,2048]{1,0:T(8,128)(2,1)} %get-tuple-element.48.refs_1_, ...), custom_call_target="tpu_custom_call" | custom-call | flops 6576668672 | bytes 41943040 | tf_op jit(solution)/shard_map/pallas_call | solution.py:724
  406.1 1.3 slice.67
  407.4 0.7 slice.66
  408.1 1.0 convert_element_type.108
  409.7 0.7 broadcast_in_dim_reshape.10
  411.0 0.6 copy.30
  411.6 2.8 bitcast_convert_fusion.3
  414.4 3.6 bitcast_convert_fusion.2
  418.0 4.4 %bitcast_convert_fusion.1 = f32[1,1024,2048]{2,1,0:T(8,128)} fusion(bf16[1024,2048]{1,0:T(8,128)(2,1)S(1)} %copy-done.6), kind=kLoop, calls=%fused_computation.1 | loop fusion | flops 2097152 | bytes 12582912 | tf_op jit(solution)/shard_map/broadcast_in_dim | solution.py:1345
  422.4 4.4 %bitcast_convert_fusion = f32[1,2048,1024]{2,1,0:T(8,128)} fusion(bf16[2048,1024]{1,0:T(8,128)(2,1)S(1)} %copy-done.5), kind=kLoop, calls=%fused_computation | loop fusion | flops 2097152 | bytes 12582912 | tf_op jit(solution)/shard_map/broadcast_in_dim | solution.py:1345
  426.9 1.2 broadcast_select_fusion
  (55 shorter events, 3.7 us)
Async XLA Ops:
  0.6 15.9 %copy-start = (bf16[1,512,1024]{2,1,0:T(8,128)(2,1)S(1)}, bf16[1,512,1024]{2,1,0:T(8,128)(2,1)}, u32[]{:S(2)}) copy-start(bf16[1,512,1024]{2,1,0:T(8,128)(2,1)} %param.19) | copy-start | bytes 3145732
  0.7 9.8 %copy-start.4 = (bf16[1,4,1,128,512]{4,3,2,1,0:T(8,128)(2,1)S(1)}, bf16[1,4,1,128,512]{4,3,2,1,0:T(8,128)(2,1)}, u32[]{:S(2)}) copy-start(bf16[1,4,1,128,512]{4,3,2,1,0:T(8,128)(2,1)} %param.12) | copy-start | bytes 1572868
  0.7 11.0 %copy-start.13 = (f32[1,512]{1,0:T(1,128)S(1)}, f32[1,512]{1,0:T(1,128)}, u32[]{:S(2)}) copy-start(f32[1,512]{1,0:T(1,128)} %param.20) | copy-start | bytes 6148
  0.7 15.1 %collective-permute-start = (bf16[512,512]{1,0:T(8,128)(2,1)}, bf16[512,512]{1,0:T(8,128)(2,1)S(1)}, u32[]{:S(2)}, u32[]{:S(2)}) collective-permute-start(bf16[512,512]{1,0:T(8,128)(2,1)} %bitcast.59), channel_id=1, source_target_pairs={{0,1},{1,0},{2,3},{3,2},{4,5},{5,4},{6,7},{7,6},{8,9},{9,8},{10,11... | collective-permute-start | bytes 1572872 | tf_op jit(solution)/shard_map/ppermute | solution.py:1148
  16.1 2.0 copy-start.2
  42.8 8.6 %copy-start.10 = (f32[512,1024]{1,0:T(8,128)S(1)}, f32[512,1024]{1,0:T(8,128)}, u32[]{:S(2)}) copy-start(f32[512,1024]{1,0:T(8,128)} %get-tuple-element.46) | copy-start | bytes 6291460
  75.5 3.2 copy-start.1
  108.5 8.6 %copy-start.11 = (f32[512,1024]{1,0:T(8,128)S(1)}, f32[512,1024]{1,0:T(8,128)}, u32[]{:S(2)}) copy-start(f32[512,1024]{1,0:T(8,128)} %get-tuple-element.54) | copy-start | bytes 6291460
  119.0 93.3 %collective-permute-start.1 = (bf16[512,512]{1,0:T(8,128)(2,1)S(1)}, bf16[512,512]{1,0:T(8,128)(2,1)S(1)}, u32[]{:S(2)}, u32[]{:S(2)}) collective-permute-start(bf16[512,512]{1,0:T(8,128)(2,1)S(1)} %select_convert_fusion), channel_id=1, source_target_pairs={{0,1},{1,0},{2,3},{3,2},{4,5},{5,4},{6,7},{7,6},{8,9},{9,8},{10,11... | collective-permute-start | bytes 1572872 | tf_op jit(solution)/shard_map/ppermute | solution.py:1163
  176.0 4.3 %copy-start.9 = (f32[512,1024]{1,0:T(8,128)S(1)}, f32[512,1024]{1,0:T(8,128)}, u32[]{:S(2)}) copy-start(f32[512,1024]{1,0:T(8,128)} %get-tuple-element.60) | copy-start | bytes 6291460
  212.3 1.4 copy-start.3
  410.4 4.0 copy-start.8
  414.4 3.6 copy-start.6
  418.0 4.5 %copy-start.5 = (bf16[2048,1024]{1,0:T(8,128)(2,1)S(1)}, bf16[2048,1024]{1,0:T(8,128)(2,1)}, u32[]{:S(2)}) copy-start(bf16[2048,1024]{1,0:T(8,128)(2,1)} %get-tuple-element.68) | copy-start | bytes 12582916
  422.4 4.4 %copy-start.7 = (f32[512,512]{1,0:T(8,128)S(1)}, f32[512,512]{1,0:T(8,128)}, u32[]{:S(2)}) copy-start(f32[512,512]{1,0:T(8,128)} %add_add_fusion) | copy-start | bytes 3145732
  422.4 4.4 %copy-start.12 = (f32[512,512]{1,0:T(8,128)S(1)}, f32[512,512]{1,0:T(8,128)}, u32[]{:S(2)}) copy-start(f32[512,512]{1,0:T(8,128)} %get-tuple-element.62) | copy-start | bytes 3145732

commit v8 on v7

--- a/solution.py
+++ b/solution.py
@@ -353,7 +353,7 @@
 CHUNK = 256
 PANEL = 512
 RING = 4
-LAG = 7
+LAG = 12
 
 
 def last_kernel(plan, *refs):
@@ -596,7 +596,7 @@
     small_ref[...] = jnp.zeros_like(small_ref)
     small_ref[8:16, :] = small_in_ref[...]
     norm_sum[...] = jnp.zeros_like(norm_sum)
-    lag = jnp.where(middle, 3, LAG)
+    lag = jnp.where(middle, 5, LAG)
 
     def one(t, carry):
         slot = t % RING

time: 429 us -> 419 us (0.977)
  Pallas kernels: 363 us -> 352 us
    pallas_call x1, Pallas kernels: 186 us -> 175 us  [last_call(): pl.pallas_call(partial(last_kernel, (count, terms)), in_specs=[SMEM] + [A...]
  transfers between devices with their start and end apart: 2 -> 2, of which waited for: 1 -> 1; matrix products, arithmetic and copies ran while one was open for 4% -> 4% of each run, Pallas kernels for 20% -> 21%
where the time goes in v8:
time: 419 us; the launch traced here: 417 us
  Pallas kernels  352 us (84%)
  other arithmetic  33.6 us (8%)
  matrix products  12.7 us (3%)
  local copies, waits for them, and re-layouts  11.2 us (3%)
    pallas_call x1, Pallas kernels, last_call(): pl.pallas_call(partial(last_kernel, (count, terms)), in_specs=[SMEM] + [A...  175 us
    pallas_call x2, Pallas kernels, hand_over(): pl.pallas_call(partial(hand_over_kernel, sender), in_specs=[IN_VMEM] * 3,...  50.3 us
    pallas_call x1, Pallas kernels, feed_backward(): link_call(partial(feed_backward_kernel, total // rows), 2, [SMEM, IN_VMEM...  33.8 us
    pallas_call x2, Pallas kernels, feed_forward(): link_call(partial(feed_forward_kernel, total // rows), 1, [SMEM, IN_VMEM,...  32.8 us
    pallas_call x1, Pallas kernels, backward(): call(back_kernel, pairs, [SMEM, SMEM] + [column(total, PAIR)] * 6 + [stat...  18 us
    pallas_call x2, Pallas kernels, forward(): call(attend_kernel, pairs, [SMEM, SMEM] + [column(total, PAIR)] * 3 + [st...  17.2 us
    pallas_call x2, Pallas kernels, forward(): call(features_kernel, pairs, [SMEM, SMEM, whole((total, D)), column(D, 3...  16.1 us
    broadcast_in_dim x4, other arithmetic, local(): return (section_ends,) + tuple((g[None] for g in grads))  15.3 us
  transfers between devices with their start and end apart: 2, of which 1 were waited for; matrix products, arithmetic and copies ran while one was open for 4% of the time, Pallas kernels for 21%

profile of v8, /device:TPU:0, one launch (start us, length us, event | category | flops | bytes accessed | tf_op | source)
XLA Modules:
  0.0 417.3 jit_solution(7494682335609427784)
XLA Ops:
  0.7 3.0 collective-permute-start
  3.7 1.3 reshape_squeeze.11.feat_ref.refs_14_
  5.1 0.8 fusion.49
  5.9 0.8 fusion.48
  7.1 0.7 subtract_convert_fusion
  8.2 0.8 concatenate.37.up_ref.refs_17_
  8.9 0.8 concatenate.36.down_ref.refs_16_
  9.7 0.8 concatenate.35.same_ref.refs_15_
  10.5 1.2 bitcast_convert_fusion.4.base_ref
  11.7 1.1 broadcast_add_fusion.base_ref
  12.8 3.0 collective-permute-done
  16.6 1.5 convolution_convert_fusion.1.ga_ref
  18.1 1.9 fusion.9
  20.1 8.1 %shard_map.203 = (bf16[512,512]{1,0:T(8,128)(2,1)}, bf16[512,512]{1,0:T(8,128)(2,1)}, bf16[512,512]{1,0:T(8,128)(2,1)}, f32[4,4,72,128]{3,2,1,0:T(8,128)}) custom-call(s32[4,4]{1,0:T(4,128)} %bitcast.73, s32[1,1]{1,0:T(1,128)} %bitcast.1.place_ref, bf16[512,1024]{1,0:T(8,128)(2,1)} %get-tuple-element.111.norm_ref, bf16[1024,1536]{1,0:T(8,128)(2,1)} %bitcast.69, ...), custom_call_target="tpu_custom_call" | custom-call | flops 2013265920 | bytes 8388608 | tf_op jit(solution)/shard_map/pallas_call | solution.py:1212
  28.1 14.6 %shard_map.204 = (f32[512,2048]{1,0:T(8,128)}, bf16[512,2048]{1,0:T(8,128)(2,1)}, f32[512,1024]{1,0:T(8,128)}, f32[4,4,72,128]{3,2,1,0:T(8,128)}) custom-call(s32[4,4]{1,0:T(4,128)} %bitcast.74, f32[4,4,72,128]{3,2,1,0:T(8,128)} %get-tuple-element.43.own_ref, bf16[512,1024]{1,0:T(8,128)(2,1)} %get-tuple-element.110.norm_ref, bf16[1024,2048]{1,0:T(8,128)(2,1)} %bitcast.61, ...), custom_call_target="tpu_custom_call" | custom-call | flops 4294967296 | bytes 16777216 | tf_op jit(solution)/shard_map/pallas_call | solution.py:1021
  42.8 8.5 %shard_map.205 = (bf16[512,512]{1,0:T(8,128)(2,1)}, f32[512,512]{1,0:T(8,128)}, f32[512,512]{1,0:T(8,128)}) custom-call(s32[4,4]{1,0:T(4,128)} %bitcast.75, s32[1,1]{1,0:T(1,128)} %bitcast.1.place_ref, bf16[512,512]{1,0:T(8,128)(2,1)} %get-tuple-element.40.q_ref, bf16[512,512]{1,0:T(8,128)(2,1)} %get-tuple-element.41.k_ref, ...), custom_call_target="tpu_custom_call" | custom-call | flops 536870912 | bytes 8388608 | tf_op jit(solution)/shard_map/pallas_call | solution.py:1222
  51.3 3.1 convolution_add_fusion.1.part_ref
  54.4 21.1 %shard_map.206 = bf16[512,1024]{1,0:T(8,128)(2,1)} custom-call(f32[512,1024]{1,0:T(8,128)} %convolution_add_fusion.1.part_ref, f32[512,512]{1,0:T(8,128)} %broadcast_add_fusion.base_ref, bf16[512,1024]{1,0:T(8,128)(2,1)} %copy-done.2), custom_call_target="tpu_custom_call" | custom-call | flops 1048576 | bytes 8388608 | tf_op jit(solution)/shard_map/pallas_call | solution.py:1132
  75.5 1.5 convert_reduce_fusion
  77.0 1.6 fusion.10
  78.7 2.7 fusion.2
  81.3 0.9 copy.27.refs_22_
  82.2 8.1 %shard_map.207 = (bf16[512,512]{1,0:T(8,128)(2,1)}, bf16[512,512]{1,0:T(8,128)(2,1)}, bf16[512,512]{1,0:T(8,128)(2,1)}, f32[4,4,72,128]{3,2,1,0:T(8,128)}) custom-call(s32[4,4]{1,0:T(4,128)} %bitcast.76, s32[1,1]{1,0:T(1,128)} %bitcast.1.place_ref, bf16[512,1024]{1,0:T(8,128)(2,1)} %get-tuple-element.108.norm_ref.refs_5_, bf16[1024,1536]{1,0:T(8,128)(2,1)} %bitcast.70, ...), custom_call_target="tpu_custom_call" | custom-call | flops 2013265920 | bytes 8388608 | tf_op jit(solution)/shard_map/pallas_call | solution.py:1212
  90.3 18.2 %shard_map.208 = (f32[512,2048]{1,0:T(8,128)}, bf16[512,2048]{1,0:T(8,128)(2,1)}, f32[512,1024]{1,0:T(8,128)}, f32[4,4,72,128]{3,2,1,0:T(8,128)}) custom-call(s32[4,4]{1,0:T(4,128)} %bitcast.77, f32[4,4,72,128]{3,2,1,0:T(8,128)} %get-tuple-element.47.own_ref, bf16[512,1024]{1,0:T(8,128)(2,1)} %get-tuple-element.109.norm_ref.refs_4_, ...), custom_call_target="tpu_custom_call" | custom-call | flops 4294967296 | bytes 16777216 | tf_op jit(solution)/shard_map/pallas_call | solution.py:1021
  108.5 8.6 %shard_map.209 = (bf16[512,512]{1,0:T(8,128)(2,1)}, f32[512,512]{1,0:T(8,128)}, f32[512,512]{1,0:T(8,128)}) custom-call(s32[4,4]{1,0:T(4,128)} %bitcast.78, s32[1,1]{1,0:T(1,128)} %bitcast.1.place_ref, bf16[512,512]{1,0:T(8,128)(2,1)} %get-tuple-element.49.q_ref.refs_6_, bf16[512,512]{1,0:T(8,128)(2,1)} %get-tuple-element.50.k_ref.refs_7_, ...), custom_call_target="tpu_custom_call" | custom-call | flops 536870912 | bytes 8388608 | tf_op jit(solution)/shard_map/pallas_call | solution.py:1222
  117.1 1.8 convolution_add_fusion
  119.0 0.6 collective-permute-start.1
  119.6 4.5 %shard_map.210.own_ref = f32[4,4,72,128]{3,2,1,0:T(8,128)} custom-call(s32[4,4]{1,0:T(4,128)} %bitcast.79, s32[1,1]{1,0:T(1,128)} %bitcast.1.place_ref, bf16[512,512]{1,0:T(8,128)(2,1)} %get-tuple-element.49.q_ref.refs_6_, bf16[512,512]{1,0:T(8,128)(2,1)} %convolution_convert_fusion.1.ga_ref, f32[512,512]{1,0:T(8,128)} %get-tuple-element.55.att_ref.refs_10_, ...), custom_call_target="tpu_custom_call" | custom-call | flops 201326592 | bytes 8388608 | tf_op jit(solution)/shard_map/pallas_call | solution.py:1239
  124.1 33.8 %shard_map.211 = (bf16[512,2048]{1,0:T(8,128)(2,1)}, f32[512,1024]{1,0:T(8,128)}, f32[4,4,72,128]{3,2,1,0:T(8,128)}) custom-call(s32[4,4]{1,0:T(4,128)} %bitcast.80, f32[4,4,72,128]{3,2,1,0:T(8,128)} %shard_map.210.own_ref, bf16[512,1024]{1,0:T(8,128)(2,1)} %copy-done.2, f32[512,2048]{1,0:T(8,128)} %get-tuple-element.57.pre_ref.refs_24_, ...), custom_call_target="tpu_custom_call" | custom-call | flops 4294967296 | bytes 16777216 | tf_op jit(solution)/shard_map/pallas_call | solution.py:1041
  157.9 18.0 %shard_map.212 = (bf16[512,1536]{1,0:T(8,128)(2,1)}, f32[4,8,128]{2,1,0:T(8,128)}) custom-call(s32[4,4]{1,0:T(4,128)} %bitcast.81, s32[1,1]{1,0:T(1,128)} %bitcast.1.place_ref, bf16[512,512]{1,0:T(8,128)(2,1)} %get-tuple-element.49.q_ref.refs_6_, bf16[512,512]{1,0:T(8,128)(2,1)} %get-tuple-element.50.k_ref.refs_7_, ...), custom_call_target="tpu_custom_call" | custom-call | flops 1342177280 | bytes 8388608 | tf_op jit(solution)/shard_map/pallas_call | solution.py:1274
  176.0 4.3 %fusion.41 = f32[512,1024]{1,0:T(8,128)S(1)} fusion(bf16[512,1536]{1,0:T(8,128)(2,1)} %get-tuple-element.59, bf16[1,1024,1536]{2,1,0:T(8,128)(2,1)} %param.16), kind=kOutput, calls=%fused_computation.89 | convolution fusion | flops 1610612736 | bytes 6815744 | tf_op jit(solution)/shard_map/dot_general | solution.py:1283
  180.3 0.8 fusion.47
  181.1 1.9 subtract_multiply_fusion.part_ref
  183.0 29.3 %shard_map.213.refs_2_ = bf16[512,1024]{1,0:T(8,128)(2,1)} custom-call(f32[512,1024]{1,0:T(8,128)} %subtract_multiply_fusion.part_ref, f32[512,512]{1,0:T(8,128)} %bitcast_convert_fusion.4.base_ref, bf16[512,1024]{1,0:T(8,128)(2,1)} %copy-done.2), custom_call_target="tpu_custom_call" | custom-call | flops 1048576 | bytes 8388608 | tf_op jit(solution)/shard_map/pallas_call | solution.py:1132
  212.3 1.3 add_add_fusion
  213.8 1.5 convolution_convert_fusion.ga_ref.refs_9_
  215.9 4.5 %shard_map.214.refs_13_ = f32[4,4,72,128]{3,2,1,0:T(8,128)} custom-call(s32[4,4]{1,0:T(4,128)} %bitcast.82, s32[1,1]{1,0:T(1,128)} %bitcast.1.place_ref, bf16[512,512]{1,0:T(8,128)(2,1)} %get-tuple-element.49.q_ref.refs_6_, bf16[512,512]{1,0:T(8,128)(2,1)} %convolution_convert_fusion.ga_ref.refs_9_, f32[512,512]{1,0:T(8,128)} %get-tuple-element.55.att_ref.refs_10_, ...), custom_call_target="tpu_custom_call" | custom-call | flops 201326592 | bytes 8388608 | tf_op jit(solution)/shard_map/pallas_call | solution.py:1239
  220.4 174.9 %shard_map.215 = (bf16[2048,1024]{1,0:T(8,128)(2,1)}, bf16[512,1024]{1,0:T(8,128)(2,1)}, bf16[1024,2048]{1,0:T(8,128)(2,1)}, bf16[1024,1536]{1,0:T(8,128)(2,1)},...) custom-call(s32[4,4]{1,0:T(4,128)} %bitcast.83, bf16[512,2048]{1,0:T(8,128)(2,1)} %get-tuple-element.48.refs_1_, ...), custom_call_target="tpu_custom_call" | custom-call | flops 6576668672 | bytes 41943040 | tf_op jit(solution)/shard_map/pallas_call | solution.py:724
  395.3 1.3 slice.67
  396.6 0.7 slice.66
  397.3 1.0 convert_element_type.108
  398.9 0.7 broadcast_in_dim_reshape.10
  400.2 0.6 copy.30
  400.8 2.8 bitcast_convert_fusion.3
  403.6 3.6 bitcast_convert_fusion.2
  407.2 4.4 %bitcast_convert_fusion.1 = f32[1,1024,2048]{2,1,0:T(8,128)} fusion(bf16[1024,2048]{1,0:T(8,128)(2,1)S(1)} %copy-done.6), kind=kLoop, calls=%fused_computation.1 | loop fusion | flops 2097152 | bytes 12582912 | tf_op jit(solution)/shard_map/broadcast_in_dim | solution.py:1345
  411.6 4.4 %bitcast_convert_fusion = f32[1,2048,1024]{2,1,0:T(8,128)} fusion(bf16[2048,1024]{1,0:T(8,128)(2,1)S(1)} %copy-done.5), kind=kLoop, calls=%fused_computation | loop fusion | flops 2097152 | bytes 12582912 | tf_op jit(solution)/shard_map/broadcast_in_dim | solution.py:1345
  416.1 1.2 broadcast_select_fusion
  (55 shorter events, 3.7 us)
Async XLA Ops:
  0.6 15.9 %copy-start = (bf16[1,512,1024]{2,1,0:T(8,128)(2,1)S(1)}, bf16[1,512,1024]{2,1,0:T(8,128)(2,1)}, u32[]{:S(2)}) copy-start(bf16[1,512,1024]{2,1,0:T(8,128)(2,1)} %param.19) | copy-start | bytes 3145732
  0.7 9.8 %copy-start.4 = (bf16[1,4,1,128,512]{4,3,2,1,0:T(8,128)(2,1)S(1)}, bf16[1,4,1,128,512]{4,3,2,1,0:T(8,128)(2,1)}, u32[]{:S(2)}) copy-start(bf16[1,4,1,128,512]{4,3,2,1,0:T(8,128)(2,1)} %param.12) | copy-start | bytes 1572868
  0.7 11.0 %copy-start.13 = (f32[1,512]{1,0:T(1,128)S(1)}, f32[1,512]{1,0:T(1,128)}, u32[]{:S(2)}) copy-start(f32[1,512]{1,0:T(1,128)} %param.20) | copy-start | bytes 6148
  0.7 15.1 %collective-permute-start = (bf16[512,512]{1,0:T(8,128)(2,1)}, bf16[512,512]{1,0:T(8,128)(2,1)S(1)}, u32[]{:S(2)}, u32[]{:S(2)}) collective-permute-start(bf16[512,512]{1,0:T(8,128)(2,1)} %bitcast.59), channel_id=1, source_target_pairs={{0,1},{1,0},{2,3},{3,2},{4,5},{5,4},{6,7},{7,6},{8,9},{9,8},{10,11... | collective-permute-start | bytes 1572872 | tf_op jit(solution)/shard_map/ppermute | solution.py:1148
  16.1 2.0 copy-start.2
  42.8 8.6 %copy-start.10 = (f32[512,1024]{1,0:T(8,128)S(1)}, f32[512,1024]{1,0:T(8,128)}, u32[]{:S(2)}) copy-start(f32[512,1024]{1,0:T(8,128)} %get-tuple-element.46) | copy-start | bytes 6291460
  75.5 3.2 copy-start.1
  108.5 8.6 %copy-start.11 = (f32[512,1024]{1,0:T(8,128)S(1)}, f32[512,1024]{1,0:T(8,128)}, u32[]{:S(2)}) copy-start(f32[512,1024]{1,0:T(8,128)} %get-tuple-element.54) | copy-start | bytes 6291460
  119.0 93.3 %collective-permute-start.1 = (bf16[512,512]{1,0:T(8,128)(2,1)S(1)}, bf16[512,512]{1,0:T(8,128)(2,1)S(1)}, u32[]{:S(2)}, u32[]{:S(2)}) collective-permute-start(bf16[512,512]{1,0:T(8,128)(2,1)S(1)} %select_convert_fusion), channel_id=1, source_target_pairs={{0,1},{1,0},{2,3},{3,2},{4,5},{5,4},{6,7},{7,6},{8,9},{9,8},{10,11... | collective-permute-start | bytes 1572872 | tf_op jit(solution)/shard_map/ppermute | solution.py:1163
  176.0 4.3 %copy-start.9 = (f32[512,1024]{1,0:T(8,128)S(1)}, f32[512,1024]{1,0:T(8,128)}, u32[]{:S(2)}) copy-start(f32[512,1024]{1,0:T(8,128)} %get-tuple-element.60) | copy-start | bytes 6291460
  212.3 1.4 copy-start.3
  399.6 4.0 copy-start.8
  403.6 3.6 copy-start.6
  407.2 4.5 %copy-start.5 = (bf16[2048,1024]{1,0:T(8,128)(2,1)S(1)}, bf16[2048,1024]{1,0:T(8,128)(2,1)}, u32[]{:S(2)}) copy-start(bf16[2048,1024]{1,0:T(8,128)(2,1)} %get-tuple-element.68) | copy-start | bytes 12582916
  411.6 4.4 %copy-start.7 = (f32[512,512]{1,0:T(8,128)S(1)}, f32[512,512]{1,0:T(8,128)}, u32[]{:S(2)}) copy-start(f32[512,512]{1,0:T(8,128)} %add_add_fusion) | copy-start | bytes 3145732
  411.6 4.4 %copy-start.12 = (f32[512,512]{1,0:T(8,128)S(1)}, f32[512,512]{1,0:T(8,128)}, u32[]{:S(2)}) copy-start(f32[512,512]{1,0:T(8,128)} %get-tuple-element.62) | copy-start | bytes 3145732

commit v9 on v8

--- a/solution.py
+++ b/solution.py
@@ -353,7 +353,7 @@
 CHUNK = 256
 PANEL = 512
 RING = 4
-LAG = 12
+LAG = 10
 
 
 def last_kernel(plan, *refs):
@@ -596,7 +596,7 @@
     small_ref[...] = jnp.zeros_like(small_ref)
     small_ref[8:16, :] = small_in_ref[...]
     norm_sum[...] = jnp.zeros_like(norm_sum)
-    lag = jnp.where(middle, 5, LAG)
+    lag = jnp.where(middle, 4, LAG)
 
     def one(t, carry):
         slot = t % RING

time: 419 us -> 417 us (level)
  no operation moved by 1% of the time
where the time goes in v9:
time: 417 us; the launch traced here: 415 us
  Pallas kernels  350 us (84%)
  other arithmetic  33.6 us (8%)
  matrix products  12.7 us (3%)
  local copies, waits for them, and re-layouts  11.2 us (3%)
    pallas_call x1, Pallas kernels, last_call(): pl.pallas_call(partial(last_kernel, (count, terms)), in_specs=[SMEM] + [A...  173 us
    pallas_call x2, Pallas kernels, hand_over(): pl.pallas_call(partial(hand_over_kernel, sender), in_specs=[IN_VMEM] * 3,...  50.3 us
    pallas_call x1, Pallas kernels, feed_backward(): link_call(partial(feed_backward_kernel, total // rows), 2, [SMEM, IN_VMEM...  33.8 us
    pallas_call x2, Pallas kernels, feed_forward(): link_call(partial(feed_forward_kernel, total // rows), 1, [SMEM, IN_VMEM,...  32.8 us
    pallas_call x1, Pallas kernels, backward(): call(back_kernel, pairs, [SMEM, SMEM] + [column(total, PAIR)] * 6 + [stat...  18 us
    pallas_call x2, Pallas kernels, forward(): call(attend_kernel, pairs, [SMEM, SMEM] + [column(total, PAIR)] * 3 + [st...  17.2 us
    pallas_call x2, Pallas kernels, forward(): call(features_kernel, pairs, [SMEM, SMEM, whole((total, D)), column(D, 3...  16.1 us
    broadcast_in_dim x4, other arithmetic, local(): return (section_ends,) + tuple((g[None] for g in grads))  15.3 us
  transfers between devices with their start and end apart: 2, of which 1 were waited for; matrix products, arithmetic and copies ran while one was open for 4% of the time, Pallas kernels for 21%

profile of v9, /device:TPU:0, one launch (start us, length us, event | category | flops | bytes accessed | tf_op | source)
XLA Modules:
  0.0 415.1 jit_solution(10726925935558605900)
XLA Ops:
  0.7 3.0 collective-permute-start
  3.7 1.3 reshape_squeeze.11.feat_ref.refs_14_
  5.1 0.8 fusion.49
  5.9 0.8 fusion.48
  7.1 0.7 subtract_convert_fusion
  8.2 0.8 concatenate.37.up_ref.refs_17_
  8.9 0.8 concatenate.36.down_ref.refs_16_
  9.7 0.8 concatenate.35.same_ref.refs_15_
  10.5 1.2 bitcast_convert_fusion.4.base_ref
  11.7 1.1 broadcast_add_fusion.base_ref
  12.8 3.0 collective-permute-done
  16.6 1.5 convolution_convert_fusion.1.ga_ref
  18.1 1.9 fusion.9
  20.1 8.1 %shard_map.203 = (bf16[512,512]{1,0:T(8,128)(2,1)}, bf16[512,512]{1,0:T(8,128)(2,1)}, bf16[512,512]{1,0:T(8,128)(2,1)}, f32[4,4,72,128]{3,2,1,0:T(8,128)}) custom-call(s32[4,4]{1,0:T(4,128)} %bitcast.73, s32[1,1]{1,0:T(1,128)} %bitcast.1.place_ref, bf16[512,1024]{1,0:T(8,128)(2,1)} %get-tuple-element.111.norm_ref, bf16[1024,1536]{1,0:T(8,128)(2,1)} %bitcast.69, ...), custom_call_target="tpu_custom_call" | custom-call | flops 2013265920 | bytes 8388608 | tf_op jit(solution)/shard_map/pallas_call | solution.py:1212
  28.1 14.6 %shard_map.204 = (f32[512,2048]{1,0:T(8,128)}, bf16[512,2048]{1,0:T(8,128)(2,1)}, f32[512,1024]{1,0:T(8,128)}, f32[4,4,72,128]{3,2,1,0:T(8,128)}) custom-call(s32[4,4]{1,0:T(4,128)} %bitcast.74, f32[4,4,72,128]{3,2,1,0:T(8,128)} %get-tuple-element.43.own_ref, bf16[512,1024]{1,0:T(8,128)(2,1)} %get-tuple-element.110.norm_ref, bf16[1024,2048]{1,0:T(8,128)(2,1)} %bitcast.61, ...), custom_call_target="tpu_custom_call" | custom-call | flops 4294967296 | bytes 16777216 | tf_op jit(solution)/shard_map/pallas_call | solution.py:1021
  42.8 8.5 %shard_map.205 = (bf16[512,512]{1,0:T(8,128)(2,1)}, f32[512,512]{1,0:T(8,128)}, f32[512,512]{1,0:T(8,128)}) custom-call(s32[4,4]{1,0:T(4,128)} %bitcast.75, s32[1,1]{1,0:T(1,128)} %bitcast.1.place_ref, bf16[512,512]{1,0:T(8,128)(2,1)} %get-tuple-element.40.q_ref, bf16[512,512]{1,0:T(8,128)(2,1)} %get-tuple-element.41.k_ref, ...), custom_call_target="tpu_custom_call" | custom-call | flops 536870912 | bytes 8388608 | tf_op jit(solution)/shard_map/pallas_call | solution.py:1222
  51.3 3.1 convolution_add_fusion.1.part_ref
  54.4 21.1 %shard_map.206 = bf16[512,1024]{1,0:T(8,128)(2,1)} custom-call(f32[512,1024]{1,0:T(8,128)} %convolution_add_fusion.1.part_ref, f32[512,512]{1,0:T(8,128)} %broadcast_add_fusion.base_ref, bf16[512,1024]{1,0:T(8,128)(2,1)} %copy-done.2), custom_call_target="tpu_custom_call" | custom-call | flops 1048576 | bytes 8388608 | tf_op jit(solution)/shard_map/pallas_call | solution.py:1132
  75.5 1.5 convert_reduce_fusion
  77.0 1.6 fusion.10
  78.7 2.7 fusion.2
  81.3 0.9 copy.27.refs_22_
  82.2 8.1 %shard_map.207 = (bf16[512,512]{1,0:T(8,128)(2,1)}, bf16[512,512]{1,0:T(8,128)(2,1)}, bf16[512,512]{1,0:T(8,128)(2,1)}, f32[4,4,72,128]{3,2,1,0:T(8,128)}) custom-call(s32[4,4]{1,0:T(4,128)} %bitcast.76, s32[1,1]{1,0:T(1,128)} %bitcast.1.place_ref, bf16[512,1024]{1,0:T(8,128)(2,1)} %get-tuple-element.108.norm_ref.refs_5_, bf16[1024,1536]{1,0:T(8,128)(2,1)} %bitcast.70, ...), custom_call_target="tpu_custom_call" | custom-call | flops 2013265920 | bytes 8388608 | tf_op jit(solution)/shard_map/pallas_call | solution.py:1212
  90.3 18.2 %shard_map.208 = (f32[512,2048]{1,0:T(8,128)}, bf16[512,2048]{1,0:T(8,128)(2,1)}, f32[512,1024]{1,0:T(8,128)}, f32[4,4,72,128]{3,2,1,0:T(8,128)}) custom-call(s32[4,4]{1,0:T(4,128)} %bitcast.77, f32[4,4,72,128]{3,2,1,0:T(8,128)} %get-tuple-element.47.own_ref, bf16[512,1024]{1,0:T(8,128)(2,1)} %get-tuple-element.109.norm_ref.refs_4_, ...), custom_call_target="tpu_custom_call" | custom-call | flops 4294967296 | bytes 16777216 | tf_op jit(solution)/shard_map/pallas_call | solution.py:1021
  108.5 8.6 %shard_map.209 = (bf16[512,512]{1,0:T(8,128)(2,1)}, f32[512,512]{1,0:T(8,128)}, f32[512,512]{1,0:T(8,128)}) custom-call(s32[4,4]{1,0:T(4,128)} %bitcast.78, s32[1,1]{1,0:T(1,128)} %bitcast.1.place_ref, bf16[512,512]{1,0:T(8,128)(2,1)} %get-tuple-element.49.q_ref.refs_6_, bf16[512,512]{1,0:T(8,128)(2,1)} %get-tuple-element.50.k_ref.refs_7_, ...), custom_call_target="tpu_custom_call" | custom-call | flops 536870912 | bytes 8388608 | tf_op jit(solution)/shard_map/pallas_call | solution.py:1222
  117.1 1.8 convolution_add_fusion
  119.0 0.6 collective-permute-start.1
  119.6 4.5 %shard_map.210.own_ref = f32[4,4,72,128]{3,2,1,0:T(8,128)} custom-call(s32[4,4]{1,0:T(4,128)} %bitcast.79, s32[1,1]{1,0:T(1,128)} %bitcast.1.place_ref, bf16[512,512]{1,0:T(8,128)(2,1)} %get-tuple-element.49.q_ref.refs_6_, bf16[512,512]{1,0:T(8,128)(2,1)} %convolution_convert_fusion.1.ga_ref, f32[512,512]{1,0:T(8,128)} %get-tuple-element.55.att_ref.refs_10_, ...), custom_call_target="tpu_custom_call" | custom-call | flops 201326592 | bytes 8388608 | tf_op jit(solution)/shard_map/pallas_call | solution.py:1239
  124.1 33.8 %shard_map.211 = (bf16[512,2048]{1,0:T(8,128)(2,1)}, f32[512,1024]{1,0:T(8,128)}, f32[4,4,72,128]{3,2,1,0:T(8,128)}) custom-call(s32[4,4]{1,0:T(4,128)} %bitcast.80, f32[4,4,72,128]{3,2,1,0:T(8,128)} %shard_map.210.own_ref, bf16[512,1024]{1,0:T(8,128)(2,1)} %copy-done.2, f32[512,2048]{1,0:T(8,128)} %get-tuple-element.57.pre_ref.refs_24_, ...), custom_call_target="tpu_custom_call" | custom-call | flops 4294967296 | bytes 16777216 | tf_op jit(solution)/shard_map/pallas_call | solution.py:1041
  157.9 18.0 %shard_map.212 = (bf16[512,1536]{1,0:T(8,128)(2,1)}, f32[4,8,128]{2,1,0:T(8,128)}) custom-call(s32[4,4]{1,0:T(4,128)} %bitcast.81, s32[1,1]{1,0:T(1,128)} %bitcast.1.place_ref, bf16[512,512]{1,0:T(8,128)(2,1)} %get-tuple-element.49.q_ref.refs_6_, bf16[512,512]{1,0:T(8,128)(2,1)} %get-tuple-element.50.k_ref.refs_7_, ...), custom_call_target="tpu_custom_call" | custom-call | flops 1342177280 | bytes 8388608 | tf_op jit(solution)/shard_map/pallas_call | solution.py:1274
  176.0 4.3 %fusion.41 = f32[512,1024]{1,0:T(8,128)S(1)} fusion(bf16[512,1536]{1,0:T(8,128)(2,1)} %get-tuple-element.59, bf16[1,1024,1536]{2,1,0:T(8,128)(2,1)} %param.16), kind=kOutput, calls=%fused_computation.89 | convolution fusion | flops 1610612736 | bytes 6815744 | tf_op jit(solution)/shard_map/dot_general | solution.py:1283
  180.3 0.8 fusion.47
  181.1 1.9 subtract_multiply_fusion.part_ref
  183.0 29.3 %shard_map.213.refs_2_ = bf16[512,1024]{1,0:T(8,128)(2,1)} custom-call(f32[512,1024]{1,0:T(8,128)} %subtract_multiply_fusion.part_ref, f32[512,512]{1,0:T(8,128)} %bitcast_convert_fusion.4.base_ref, bf16[512,1024]{1,0:T(8,128)(2,1)} %copy-done.2), custom_call_target="tpu_custom_call" | custom-call | flops 1048576 | bytes 8388608 | tf_op jit(solution)/shard_map/pallas_call | solution.py:1132
  212.3 1.3 add_add_fusion
  213.8 1.5 convolution_convert_fusion.ga_ref.refs_9_
  215.9 4.5 %shard_map.214.refs_13_ = f32[4,4,72,128]{3,2,1,0:T(8,128)} custom-call(s32[4,4]{1,0:T(4,128)} %bitcast.82, s32[1,1]{1,0:T(1,128)} %bitcast.1.place_ref, bf16[512,512]{1,0:T(8,128)(2,1)} %get-tuple-element.49.q_ref.refs_6_, bf16[512,512]{1,0:T(8,128)(2,1)} %convolution_convert_fusion.ga_ref.refs_9_, f32[512,512]{1,0:T(8,128)} %get-tuple-element.55.att_ref.refs_10_, ...), custom_call_target="tpu_custom_call" | custom-call | flops 201326592 | bytes 8388608 | tf_op jit(solution)/shard_map/pallas_call | solution.py:1239
  220.4 172.7 %shard_map.215 = (bf16[2048,1024]{1,0:T(8,128)(2,1)}, bf16[512,1024]{1,0:T(8,128)(2,1)}, bf16[1024,2048]{1,0:T(8,128)(2,1)}, bf16[1024,1536]{1,0:T(8,128)(2,1)},...) custom-call(s32[4,4]{1,0:T(4,128)} %bitcast.83, bf16[512,2048]{1,0:T(8,128)(2,1)} %get-tuple-element.48.refs_1_, ...), custom_call_target="tpu_custom_call" | custom-call | flops 6576668672 | bytes 41943040 | tf_op jit(solution)/shard_map/pallas_call | solution.py:724
  393.1 1.3 slice.67
  394.4 0.7 slice.66
  395.1 1.0 convert_element_type.108
  396.7 0.7 broadcast_in_dim_reshape.10
  398.0 0.6 copy.30
  398.6 2.8 bitcast_convert_fusion.3
  401.4 3.6 bitcast_convert_fusion.2
  405.0 4.4 %bitcast_convert_fusion.1 = f32[1,1024,2048]{2,1,0:T(8,128)} fusion(bf16[1024,2048]{1,0:T(8,128)(2,1)S(1)} %copy-done.6), kind=kLoop, calls=%fused_computation.1 | loop fusion | flops 2097152 | bytes 12582912 | tf_op jit(solution)/shard_map/broadcast_in_dim | solution.py:1345
  409.4 4.4 %bitcast_convert_fusion = f32[1,2048,1024]{2,1,0:T(8,128)} fusion(bf16[2048,1024]{1,0:T(8,128)(2,1)S(1)} %copy-done.5), kind=kLoop, calls=%fused_computation | loop fusion | flops 2097152 | bytes 12582912 | tf_op jit(solution)/shard_map/broadcast_in_dim | solution.py:1345
  413.9 1.2 broadcast_select_fusion
  (55 shorter events, 3.7 us)
Async XLA Ops:
  0.6 15.9 %copy-start = (bf16[1,512,1024]{2,1,0:T(8,128)(2,1)S(1)}, bf16[1,512,1024]{2,1,0:T(8,128)(2,1)}, u32[]{:S(2)}) copy-start(bf16[1,512,1024]{2,1,0:T(8,128)(2,1)} %param.19) | copy-start | bytes 3145732
  0.7 9.8 %copy-start.4 = (bf16[1,4,1,128,512]{4,3,2,1,0:T(8,128)(2,1)S(1)}, bf16[1,4,1,128,512]{4,3,2,1,0:T(8,128)(2,1)}, u32[]{:S(2)}) copy-start(bf16[1,4,1,128,512]{4,3,2,1,0:T(8,128)(2,1)} %param.12) | copy-start | bytes 1572868
  0.7 11.0 %copy-start.13 = (f32[1,512]{1,0:T(1,128)S(1)}, f32[1,512]{1,0:T(1,128)}, u32[]{:S(2)}) copy-start(f32[1,512]{1,0:T(1,128)} %param.20) | copy-start | bytes 6148
  0.7 15.1 %collective-permute-start = (bf16[512,512]{1,0:T(8,128)(2,1)}, bf16[512,512]{1,0:T(8,128)(2,1)S(1)}, u32[]{:S(2)}, u32[]{:S(2)}) collective-permute-start(bf16[512,512]{1,0:T(8,128)(2,1)} %bitcast.59), channel_id=1, source_target_pairs={{0,1},{1,0},{2,3},{3,2},{4,5},{5,4},{6,7},{7,6},{8,9},{9,8},{10,11... | collective-permute-start | bytes 1572872 | tf_op jit(solution)/shard_map/ppermute | solution.py:1148
  16.1 2.0 copy-start.2
  42.8 8.6 %copy-start.10 = (f32[512,1024]{1,0:T(8,128)S(1)}, f32[512,1024]{1,0:T(8,128)}, u32[]{:S(2)}) copy-start(f32[512,1024]{1,0:T(8,128)} %get-tuple-element.46) | copy-start | bytes 6291460
  75.5 3.2 copy-start.1
  108.5 8.6 %copy-start.11 = (f32[512,1024]{1,0:T(8,128)S(1)}, f32[512,1024]{1,0:T(8,128)}, u32[]{:S(2)}) copy-start(f32[512,1024]{1,0:T(8,128)} %get-tuple-element.54) | copy-start | bytes 6291460
  119.0 93.3 %collective-permute-start.1 = (bf16[512,512]{1,0:T(8,128)(2,1)S(1)}, bf16[512,512]{1,0:T(8,128)(2,1)S(1)}, u32[]{:S(2)}, u32[]{:S(2)}) collective-permute-start(bf16[512,512]{1,0:T(8,128)(2,1)S(1)} %select_convert_fusion), channel_id=1, source_target_pairs={{0,1},{1,0},{2,3},{3,2},{4,5},{5,4},{6,7},{7,6},{8,9},{9,8},{10,11... | collective-permute-start | bytes 1572872 | tf_op jit(solution)/shard_map/ppermute | solution.py:1163
  176.0 4.3 %copy-start.9 = (f32[512,1024]{1,0:T(8,128)S(1)}, f32[512,1024]{1,0:T(8,128)}, u32[]{:S(2)}) copy-start(f32[512,1024]{1,0:T(8,128)} %get-tuple-element.60) | copy-start | bytes 6291460
  212.3 1.4 copy-start.3
  397.4 4.0 copy-start.8
  401.4 3.6 copy-start.6
  405.0 4.5 %copy-start.5 = (bf16[2048,1024]{1,0:T(8,128)(2,1)S(1)}, bf16[2048,1024]{1,0:T(8,128)(2,1)}, u32[]{:S(2)}) copy-start(bf16[2048,1024]{1,0:T(8,128)(2,1)} %get-tuple-element.68) | copy-start | bytes 12582916
  409.4 4.4 %copy-start.7 = (f32[512,512]{1,0:T(8,128)S(1)}, f32[512,512]{1,0:T(8,128)}, u32[]{:S(2)}) copy-start(f32[512,512]{1,0:T(8,128)} %add_add_fusion) | copy-start | bytes 3145732
  409.4 4.4 %copy-start.12 = (f32[512,512]{1,0:T(8,128)S(1)}, f32[512,512]{1,0:T(8,128)}, u32[]{:S(2)}) copy-start(f32[512,512]{1,0:T(8,128)} %get-tuple-element.62) | copy-start | bytes 3145732
